TPU v7x, 256 devices: a whole 4x4x8 slice. The times are simulated.
256 devices in a mesh: region: 8 (over x, core), tile: 32 (over z, y).
Axes of the slice: x: 4, y: 4, z: 8, core: 2. Of those that a mesh axis runs over, the one named last changes fastest.
Arguments:
- kx: float32 [8, 128, 4096], P(None, 'region', 'tile'), may hold values from 0.05 to 0.24
- ky: float32 [8, 128, 4096], P(None, 'region', 'tile'), may hold values from 0.05 to 0.24
- mask: int32 [8, 128, 4096], P(None, 'region', 'tile'), may hold values 0 or 1
- obs_owner: int32 [131072, 1], P(('region', 'tile')), may hold values from 0 to 31; in each aligned block of 512 rows (0 to 511, 512 to 1023, ...) at most 32 rows name the same one
- obs_row: int32 [131072], P(('region', 'tile')), may hold values from 0 to 14
- obs_col: int32 [131072], P(('region', 'tile')), may hold values from 0 to 126
- obs_weight: float32 [131072, 128], P(('region', 'tile')), may hold values from -1 to 1
- innovation: float32 [131072], P(('region', 'tile')), may hold values from -6 to 6
- inverse_var: float32 [131072], P(('region', 'tile')), may hold values from 0.5 to 4
Outputs:
- control: float32 [4, 8, 128, 4096], P(None, None, 'region', 'tile')
- residual: float32 [4, 8, 128, 4096], P(None, None, 'region', 'tile')
Inputs may be any that keep to these rules, and one draw needn't show every extreme that they name: `obs_owner`: within the rows of one device no tile is named more than 32 times.
All inputs are finite; a program needn't handle non-finite values. No bound on the sum of `mask` on one device may be relied on, other than what follows from the above.
Results may differ from a plain program's by a relative error of at most 0.009.
Values sent between devices are 32-bit elements; how exact they have to be, the bound alone decides.
A program may use at most 64 MiB of HBM per device.

v0:
```python
import jax
import jax.numpy as jnp
from jax import lax
from jax.sharding import PartitionSpec as P

STEPS = 4
ITERS = 2


def padded_2(cells, sides, width):
    for axis, dim in sides:
        count = lax.axis_size(axis)
        ends = count - 1
        head = lax.slice_in_dim(cells, 0, width, axis=dim)
        tail = lax.slice_in_dim(cells, cells.shape[dim] - width, cells.shape[dim], axis=dim)
        cells = jnp.concatenate(
            [
                lax.ppermute(tail, axis, [(i, (i + 1) % count) for i in range(ends)]),
                cells,
                lax.ppermute(head, axis, [((i + 1) % count, i) for i in range(ends)]),
            ],
            axis=dim,
        )
    return cells


def diffuse(field, wet, east, north):
    plain = field * wet
    centre = plain[..., 1:-1, 1:-1]
    flux = east[:, 1:-1, 1:-1] * (plain[..., 2:, 1:-1] - centre)
    flux = flux - east[:, :-2, 1:-1] * (centre - plain[..., :-2, 1:-1])
    flux = flux + north[:, 1:-1, 1:-1] * (plain[..., 1:-1, 2:] - centre)
    flux = flux - north[:, 1:-1, :-2] * (centre - plain[..., 1:-1, :-2])
    return wet[:, 1:-1, 1:-1] * (centre + flux)


def squares(residual):
    return lax.psum(jnp.sum(residual * residual), ("region", "tile"))


def body(kx, ky, mask, obs_owner, obs_row, obs_col, obs_weight, innovation, inverse_var):
    levels, rows_x, cols_y = kx.shape
    tiles = lax.axis_size("tile")
    count = obs_owner.shape[0]
    width = obs_weight.shape[1]
    slices = width // 4
    capacity = 2 * count // tiles
    stacked = jnp.stack([kx, ky, mask.astype(jnp.float32)])
    extended = padded_2(stacked, (("region", 2), ("tile", 3)), STEPS)
    wet = extended[2]
    padded = jnp.pad(wet, ((0, 0), (0, 1), (0, 1)))
    east = extended[0] * wet * padded[:, 1:, :-1]
    north = extended[1] * wet * padded[:, :-1, 1:]

    def spread(field):
        inner = (
            slice(None),
            slice(STEPS - 1, STEPS + rows_x + 1),
            slice(STEPS - 1, STEPS + cols_y + 1),
        )
        for step in range(STEPS):
            framed = padded_2(field, (("region", 2), ("tile", 3)), 1)
            field = diffuse(framed, wet[inner], east[inner], north[inner])
        return field

    owner = obs_owner[:, 0]
    marks = (owner[:, None] == jnp.arange(tiles, dtype=jnp.int32)[None, :]).astype(jnp.int32)
    order = jnp.sum(jnp.cumsum(marks, axis=0) * marks, axis=1) - 1
    slots = owner * capacity + order
    send_places = (
        jnp.zeros((tiles * capacity,), jnp.int32).at[slots].set(obs_row * cols_y + obs_col)
    )
    places = lax.all_to_all(
        send_places.reshape(tiles, capacity), "tile", split_axis=0, concat_axis=0, tiled=True
    ).reshape(-1)
    corners = places[:, None] + jnp.array([0, 1, cols_y, cols_y + 1], jnp.int32)[None, :]
    send_blocks = jnp.zeros((tiles * capacity, width), jnp.float32).at[slots].set(obs_weight)
    send_innov = jnp.zeros((tiles * capacity,), jnp.float32).at[slots].set(innovation)
    send_scale = jnp.zeros((tiles * capacity,), jnp.float32).at[slots].set(inverse_var)

    def place(terms):
        table = (
            jnp.zeros((rows_x * cols_y, slices), jnp.float32)
            .at[corners.reshape(-1)]
            .add(terms.reshape(-1, slices))
        )
        return table.T.reshape(-1, levels, rows_x, cols_y)

    def to_owner(terms):
        back = lax.all_to_all(
            terms.reshape(tiles, capacity, width), "tile", split_axis=0, concat_axis=0, tiled=True
        )
        return place(back.reshape(-1, width))

    first_term = to_owner(send_blocks * (send_scale * send_innov)[:, None])
    right_side = spread(first_term)
    control = jnp.zeros_like(right_side)
    residual = right_side
    direction = right_side
    norm_now = squares(residual)
    for step in range(ITERS):
        pick_table = spread(direction).reshape(slices, rows_x * cols_y).T
        values = lax.all_to_all(
            pick_table[corners].reshape(-1, width).reshape(tiles, capacity, width),
            "tile",
            split_axis=0,
            concat_axis=0,
            tiled=True,
        )
        observed = jnp.sum(send_blocks * values.reshape(-1, width), axis=1)
        image = direction + spread(to_owner(send_blocks * (send_scale * observed)[:, None]))
        alpha = norm_now / lax.psum(jnp.sum(direction * image), ("region", "tile"))
        control = control + alpha * direction
        residual = residual - alpha * image
        norm_next = squares(residual)
        direction = residual + norm_next / norm_now * direction
        norm_now = norm_next
    return (control, residual)


def solution(mesh):
    return jax.shard_map(
        body,
        mesh=mesh,
        in_specs=(
            P(None, "region", "tile"),
            P(None, "region", "tile"),
            P(None, "region", "tile"),
            P(("region", "tile"), None),
            P(("region", "tile")),
            P(("region", "tile")),
            P(("region", "tile"), None),
            P(("region", "tile")),
            P(("region", "tile")),
        ),
        out_specs=(P(None, None, "region", "tile"), P(None, None, "region", "tile")),
        check_vma=False,
    )
```

profile of v0, /device:TPU:1, one launch (start us, length us, event | category | flops | bytes accessed | tf_op | source)
XLA Modules:
  0.0 1016.1 jit_solution(4948081468598664369)
XLA Ops:
  8.1 12.0 %all-to-all-start = ((s32[32,1,32]{2,1,0:T(1,128)}), s32[32,1,32]{2,1,0:T(1,128)S(1)}, u32[]{:S(2)}, u32[]{:S(2)}) async-start(s32[32,1,32]{2,1,0:T(1,128)} %all_to_all.21), calls=%async_computation | async-start | bytes 32768 | tf_op jit(solution)/shard_map/all_to_all | solution.py:73
  36.3 9.5 all-to-all-start.1
  52.3 7.6 collective-permute-done.2
  64.9 22.9 %scatter_custom_fusion.4 = f32[2048,32]{1,0:T(8,128)S(1)} fusion(s32[4096]{0:T(1024)S(1)} %bitcast.107, f32[4096,32]{1,0:T(8,128)} %reshape.222, f32[]{:T(128)} %constant.8.clone.1), kind=kCustom, calls=%fused_computation.39 | custom fusion | flops 131072 | bytes 262656 | tf_op jit(solution)/shard_map/scatter-add | solution.py:85
  88.2 4.8 collective-permute-start.4
  103.4 5.7 collective-permute-done.6
  114.1 4.6 collective-permute-start.8
  129.0 6.1 collective-permute-done.10
  135.1 4.8 collective-permute-done.11
  140.8 4.5 collective-permute-start.12
  150.5 5.7 collective-permute-start.14
  157.6 6.1 collective-permute-done.14
  163.7 4.1 collective-permute-done.15
  182.4 6.1 collective-permute-done.18
  188.5 4.1 collective-permute-done.19
  206.4 6.1 collective-permute-done.22
  229.8 6.6 collective-permute-done.26
  253.7 6.6 collective-permute-done.30
  277.6 6.6 collective-permute-done.34
  289.6 14.2 %gather_fusion = f32[4096,32]{1,0:T(8,128)} fusion(f32[2048,32]{1,0:T(8,128)S(1)} %bitcast.88, s32[4096]{0:T(1024)S(1)} %broadcast_clamp_fusion), kind=kCustom, calls=%fused_computation | custom fusion | bytes 1064960 | tf_op jit(solution)/shard_map/gather | solution.py:104
  305.8 37.1 %all_to_all.34 = f32[32,32,128]{2,1,0:T(8,128)S(1)} all-to-all(f32[32,32,128]{2,1,0:T(8,128)S(1)} %reshape_reshape.16), channel_id=1, replica_groups=mesh['region'=8,'tile'=32] {'tile'}, dimensions={0} | all-to-all | bytes 1048576 | tf_op jit(solution)/shard_map/all_to_all | solution.py:103
  343.3 19.7 %all_to_all.35 = f32[32,32,128]{2,1,0:T(8,128)S(1)} all-to-all(f32[32,32,128]{2,1,0:T(8,128)S(1)} %bitcast.93), channel_id=1, replica_groups=mesh['region'=8,'tile'=32] {'tile'}, dimensions={0} | all-to-all | bytes 1048576 | tf_op jit(solution)/shard_map/all_to_all | solution.py:90
  364.8 22.9 %scatter_custom_fusion.5 = f32[2048,32]{1,0:T(8,128)S(1)} fusion(s32[4096]{0:T(1024)S(1)} %bitcast.108, f32[4096,32]{1,0:T(8,128)} %reshape.230, f32[]{:T(128)} %constant.8.clone.1), kind=kCustom, calls=%fused_computation.37 | custom fusion | flops 131072 | bytes 262656 | tf_op jit(solution)/shard_map/scatter-add | solution.py:85
  390.0 4.7 collective-permute-start.37
  399.5 6.8 collective-permute-done.38
  423.1 6.7 collective-permute-done.42
  442.1 4.6 collective-permute-start.46
  448.0 6.6 collective-permute-done.46
  471.9 6.6 collective-permute-done.50
  484.3 79.5 %all-reduce.1 = (f32[]{:T(128)}, f32[]{:T(128)}) all-reduce(f32[]{:T(128)} %get-tuple-element.3, f32[]{:T(128)} %get-tuple-element.2), channel_id=1, replica_groups=mesh['region'=8,'tile'=32] {'region','tile'}, use_global_device_ids=true, to_apply=%region_9.10 | all-reduce | flops 2 | bytes 16 | tf_op jit(solution)/shard_map/psum | solution.py:38
  566.1 73.5 %psum.30 = f32[]{:T(128)} all-reduce(f32[]{:T(128)} %multiply_reduce_fusion.1), channel_id=1, replica_groups=mesh['region'=8,'tile'=32] {'region','tile'}, use_global_device_ids=true, to_apply=%region_15.16 | all-reduce | flops 1 | bytes 8 | tf_op jit(solution)/shard_map/psum | solution.py:38
  653.0 6.6 collective-permute-done.54
  677.9 6.1 collective-permute-done.58
  684.0 4.6 collective-permute-done.59
  698.0 6.1 collective-permute-start.62
  705.4 6.1 collective-permute-done.62
  716.5 4.4 collective-permute-start.64
  731.6 6.1 collective-permute-done.66
  744.7 14.2 %gather_fusion.1 = f32[4096,32]{1,0:T(8,128)} fusion(f32[2048,32]{1,0:T(8,128)S(1)} %bitcast.87, s32[4096]{0:T(1024)S(1)} %broadcast_clamp_fusion), kind=kCustom, calls=%fused_computation.1 | custom fusion | bytes 1064960 | tf_op jit(solution)/shard_map/gather | solution.py:104
  760.9 29.4 %all_to_all.36 = f32[32,32,128]{2,1,0:T(8,128)S(1)} all-to-all(f32[32,32,128]{2,1,0:T(8,128)S(1)} %reshape_reshape.18), channel_id=1, replica_groups=mesh['region'=8,'tile'=32] {'tile'}, dimensions={0} | all-to-all | bytes 1048576 | tf_op jit(solution)/shard_map/all_to_all | solution.py:103
  790.8 21.4 %all_to_all.37 = f32[32,32,128]{2,1,0:T(8,128)S(1)} all-to-all(f32[32,32,128]{2,1,0:T(8,128)S(1)} %bitcast.92), channel_id=1, replica_groups=mesh['region'=8,'tile'=32] {'tile'}, dimensions={0} | all-to-all | bytes 1048576 | tf_op jit(solution)/shard_map/all_to_all | solution.py:90
  814.1 22.9 %scatter_custom_fusion.6 = f32[2048,32]{1,0:T(8,128)S(1)} fusion(s32[4096]{0:T(1024)S(1)} %bitcast.109, f32[4096,32]{1,0:T(8,128)} %reshape.238, f32[]{:T(128)} %constant.8.clone.1), kind=kCustom, calls=%fused_computation.35 | custom fusion | flops 131072 | bytes 262656 | tf_op jit(solution)/shard_map/scatter-add | solution.py:85
  850.2 6.1 collective-permute-done.70
  873.2 6.6 collective-permute-done.74
  892.0 4.8 collective-permute-start.78
  898.1 6.6 collective-permute-done.78
  922.0 6.6 collective-permute-done.82
  934.2 79.2 %psum.31 = f32[]{:T(128)} all-reduce(f32[]{:T(128)} %get-tuple-element.6), channel_id=1, replica_groups=mesh['region'=8,'tile'=32] {'region','tile'}, use_global_device_ids=true, to_apply=%region_19.20 | all-reduce | flops 1 | bytes 8 | tf_op jit(solution)/shard_map/psum | solution.py:112
  (301 shorter events, 354.7 us)
Async XLA Ops:
  8.1 28.2 %all-to-all-start = ((s32[32,1,32]{2,1,0:T(1,128)}), s32[32,1,32]{2,1,0:T(1,128)S(1)}, u32[]{:S(2)}, u32[]{:S(2)}) async-start(s32[32,1,32]{2,1,0:T(1,128)} %all_to_all.21), calls=%async_computation | async-start | bytes 32768 | tf_op jit(solution)/shard_map/all_to_all | solution.py:73
  21.9 25.7 %collective-permute-start = (f32[3,8,4,128]{3,2,1,0:T(4,128)S(1)}, f32[3,8,4,128]{3,2,1,0:T(4,128)S(1)}, u32[]{:S(2)}, u32[]{:S(2)}) collective-permute-start(f32[3,8,4,128]{3,2,1,0:T(4,128)S(1)} %get-tuple-element.99), channel_id=1, source_target_pairs={{0,32},{32,64},{64,96},{96,128},{128,160},{160,192},{192,224},{1,3... | collective-permute-start | bytes 147464 | tf_op jit(solution)/shard_map/ppermute | solution.py:18
  25.8 21.8 %collective-permute-start.1 = (f32[3,8,4,128]{3,2,1,0:T(4,128)S(1)}, f32[3,8,4,128]{3,2,1,0:T(4,128)S(1)}, u32[]{:S(2)}, u32[]{:S(2)}) collective-permute-start(f32[3,8,4,128]{3,2,1,0:T(4,128)S(1)} %get-tuple-element.100), channel_id=1, source_target_pairs={{32,0},{64,32},{96,64},{128,96},{160,128},{192,160},{224,192},{33,... | collective-permute-start | bytes 147464 | tf_op jit(solution)/shard_map/ppermute | solution.py:20
  36.3 26.8 %all-to-all-start.1 = ((f32[32,32,128]{2,1,0:T(8,128)}), f32[32,32,128]{2,1,0:T(8,128)S(1)}, u32[]{:S(2)}, u32[]{:S(2)}) async-start(f32[32,32,128]{2,1,0:T(8,128)} %bitcast.10), calls=%async_computation.1 | async-start | bytes 1048576 | tf_op jit(solution)/shard_map/all_to_all | solution.py:90
  47.8 12.1 %collective-permute-start.2 = (f32[3,8,24,4]{3,2,1,0:T(8,128)S(1)}, f32[3,8,24,4]{3,2,1,0:T(8,128)S(1)}, u32[]{:S(2)}, u32[]{:S(2)}) collective-permute-start(f32[3,8,24,4]{3,2,1,0:T(8,128)S(1)} %get-tuple-element.51), channel_id=1, source_target_pairs={{0,1},{1,2},{2,3},{3,4},{4,5},{5,6},{6,7},{7,8},{8,9},{9,10},{10,1... | collective-permute-start | bytes 27656 | tf_op jit(solution)/shard_map/ppermute | solution.py:18
  51.0 11.6 %collective-permute-start.3 = (f32[3,8,24,4]{3,2,1,0:T(8,128)S(1)}, f32[3,8,24,4]{3,2,1,0:T(8,128)S(1)}, u32[]{:S(2)}, u32[]{:S(2)}) collective-permute-start(f32[3,8,24,4]{3,2,1,0:T(8,128)S(1)} %get-tuple-element.52), channel_id=1, source_target_pairs={{1,0},{2,1},{3,2},{4,3},{5,4},{6,5},{7,6},{8,7},{9,8},{10,9},{11,1... | collective-permute-start | bytes 27656 | tf_op jit(solution)/shard_map/ppermute | solution.py:20
  88.2 6.9 collective-permute-start.4
  98.3 10.8 %collective-permute-start.6 = (f32[4,8,18,1]{3,2,1,0:T(8,128)S(1)}, f32[4,8,18,1]{3,2,1,0:T(8,128)S(1)}, u32[]{:S(2)}, u32[]{:S(2)}) collective-permute-start(f32[4,8,18,1]{3,2,1,0:T(8,128)S(1)} %get-tuple-element.49), channel_id=1, source_target_pairs={{0,1},{1,2},{2,3},{3,4},{4,5},{5,6},{6,7},{7,8},{8,9},{9,10},{10,1... | collective-permute-start | bytes 6920 | tf_op jit(solution)/shard_map/ppermute | solution.py:18
  101.7 11.5 %collective-permute-start.7 = (f32[4,8,18,1]{3,2,1,0:T(8,128)S(1)}, f32[4,8,18,1]{3,2,1,0:T(8,128)S(1)}, u32[]{:S(2)}, u32[]{:S(2)}) collective-permute-start(f32[4,8,18,1]{3,2,1,0:T(8,128)S(1)} %get-tuple-element.50), channel_id=1, source_target_pairs={{1,0},{2,1},{3,2},{4,3},{5,4},{6,5},{7,6},{8,7},{9,8},{10,9},{11,1... | collective-permute-start | bytes 6920 | tf_op jit(solution)/shard_map/ppermute | solution.py:20
  114.1 6.7 collective-permute-start.8
  124.0 11.1 %collective-permute-start.10 = (f32[4,8,18,1]{3,2,1,0:T(8,128)S(1)}, f32[4,8,18,1]{3,2,1,0:T(8,128)S(1)}, u32[]{:S(2)}, u32[]{:S(2)}) collective-permute-start(f32[4,8,18,1]{3,2,1,0:T(8,128)S(1)} %get-tuple-element.47), channel_id=1, source_target_pairs={{0,1},{1,2},{2,3},{3,4},{4,5},{5,6},{6,7},{7,8},{8,9},{9,10},{10,1... | collective-permute-start | bytes 6920 | tf_op jit(solution)/shard_map/ppermute | solution.py:18
  127.7 12.1 %collective-permute-start.11 = (f32[4,8,18,1]{3,2,1,0:T(8,128)S(1)}, f32[4,8,18,1]{3,2,1,0:T(8,128)S(1)}, u32[]{:S(2)}, u32[]{:S(2)}) collective-permute-start(f32[4,8,18,1]{3,2,1,0:T(8,128)S(1)} %get-tuple-element.48), channel_id=1, source_target_pairs={{1,0},{2,1},{3,2},{4,3},{5,4},{6,5},{7,6},{8,7},{9,8},{10,9},{11,1... | collective-permute-start | bytes 6920 | tf_op jit(solution)/shard_map/ppermute | solution.py:20
  150.5 13.1 %collective-permute-start.14 = (f32[4,8,18,1]{3,2,1,0:T(8,128)S(1)}, f32[4,8,18,1]{3,2,1,0:T(8,128)S(1)}, u32[]{:S(2)}, u32[]{:S(2)}) collective-permute-start(f32[4,8,18,1]{3,2,1,0:T(8,128)S(1)} %get-tuple-element.45), channel_id=1, source_target_pairs={{0,1},{1,2},{2,3},{3,4},{4,5},{5,6},{6,7},{7,8},{8,9},{9,10},{10,1... | collective-permute-start | bytes 6920 | tf_op jit(solution)/shard_map/ppermute | solution.py:18
  156.3 11.5 %collective-permute-start.15 = (f32[4,8,18,1]{3,2,1,0:T(8,128)S(1)}, f32[4,8,18,1]{3,2,1,0:T(8,128)S(1)}, u32[]{:S(2)}, u32[]{:S(2)}) collective-permute-start(f32[4,8,18,1]{3,2,1,0:T(8,128)S(1)} %get-tuple-element.46), channel_id=1, source_target_pairs={{1,0},{2,1},{3,2},{4,3},{5,4},{6,5},{7,6},{8,7},{9,8},{10,9},{11,1... | collective-permute-start | bytes 6920 | tf_op jit(solution)/shard_map/ppermute | solution.py:20
  177.1 11.4 %collective-permute-start.18 = (f32[4,8,18,1]{3,2,1,0:T(8,128)S(1)}, f32[4,8,18,1]{3,2,1,0:T(8,128)S(1)}, u32[]{:S(2)}, u32[]{:S(2)}) collective-permute-start(f32[4,8,18,1]{3,2,1,0:T(8,128)S(1)} %get-tuple-element.43), channel_id=1, source_target_pairs={{0,1},{1,2},{2,3},{3,4},{4,5},{5,6},{6,7},{7,8},{8,9},{9,10},{10,1... | collective-permute-start | bytes 6920 | tf_op jit(solution)/shard_map/ppermute | solution.py:18
  181.1 11.5 %collective-permute-start.19 = (f32[4,8,18,1]{3,2,1,0:T(8,128)S(1)}, f32[4,8,18,1]{3,2,1,0:T(8,128)S(1)}, u32[]{:S(2)}, u32[]{:S(2)}) collective-permute-start(f32[4,8,18,1]{3,2,1,0:T(8,128)S(1)} %get-tuple-element.44), channel_id=1, source_target_pairs={{1,0},{2,1},{3,2},{4,3},{5,4},{6,5},{7,6},{8,7},{9,8},{10,9},{11,1... | collective-permute-start | bytes 6920 | tf_op jit(solution)/shard_map/ppermute | solution.py:20
  201.0 11.4 %collective-permute-start.22 = (f32[4,8,18,1]{3,2,1,0:T(8,128)S(1)}, f32[4,8,18,1]{3,2,1,0:T(8,128)S(1)}, u32[]{:S(2)}, u32[]{:S(2)}) collective-permute-start(f32[4,8,18,1]{3,2,1,0:T(8,128)S(1)} %get-tuple-element.41), channel_id=1, source_target_pairs={{0,1},{1,2},{2,3},{3,4},{4,5},{5,6},{6,7},{7,8},{8,9},{9,10},{10,1... | collective-permute-start | bytes 6920 | tf_op jit(solution)/shard_map/ppermute | solution.py:18
  205.1 11.5 %collective-permute-start.23 = (f32[4,8,18,1]{3,2,1,0:T(8,128)S(1)}, f32[4,8,18,1]{3,2,1,0:T(8,128)S(1)}, u32[]{:S(2)}, u32[]{:S(2)}) collective-permute-start(f32[4,8,18,1]{3,2,1,0:T(8,128)S(1)} %get-tuple-element.42), channel_id=1, source_target_pairs={{1,0},{2,1},{3,2},{4,3},{5,4},{6,5},{7,6},{8,7},{9,8},{10,9},{11,1... | collective-permute-start | bytes 6920 | tf_op jit(solution)/shard_map/ppermute | solution.py:20
  224.7 11.6 %collective-permute-start.26 = (f32[4,8,18,1]{3,2,1,0:T(8,128)S(1)}, f32[4,8,18,1]{3,2,1,0:T(8,128)S(1)}, u32[]{:S(2)}, u32[]{:S(2)}) collective-permute-start(f32[4,8,18,1]{3,2,1,0:T(8,128)S(1)} %get-tuple-element.39), channel_id=1, source_target_pairs={{0,1},{1,2},{2,3},{3,4},{4,5},{5,6},{6,7},{7,8},{8,9},{9,10},{10,1... | collective-permute-start | bytes 6920 | tf_op jit(solution)/shard_map/ppermute | solution.py:18
  228.5 12.0 %collective-permute-start.27 = (f32[4,8,18,1]{3,2,1,0:T(8,128)S(1)}, f32[4,8,18,1]{3,2,1,0:T(8,128)S(1)}, u32[]{:S(2)}, u32[]{:S(2)}) collective-permute-start(f32[4,8,18,1]{3,2,1,0:T(8,128)S(1)} %get-tuple-element.40), channel_id=1, source_target_pairs={{1,0},{2,1},{3,2},{4,3},{5,4},{6,5},{7,6},{8,7},{9,8},{10,9},{11,1... | collective-permute-start | bytes 6920 | tf_op jit(solution)/shard_map/ppermute | solution.py:20
  248.6 11.6 %collective-permute-start.30 = (f32[4,8,18,1]{3,2,1,0:T(8,128)S(1)}, f32[4,8,18,1]{3,2,1,0:T(8,128)S(1)}, u32[]{:S(2)}, u32[]{:S(2)}) collective-permute-start(f32[4,8,18,1]{3,2,1,0:T(8,128)S(1)} %get-tuple-element.37), channel_id=1, source_target_pairs={{0,1},{1,2},{2,3},{3,4},{4,5},{5,6},{6,7},{7,8},{8,9},{9,10},{10,1... | collective-permute-start | bytes 6920 | tf_op jit(solution)/shard_map/ppermute | solution.py:18
  252.4 12.0 %collective-permute-start.31 = (f32[4,8,18,1]{3,2,1,0:T(8,128)S(1)}, f32[4,8,18,1]{3,2,1,0:T(8,128)S(1)}, u32[]{:S(2)}, u32[]{:S(2)}) collective-permute-start(f32[4,8,18,1]{3,2,1,0:T(8,128)S(1)} %get-tuple-element.38), channel_id=1, source_target_pairs={{1,0},{2,1},{3,2},{4,3},{5,4},{6,5},{7,6},{8,7},{9,8},{10,9},{11,1... | collective-permute-start | bytes 6920 | tf_op jit(solution)/shard_map/ppermute | solution.py:20
  272.5 11.6 %collective-permute-start.34 = (f32[4,8,18,1]{3,2,1,0:T(8,128)S(1)}, f32[4,8,18,1]{3,2,1,0:T(8,128)S(1)}, u32[]{:S(2)}, u32[]{:S(2)}) collective-permute-start(f32[4,8,18,1]{3,2,1,0:T(8,128)S(1)} %get-tuple-element.35), channel_id=1, source_target_pairs={{0,1},{1,2},{2,3},{3,4},{4,5},{5,6},{6,7},{7,8},{8,9},{9,10},{10,1... | collective-permute-start | bytes 6920 | tf_op jit(solution)/shard_map/ppermute | solution.py:18
  276.3 12.0 %collective-permute-start.35 = (f32[4,8,18,1]{3,2,1,0:T(8,128)S(1)}, f32[4,8,18,1]{3,2,1,0:T(8,128)S(1)}, u32[]{:S(2)}, u32[]{:S(2)}) collective-permute-start(f32[4,8,18,1]{3,2,1,0:T(8,128)S(1)} %get-tuple-element.36), channel_id=1, source_target_pairs={{1,0},{2,1},{3,2},{4,3},{5,4},{6,5},{7,6},{8,7},{9,8},{10,9},{11,1... | collective-permute-start | bytes 6920 | tf_op jit(solution)/shard_map/ppermute | solution.py:20
  395.8 10.6 %collective-permute-start.38 = (f32[4,8,18,1]{3,2,1,0:T(8,128)S(1)}, f32[4,8,18,1]{3,2,1,0:T(8,128)S(1)}, u32[]{:S(2)}, u32[]{:S(2)}) collective-permute-start(f32[4,8,18,1]{3,2,1,0:T(8,128)S(1)} %get-tuple-element.33), channel_id=1, source_target_pairs={{0,1},{1,2},{2,3},{3,4},{4,5},{5,6},{6,7},{7,8},{8,9},{9,10},{10,1... | collective-permute-start | bytes 6920 | tf_op jit(solution)/shard_map/ppermute | solution.py:18
  398.2 11.9 %collective-permute-start.39 = (f32[4,8,18,1]{3,2,1,0:T(8,128)S(1)}, f32[4,8,18,1]{3,2,1,0:T(8,128)S(1)}, u32[]{:S(2)}, u32[]{:S(2)}) collective-permute-start(f32[4,8,18,1]{3,2,1,0:T(8,128)S(1)} %get-tuple-element.34), channel_id=1, source_target_pairs={{1,0},{2,1},{3,2},{4,3},{5,4},{6,5},{7,6},{8,7},{9,8},{10,9},{11,1... | collective-permute-start | bytes 6920 | tf_op jit(solution)/shard_map/ppermute | solution.py:20
  418.3 11.6 %collective-permute-start.42 = (f32[4,8,18,1]{3,2,1,0:T(8,128)S(1)}, f32[4,8,18,1]{3,2,1,0:T(8,128)S(1)}, u32[]{:S(2)}, u32[]{:S(2)}) collective-permute-start(f32[4,8,18,1]{3,2,1,0:T(8,128)S(1)} %get-tuple-element.31), channel_id=1, source_target_pairs={{0,1},{1,2},{2,3},{3,4},{4,5},{5,6},{6,7},{7,8},{8,9},{9,10},{10,1... | collective-permute-start | bytes 6920 | tf_op jit(solution)/shard_map/ppermute | solution.py:18
  421.8 12.1 %collective-permute-start.43 = (f32[4,8,18,1]{3,2,1,0:T(8,128)S(1)}, f32[4,8,18,1]{3,2,1,0:T(8,128)S(1)}, u32[]{:S(2)}, u32[]{:S(2)}) collective-permute-start(f32[4,8,18,1]{3,2,1,0:T(8,128)S(1)} %get-tuple-element.32), channel_id=1, source_target_pairs={{1,0},{2,1},{3,2},{4,3},{5,4},{6,5},{7,6},{8,7},{9,8},{10,9},{11,1... | collective-permute-start | bytes 6920 | tf_op jit(solution)/shard_map/ppermute | solution.py:20
  442.1 12.4 %collective-permute-start.46 = (f32[4,8,18,1]{3,2,1,0:T(8,128)S(1)}, f32[4,8,18,1]{3,2,1,0:T(8,128)S(1)}, u32[]{:S(2)}, u32[]{:S(2)}) collective-permute-start(f32[4,8,18,1]{3,2,1,0:T(8,128)S(1)} %get-tuple-element.29), channel_id=1, source_target_pairs={{0,1},{1,2},{2,3},{3,4},{4,5},{5,6},{6,7},{7,8},{8,9},{9,10},{10,1... | collective-permute-start | bytes 6920 | tf_op jit(solution)/shard_map/ppermute | solution.py:18
  446.7 12.0 %collective-permute-start.47 = (f32[4,8,18,1]{3,2,1,0:T(8,128)S(1)}, f32[4,8,18,1]{3,2,1,0:T(8,128)S(1)}, u32[]{:S(2)}, u32[]{:S(2)}) collective-permute-start(f32[4,8,18,1]{3,2,1,0:T(8,128)S(1)} %get-tuple-element.30), channel_id=1, source_target_pairs={{1,0},{2,1},{3,2},{4,3},{5,4},{6,5},{7,6},{8,7},{9,8},{10,9},{11,1... | collective-permute-start | bytes 6920 | tf_op jit(solution)/shard_map/ppermute | solution.py:20
  466.8 11.6 %collective-permute-start.50 = (f32[4,8,18,1]{3,2,1,0:T(8,128)S(1)}, f32[4,8,18,1]{3,2,1,0:T(8,128)S(1)}, u32[]{:S(2)}, u32[]{:S(2)}) collective-permute-start(f32[4,8,18,1]{3,2,1,0:T(8,128)S(1)} %get-tuple-element.27), channel_id=1, source_target_pairs={{0,1},{1,2},{2,3},{3,4},{4,5},{5,6},{6,7},{7,8},{8,9},{9,10},{10,1... | collective-permute-start | bytes 6920 | tf_op jit(solution)/shard_map/ppermute | solution.py:18
  470.6 12.0 %collective-permute-start.51 = (f32[4,8,18,1]{3,2,1,0:T(8,128)S(1)}, f32[4,8,18,1]{3,2,1,0:T(8,128)S(1)}, u32[]{:S(2)}, u32[]{:S(2)}) collective-permute-start(f32[4,8,18,1]{3,2,1,0:T(8,128)S(1)} %get-tuple-element.28), channel_id=1, source_target_pairs={{1,0},{2,1},{3,2},{4,3},{5,4},{6,5},{7,6},{8,7},{9,8},{10,9},{11,1... | collective-permute-start | bytes 6920 | tf_op jit(solution)/shard_map/ppermute | solution.py:20
  650.2 9.4 collective-permute-start.54
  651.7 12.0 %collective-permute-start.55 = (f32[4,8,18,1]{3,2,1,0:T(8,128)S(1)}, f32[4,8,18,1]{3,2,1,0:T(8,128)S(1)}, u32[]{:S(2)}, u32[]{:S(2)}) collective-permute-start(f32[4,8,18,1]{3,2,1,0:T(8,128)S(1)} %get-tuple-element.26), channel_id=1, source_target_pairs={{1,0},{2,1},{3,2},{4,3},{5,4},{6,5},{7,6},{8,7},{9,8},{10,9},{11,1... | collective-permute-start | bytes 6920 | tf_op jit(solution)/shard_map/ppermute | solution.py:20
  673.4 10.6 %collective-permute-start.58 = (f32[4,8,18,1]{3,2,1,0:T(8,128)S(1)}, f32[4,8,18,1]{3,2,1,0:T(8,128)S(1)}, u32[]{:S(2)}, u32[]{:S(2)}) collective-permute-start(f32[4,8,18,1]{3,2,1,0:T(8,128)S(1)} %get-tuple-element.23), channel_id=1, source_target_pairs={{0,1},{1,2},{2,3},{3,4},{4,5},{5,6},{6,7},{7,8},{8,9},{9,10},{10,1... | collective-permute-start | bytes 6920 | tf_op jit(solution)/shard_map/ppermute | solution.py:18
  676.6 12.0 %collective-permute-start.59 = (f32[4,8,18,1]{3,2,1,0:T(8,128)S(1)}, f32[4,8,18,1]{3,2,1,0:T(8,128)S(1)}, u32[]{:S(2)}, u32[]{:S(2)}) collective-permute-start(f32[4,8,18,1]{3,2,1,0:T(8,128)S(1)} %get-tuple-element.24), channel_id=1, source_target_pairs={{1,0},{2,1},{3,2},{4,3},{5,4},{6,5},{7,6},{8,7},{9,8},{10,9},{11,1... | collective-permute-start | bytes 6920 | tf_op jit(solution)/shard_map/ppermute | solution.py:20
  698.0 13.5 %collective-permute-start.62 = (f32[4,8,18,1]{3,2,1,0:T(8,128)S(1)}, f32[4,8,18,1]{3,2,1,0:T(8,128)S(1)}, u32[]{:S(2)}, u32[]{:S(2)}) collective-permute-start(f32[4,8,18,1]{3,2,1,0:T(8,128)S(1)} %get-tuple-element.21), channel_id=1, source_target_pairs={{0,1},{1,2},{2,3},{3,4},{4,5},{5,6},{6,7},{7,8},{8,9},{9,10},{10,1... | collective-permute-start | bytes 6920 | tf_op jit(solution)/shard_map/ppermute | solution.py:18
  704.1 11.5 %collective-permute-start.63 = (f32[4,8,18,1]{3,2,1,0:T(8,128)S(1)}, f32[4,8,18,1]{3,2,1,0:T(8,128)S(1)}, u32[]{:S(2)}, u32[]{:S(2)}) collective-permute-start(f32[4,8,18,1]{3,2,1,0:T(8,128)S(1)} %get-tuple-element.22), channel_id=1, source_target_pairs={{1,0},{2,1},{3,2},{4,3},{5,4},{6,5},{7,6},{8,7},{9,8},{10,9},{11,1... | collective-permute-start | bytes 6920 | tf_op jit(solution)/shard_map/ppermute | solution.py:20
  726.2 11.4 %collective-permute-start.66 = (f32[4,8,18,1]{3,2,1,0:T(8,128)S(1)}, f32[4,8,18,1]{3,2,1,0:T(8,128)S(1)}, u32[]{:S(2)}, u32[]{:S(2)}) collective-permute-start(f32[4,8,18,1]{3,2,1,0:T(8,128)S(1)} %get-tuple-element.19), channel_id=1, source_target_pairs={{0,1},{1,2},{2,3},{3,4},{4,5},{5,6},{6,7},{7,8},{8,9},{9,10},{10,1... | collective-permute-start | bytes 6920 | tf_op jit(solution)/shard_map/ppermute | solution.py:18
  730.3 11.5 %collective-permute-start.67 = (f32[4,8,18,1]{3,2,1,0:T(8,128)S(1)}, f32[4,8,18,1]{3,2,1,0:T(8,128)S(1)}, u32[]{:S(2)}, u32[]{:S(2)}) collective-permute-start(f32[4,8,18,1]{3,2,1,0:T(8,128)S(1)} %get-tuple-element.20), channel_id=1, source_target_pairs={{1,0},{2,1},{3,2},{4,3},{5,4},{6,5},{7,6},{8,7},{9,8},{10,9},{11,1... | collective-permute-start | bytes 6920 | tf_op jit(solution)/shard_map/ppermute | solution.py:20
  846.5 9.8 collective-permute-start.70
  848.9 11.5 %collective-permute-start.71 = (f32[4,8,18,1]{3,2,1,0:T(8,128)S(1)}, f32[4,8,18,1]{3,2,1,0:T(8,128)S(1)}, u32[]{:S(2)}, u32[]{:S(2)}) collective-permute-start(f32[4,8,18,1]{3,2,1,0:T(8,128)S(1)} %get-tuple-element.18), channel_id=1, source_target_pairs={{1,0},{2,1},{3,2},{4,3},{5,4},{6,5},{7,6},{8,7},{9,8},{10,9},{11,1... | collective-permute-start | bytes 6920 | tf_op jit(solution)/shard_map/ppermute | solution.py:20
  868.6 11.1 %collective-permute-start.74 = (f32[4,8,18,1]{3,2,1,0:T(8,128)S(1)}, f32[4,8,18,1]{3,2,1,0:T(8,128)S(1)}, u32[]{:S(2)}, u32[]{:S(2)}) collective-permute-start(f32[4,8,18,1]{3,2,1,0:T(8,128)S(1)} %get-tuple-element.15), channel_id=1, source_target_pairs={{0,1},{1,2},{2,3},{3,4},{4,5},{5,6},{6,7},{7,8},{8,9},{9,10},{10,1... | collective-permute-start | bytes 6920 | tf_op jit(solution)/shard_map/ppermute | solution.py:18
  871.9 12.0 %collective-permute-start.75 = (f32[4,8,18,1]{3,2,1,0:T(8,128)S(1)}, f32[4,8,18,1]{3,2,1,0:T(8,128)S(1)}, u32[]{:S(2)}, u32[]{:S(2)}) collective-permute-start(f32[4,8,18,1]{3,2,1,0:T(8,128)S(1)} %get-tuple-element.16), channel_id=1, source_target_pairs={{1,0},{2,1},{3,2},{4,3},{5,4},{6,5},{7,6},{8,7},{9,8},{10,9},{11,1... | collective-permute-start | bytes 6920 | tf_op jit(solution)/shard_map/ppermute | solution.py:20
  892.0 12.7 %collective-permute-start.78 = (f32[4,8,18,1]{3,2,1,0:T(8,128)S(1)}, f32[4,8,18,1]{3,2,1,0:T(8,128)S(1)}, u32[]{:S(2)}, u32[]{:S(2)}) collective-permute-start(f32[4,8,18,1]{3,2,1,0:T(8,128)S(1)} %get-tuple-element.13), channel_id=1, source_target_pairs={{0,1},{1,2},{2,3},{3,4},{4,5},{5,6},{6,7},{7,8},{8,9},{9,10},{10,1... | collective-permute-start | bytes 6920 | tf_op jit(solution)/shard_map/ppermute | solution.py:18
  896.8 12.0 %collective-permute-start.79 = (f32[4,8,18,1]{3,2,1,0:T(8,128)S(1)}, f32[4,8,18,1]{3,2,1,0:T(8,128)S(1)}, u32[]{:S(2)}, u32[]{:S(2)}) collective-permute-start(f32[4,8,18,1]{3,2,1,0:T(8,128)S(1)} %get-tuple-element.14), channel_id=1, source_target_pairs={{1,0},{2,1},{3,2},{4,3},{5,4},{6,5},{7,6},{8,7},{9,8},{10,9},{11,1... | collective-permute-start | bytes 6920 | tf_op jit(solution)/shard_map/ppermute | solution.py:20
  917.0 11.6 %collective-permute-start.82 = (f32[4,8,18,1]{3,2,1,0:T(8,128)S(1)}, f32[4,8,18,1]{3,2,1,0:T(8,128)S(1)}, u32[]{:S(2)}, u32[]{:S(2)}) collective-permute-start(f32[4,8,18,1]{3,2,1,0:T(8,128)S(1)} %get-tuple-element.11), channel_id=1, source_target_pairs={{0,1},{1,2},{2,3},{3,4},{4,5},{5,6},{6,7},{7,8},{8,9},{9,10},{10,1... | collective-permute-start | bytes 6920 | tf_op jit(solution)/shard_map/ppermute | solution.py:18
  920.7 12.0 %collective-permute-start.83 = (f32[4,8,18,1]{3,2,1,0:T(8,128)S(1)}, f32[4,8,18,1]{3,2,1,0:T(8,128)S(1)}, u32[]{:S(2)}, u32[]{:S(2)}) collective-permute-start(f32[4,8,18,1]{3,2,1,0:T(8,128)S(1)} %get-tuple-element.12), channel_id=1, source_target_pairs={{1,0},{2,1},{3,2},{4,3},{5,4},{6,5},{7,6},{8,7},{9,8},{10,9},{11,1... | collective-permute-start | bytes 6920 | tf_op jit(solution)/shard_map/ppermute | solution.py:20
  (41 other events, 293.7 us)
where the time goes:
time: 1030 us; the launch traced here: 1020 us
  blocking collectives  340 us (33%)
  waiting for transfers between devices  275 us (27%)
  starting transfers between devices  237 us (23%)
  other arithmetic  100 us (10%)
  local copies, waits for them, and re-layouts  58 us (6%)
    psum x2, blocking collectives, squares(): return lax.psum(jnp.sum(residual * residual), ('region', 'tile'))  153 us
    ppermute x42, waiting for transfers between devices, padded_2(): lax.ppermute(head, axis, [((i + 1) % count, i) for i in range(ends)])  140 us
    ppermute x42, starting transfers between devices, padded_2(): lax.ppermute(tail, axis, [(i, (i + 1) % count) for i in range(ends)])  139 us
    ppermute x42, waiting for transfers between devices, padded_2(): lax.ppermute(tail, axis, [(i, (i + 1) % count) for i in range(ends)])  135 us
    psum x1, blocking collectives, body(): alpha = norm_now / lax.psum(jnp.sum(direction * image), ('region', 'tile'))  79.2 us
    ppermute x42, starting transfers between devices, padded_2(): lax.ppermute(head, axis, [((i + 1) % count, i) for i in range(ends)])  75.7 us
    scatter-add x3, other arithmetic, place(): table = jnp.zeros((rows_x * cols_y, slices), jnp.float32).at[corners.resh...  68.7 us
    all_to_all x2, blocking collectives, body(): lax.all_to_all(pick_table[corners].reshape(-1, width).reshape(tiles, capa...  66.5 us
  transfers between devices with their start and end apart: 86, of which 63 were waited for; matrix products, arithmetic and copies ran while one was open for 1% of the time, Pallas kernels for 0%

commit v1 on v0

v1 whole, which is shorter than its diff:
```python
import functools

import jax
import jax.numpy as jnp
from jax import lax
from jax.experimental import pallas as pl
from jax.experimental.pallas import tpu as pltpu
from jax.sharding import PartitionSpec as P

MESH = pl.DeviceIdType.MESH
F32 = jnp.float32
BF16 = jnp.bfloat16
CAP = 32
LANES = 128
GROUPS = 4
WIDE = 40
FRAME_ROWS = 25


def iota(shape, dim):
    return lax.broadcasted_iota(jnp.int32, shape, dim)


def split(x, parts):
    out = []
    for i in range(parts):
        part = x.astype(BF16)
        out.append(part)
        if i + 1 < parts:
            x = x - part.astype(F32)
    return out


def dot(a, b):
    return jnp.dot(a, b, preferred_element_type=F32)


def dot_nt(a, b):
    return lax.dot_general(a, b, (((1,), (1,)), ((), ())), preferred_element_type=F32)


def kernel(
    regions, tiles, kx_ref, ky_ref, mask_ref, owner_ref, row_ref, col_ref, innov_ref, var_ref, weight_ref,
    control_ref, residual_ref,
    dense, rows_in, left_in, right_in, packed, frame, coef, wsplit, wsend, wrecv, msend, mrecv, expanded,
    pick, pick_t, terms, var_b, z_b, acc, state16, fields, sums_send, sums_tile, sums_mid, sums_region,
    halo_send, halo_recv, w_send_sem, w_recv_sem, m_send_sem, m_recv_sem, t_send_sem, t_recv_sem, r_send_sem, r_recv_sem,
):
    reg, til = lax.axis_index("region"), lax.axis_index("tile")
    up, down = lax.rem(reg + regions - 1, regions), lax.rem(reg + 1, regions)
    left, right = lax.rem(til + tiles - 1, tiles), lax.rem(til + 1, tiles)
    count = owner_ref.shape[1]
    slots = tiles * CAP

    barrier = pltpu.get_barrier_semaphore()

    def greet_tile(i, _):
        pl.semaphore_signal(barrier, inc=1, device_id=(reg, lax.rem(til + i, tiles)), device_id_type=MESH)
        return 0

    def greet_region(i, _):
        pl.semaphore_signal(barrier, inc=1, device_id=(lax.rem(reg + i, regions), til), device_id_type=MESH)
        return 0

    lax.fori_loop(1, tiles, greet_tile, 0)
    lax.fori_loop(1, regions, greet_region, 0)
    for a in (up, down):
        for b in (left, right):
            pl.semaphore_signal(barrier, inc=1, device_id=(a, b), device_id_type=MESH)

    owner = owner_ref[...]
    marks = jnp.where(iota((tiles, count), 0) == owner, 1.0, 0.0)
    upper = jnp.where(iota((count, count), 0) < iota((count, count), 1), 1.0, 0.0).astype(BF16)
    before = dot(marks.astype(BF16), upper)
    slot = owner * CAP + jnp.sum(before * marks, axis=0, keepdims=True).astype(jnp.int32)
    for i, part in enumerate(split(weight_ref[...], 3)):
        wsplit[:, i * LANES:(i + 1) * LANES] = part
    meta_rows = [row_ref[...].astype(F32), col_ref[...].astype(F32)]
    meta_rows += [p.astype(F32) for p in split(innov_ref[...], 3) + split(var_ref[...], 3)]
    meta = jnp.zeros((8, count), F32)
    for i, line in enumerate(meta_rows):
        meta = jnp.where(iota((8, count), 0) == i, line, meta)
    meta = meta.astype(BF16)
    lane8 = iota((8, LANES), 1)
    for b in range(tiles // 4):
        chosen = jnp.where(iota((LANES, count), 0) + b * LANES == slot, 1.0, 0.0).astype(BF16)
        block = dot(chosen, wsplit[...])
        block = block[:, :LANES] + block[:, LANES:2 * LANES] + block[:, 2 * LANES:]
        wsend[4 * b:4 * b + 4] = block.reshape(4, CAP, LANES)
        facts = dot_nt(meta, chosen)
        place = jnp.broadcast_to(facts[0:1] * LANES + facts[1:2], (8, LANES))
        innov = jnp.broadcast_to(facts[2:3] + facts[3:4] + facts[4:5], (8, LANES))
        var = jnp.broadcast_to(facts[5:6] + facts[6:7] + facts[7:8], (8, LANES))
        for k in range(4):
            turned = [pltpu.roll(x, (i - k) * 32 % LANES, 1) for i, x in enumerate((place, innov, var))]
            line = jnp.where(lane8 < 32, turned[0], jnp.where(lane8 < 64, turned[1], jnp.where(lane8 < 96, turned[2], 0.0)))
            msend[4 * b + k] = line[0:1]

    pl.semaphore_wait(barrier, (tiles - 1) + (regions - 1) + 4)

    def peer(i):
        return lax.rem(til + i, tiles)

    def w_copy(i):
        return pltpu.make_async_remote_copy(
            src_ref=wsend.at[peer(i)], dst_ref=wrecv.at[til], send_sem=w_send_sem.at[i], recv_sem=w_recv_sem.at[i],
            device_id=(reg, peer(i)), device_id_type=MESH)

    def m_copy(i):
        return pltpu.make_async_remote_copy(
            src_ref=msend.at[peer(i)], dst_ref=mrecv.at[til], send_sem=m_send_sem.at[i], recv_sem=m_recv_sem.at[i],
            device_id=(reg, peer(i)), device_id_type=MESH)

    def each(lo, hi, act):
        def step(i, _):
            act(i)
            return 0
        lax.fori_loop(lo, hi, step, 0)

    each(1, tiles, lambda i: m_copy(i).start())
    each(1, tiles, lambda i: w_copy(i).start())
    wrecv[til] = wsend[til]
    mrecv[til] = msend[til]

    sub8 = iota((8, LANES), 0)

    def halo_copies(e):
        def copy(n, src, dst, device):
            return pltpu.make_async_remote_copy(
                src_ref=src, dst_ref=dst, send_sem=halo_send.at[e, n], recv_sem=halo_recv.at[e, n],
                device_id=device, device_id_type=MESH)
        return [
            copy(0, dense.at[e, pl.ds(0, 128)], rows_in.at[e, 1], (up, til)),
            copy(1, dense.at[e, pl.ds(384, 128)], rows_in.at[e, 0], (down, til)),
            copy(2, packed.at[e, pl.ds(0, 4)], left_in.at[e, pl.ds(1, 4)], (reg, right)),
            copy(3, packed.at[e, pl.ds(4, 4)], right_in.at[e, pl.ds(1, 4)], (reg, left)),
            copy(4, packed.at[e, 0], left_in.at[e, 5], (up, right)),
            copy(5, packed.at[e, 3], left_in.at[e, 0], (down, right)),
            copy(6, packed.at[e, 4], right_in.at[e, 5], (up, left)),
            copy(7, packed.at[e, 7], right_in.at[e, 0], (down, left)),
        ]

    def halo_start(e):
        for j in range(4):
            to_right = jnp.zeros((8, LANES), F32)
            to_left = jnp.zeros((8, LANES), F32)
            for b in range(4):
                base = (4 * j + b) * 32
                here = (lane8 >= 32 * b) & (lane8 < 32 * b + 32)
                to_right = jnp.where(here, pltpu.roll(dense[e, base + 24:base + 32, :], (b - 3) * 32 % LANES, 1), to_right)
                to_left = jnp.where(here, pltpu.roll(dense[e, base:base + 8, :], b * 32 % LANES, 1), to_left)
            packed[e, j] = to_right
            packed[e, 4 + j] = to_left
        for c in halo_copies(e):
            c.start()

    def halo_finish(e, out):
        for j in range(16):
            out[(4 + j) * WIDE + 8:(5 + j) * WIDE, :] = dense[e, j * 32:(j + 1) * 32, :]
        for c in halo_copies(e):
            c.wait()

    def build_frame(e, out):
        for j in range(4):
            out[j * WIDE + 8:(j + 1) * WIDE, :] = rows_in[e, 0, j * 32:(j + 1) * 32, :]
            out[(20 + j) * WIDE + 8:(21 + j) * WIDE, :] = rows_in[e, 1, j * 32:(j + 1) * 32, :]

        carry = jnp.zeros((8, LANES), F32)
        for k in range(24):
            j, b = k // 4, k % 4
            base = k * WIDE
            from_left = jnp.where(lane8 < 32, pltpu.roll(left_in[e, j], -b * 32 % LANES, 1), pltpu.roll(out[base + 32:base + 40, :], 32, 1))
            from_right = jnp.where(lane8 >= 96, pltpu.roll(right_in[e, j], (3 - b) * 32, 1), pltpu.roll(out[base + 8:base + 16, :], 96, 1))
            out[base:base + 8, :] = jnp.where(sub8 >= 4, from_left, carry)
            carry = from_right
        out[24 * WIDE:24 * WIDE + 8, :] = carry

    def to_cells(source, e):
        group_of_row = iota((LANES, LANES), 0) // 32
        group_of_lane = iota((LANES, LANES), 1) // 32
        fold = jnp.where(iota((32, LANES), 0) == iota((32, LANES), 1) % 32, 1.0, 0.0).astype(BF16)
        for r in range(16):
            line = source[pl.ds(r, 8, stride=16), :].astype(F32)
            many = jnp.where(group_of_row == group_of_lane, jnp.concatenate([line] * 16, axis=0), 0.0)
            total = jnp.zeros((32, LANES), F32)
            for part in split(many, 3):
                total = total + dot_nt(fold, part)
            dense[e, r * 32:(r + 1) * 32, :] = total

    for e, source in enumerate((mask_ref, kx_ref, ky_ref)):
        to_cells(source, e)
        halo_start(e)
    for e in range(3):
        halo_finish(e, coef.at[e])
        if e == 0:
            inside_up = jnp.where(reg > 0, 1.0, 0.0)
            inside_down = jnp.where(reg < regions - 1, 1.0, 0.0)
            inside_left = jnp.where(til > 0, 1.0, 0.0)
            inside_right = jnp.where(til < tiles - 1, 1.0, 0.0)
            rows_in[0, 0] = rows_in[0, 0] * inside_up
            rows_in[0, 1] = rows_in[0, 1] * inside_down
            left_in[0] = left_in[0] * inside_left
            right_in[0] = right_in[0] * inside_right
            for side in (left_in, right_in):
                side[0, 0] = side[0, 0] * inside_up
                side[0, 5] = side[0, 5] * inside_down
        build_frame(e, coef.at[e])

    def make_faces(k, _):
        base = pl.multiple_of(k * WIDE, 8)
        wet = coef[0, pl.ds(base, WIDE), :]
        coef[1, pl.ds(base, WIDE), :] = coef[1, pl.ds(base, WIDE), :] * wet * coef[0, pl.ds(base + WIDE, WIDE), :]
        coef[2, pl.ds(base, WIDE), :] = coef[2, pl.ds(base, WIDE), :] * wet * coef[0, pl.ds(base + 1, WIDE), :]
        return 0

    lax.fori_loop(0, 24, make_faces, 0)

    def make_centre(k, _):
        base = pl.multiple_of(k * WIDE, 8)
        faces = coef[1, pl.ds(base, WIDE), :] + coef[1, pl.ds(base - WIDE, WIDE), :]
        faces = faces + coef[2, pl.ds(base, WIDE), :] + coef[2, pl.ds(base - 1, WIDE), :]
        coef[0, pl.ds(base, WIDE), :] = coef[0, pl.ds(base, WIDE), :] - faces
        return 0

    lax.fori_loop(1, 24, make_centre, 0)

    def stencil(src, base):
        out = coef[0, pl.ds(base, WIDE), :] * frame[src, pl.ds(base, WIDE), :]
        out = out + coef[1, pl.ds(base, WIDE), :] * frame[src, pl.ds(base + WIDE, WIDE), :]
        out = out + coef[1, pl.ds(base - WIDE, WIDE), :] * frame[src, pl.ds(base - WIDE, WIDE), :]
        out = out + coef[2, pl.ds(base, WIDE), :] * frame[src, pl.ds(base + 1, WIDE), :]
        out = out + coef[2, pl.ds(base - 1, WIDE), :] * frame[src, pl.ds(base - 1, WIDE), :]
        return out

    def spread_finish(e, out):
        halo_finish(e, frame.at[0])
        build_frame(e, frame.at[0])
        for step in range(3):
            src, dst = step % 2, (step + 1) % 2

            def line(k, _):
                base = pl.multiple_of(k * WIDE, 8)
                frame[dst, pl.ds(base, WIDE), :] = stencil(src, base)
                return 0

            lax.fori_loop(step + 1, 24 - step, line, 0)

        def last(k, _):
            base = pl.multiple_of(k * WIDE, 8)
            out[pl.ds(pl.multiple_of((k - 4) * 32, 8), 32), :] = stencil(1, base)[8:, :]
            return 0

        lax.fori_loop(4, 20, last, 0)

    each(1, tiles, lambda i: m_copy(i).wait_recv())
    lane = iota((slots, LANES), 1)
    seat = iota((slots, LANES), 0) % CAP
    facts = jnp.broadcast_to(mrecv[...], (tiles, CAP, LANES)).reshape(slots, LANES)
    ones = jnp.ones((3 * LANES, LANES), BF16)

    def spread_lanes(kind):
        parts = split(jnp.where(lane == seat + 32 * kind, facts, 0.0), 3)
        return jnp.concatenate(parts, axis=1)

    place3 = spread_lanes(0)
    place_col = dot(place3, ones).astype(jnp.int32)
    place_row = dot_nt(jnp.ones((8, 3 * LANES), BF16), place3).astype(jnp.int32)[0:1]
    var_b[...] = dot(spread_lanes(2), ones)
    z_b[...] = var_b[...] * dot(spread_lanes(1), ones)

    def corner_of(place, c):
        row = (place >> 7) + c // 2
        col = (place & 127) + c % 2
        return row * 32 + (col & 31), col >> 5

    cells = pick.shape[2]
    for c in range(4):
        cell, _ = corner_of(place_col, c)
        for t in range(cells // LANES):
            pick[c, :, t * LANES:(t + 1) * LANES] = jnp.where(cell == lane + t * LANES, 1.0, 0.0).astype(BF16)
        cell, _ = corner_of(place_row, c)
        pick_t[:, c * slots:(c + 1) * slots] = jnp.where(iota((cells, slots), 0) == cell, 1.0, 0.0).astype(BF16)

    each(1, tiles, lambda i: w_copy(i).wait_recv())
    w3 = jnp.concatenate(split(wrecv[...].reshape(slots, LANES), 3), axis=1)
    for c in range(4):
        copy_lanes = jnp.where(iota((3 * LANES, LANES), 0) % LANES == c * 32 + iota((3 * LANES, LANES), 1) % 32, 1.0, 0.0).astype(BF16)
        _, group = corner_of(place_col, c)
        expanded[c] = jnp.where(group == lane // 32, dot(w3, copy_lanes), 0.0)

    def adjoint(e):
        def one(c, _):
            hi, lo = split(z_b[...] * expanded[c], 2)
            at = pl.ds(pl.multiple_of(c * slots, 128), slots)
            terms[at, :LANES] = hi
            terms[at, LANES:] = lo
            return 0
        lax.fori_loop(0, 4, one, 0)
        total = dot(pick_t[...], terms[...])
        dense[e] = total[:, :LANES] + total[:, LANES:]

    def observe(field):
        hi, lo = split(field, 2)
        state16[:, :LANES] = hi
        state16[:, LANES:] = lo
        acc[...] = jnp.zeros_like(acc)

        def one(c, _):
            values = dot(pick[c], state16[...])
            acc[...] += (values[:, :LANES] + values[:, LANES:]) * expanded[c]
            return 0

        lax.fori_loop(0, 4, one, 0)
        z_b[...] = var_b[...] * dot(jnp.concatenate(split(acc[...], 2), axis=1), ones[:2 * LANES])

    def t_copy(n, i):
        return pltpu.make_async_remote_copy(
            src_ref=sums_send.at[n], dst_ref=sums_tile.at[n, til], send_sem=t_send_sem.at[n, i], recv_sem=t_recv_sem.at[n, i],
            device_id=(reg, peer(i)), device_id_type=MESH)

    def r_copy(n, i):
        return pltpu.make_async_remote_copy(
            src_ref=sums_mid.at[n], dst_ref=sums_region.at[n, reg], send_sem=r_send_sem.at[n, i], recv_sem=r_recv_sem.at[n, i],
            device_id=(lax.rem(reg + i, regions), til), device_id_type=MESH)

    def sums_start(n, products):
        for i, x in enumerate(products):
            sums_send[n, i:i + 1, :] = jnp.sum(x, axis=0, keepdims=True)
        for i in range(len(products), 2):
            sums_send[n, i:i + 1, :] = jnp.zeros((1, LANES), F32)
        each(1, tiles, lambda i: t_copy(n, i).start())
        sums_tile[n, til] = sums_send[n]

    def sums_middle(n):
        each(1, tiles, lambda i: t_copy(n, i).wait())
        sums_mid[n] = jnp.sum(sums_tile[n], axis=0)
        each(1, regions, lambda i: r_copy(n, i).start())
        sums_region[n, reg] = sums_mid[n]

    def sums_finish(n):
        each(1, regions, lambda i: r_copy(n, i).wait())
        total = jnp.sum(sums_region[n], axis=0)
        return jnp.sum(total, axis=1, keepdims=True)

    adjoint(3)
    halo_start(3)
    spread_finish(3, dense.at[4])
    halo_start(4)
    fields[0] = dense[4]
    spread_finish(4, fields.at[1])
    observe(fields[1])
    adjoint(5)
    halo_start(5)
    spread_finish(5, fields.at[2])
    fields[2] = fields[0] + fields[2]
    dense[6] = fields[2]
    halo_start(6)
    sums_start(0, (fields[0] * fields[0], fields[0] * fields[2]))
    spread_finish(6, fields.at[3])
    sums_middle(0)
    found = sums_finish(0)
    norm_0 = found[0:1]
    alpha = norm_0 / found[1:2]
    fields[4] = fields[0] - alpha * fields[2]
    fields[1] = fields[1] - alpha * fields[3]
    sums_start(1, (fields[4] * fields[4],))
    observe(fields[1])
    sums_middle(1)
    adjoint(7)
    halo_start(7)
    norm_1 = sums_finish(1)[0:1]
    beta = norm_1 / norm_0
    spread_finish(7, fields.at[6])
    fields[5] = fields[4] + beta * fields[0]
    fields[6] = fields[4] + fields[6] + beta * fields[2]
    sums_start(2, (fields[5] * fields[6],))
    sums_middle(2)
    alpha_1 = norm_1 / sums_finish(2)[0:1]
    fields[0] = alpha * fields[0] + alpha_1 * fields[5]
    fields[4] = fields[4] - alpha_1 * fields[6]

    group_of_row = iota((LANES, LANES), 0) // 32
    group_of_lane = iota((LANES, LANES), 1) // 32
    slice_of = jnp.where(iota((32, LANES), 0) == iota((32, LANES), 1) % 32, 1.0, 0.0).astype(BF16)
    for at, out in ((0, control_ref), (4, residual_ref)):
        for r in range(16):
            line = fields[at, r * 32:(r + 1) * 32, :]
            many = jnp.where(group_of_row == group_of_lane, jnp.concatenate([line] * 4, axis=0), 0.0)
            total = jnp.zeros((32, LANES), F32)
            for part in split(many, 3):
                total = total + dot_nt(slice_of, part)
            out[pl.ds(r, 32, stride=16), :] = total

    each(1, tiles, lambda i: m_copy(i).wait_send())
    each(1, tiles, lambda i: w_copy(i).wait_send())


def body(regions, tiles, kx, ky, mask, obs_owner, obs_row, obs_col, obs_weight, innovation, inverse_var):
    levels, rows_x, cols_y = kx.shape
    count = obs_row.shape[0]
    slots = tiles * CAP
    cells = rows_x * cols_y // GROUPS
    line = (1, count)
    vmem = pl.BlockSpec(memory_space=pltpu.VMEM)
    out = jax.ShapeDtypeStruct((32 * rows_x, cols_y), F32)
    dma = pltpu.SemaphoreType.DMA
    control, residual = pl.pallas_call(
        functools.partial(kernel, regions, tiles),
        out_shape=(out, out),
        in_specs=[vmem] * 9,
        out_specs=(vmem, vmem),
        scratch_shapes=[
            pltpu.VMEM((8, cells, LANES), F32),
            pltpu.VMEM((8, 2, 128, LANES), F32),
            pltpu.VMEM((8, 6, 8, LANES), F32),
            pltpu.VMEM((8, 6, 8, LANES), F32),
            pltpu.VMEM((8, 8, 8, LANES), F32),
            pltpu.VMEM((2, FRAME_ROWS * WIDE, LANES), F32),
            pltpu.VMEM((3, FRAME_ROWS * WIDE, LANES), F32),
            pltpu.VMEM((count, 3 * LANES), BF16),
            pltpu.VMEM((tiles, CAP, LANES), F32),
            pltpu.VMEM((tiles, CAP, LANES), F32),
            pltpu.VMEM((tiles, 1, LANES), F32),
            pltpu.VMEM((tiles, 1, LANES), F32),
            pltpu.VMEM((4, slots, LANES), F32),
            pltpu.VMEM((4, slots, cells), BF16),
            pltpu.VMEM((cells, 4 * slots), BF16),
            pltpu.VMEM((4 * slots, 2 * LANES), BF16),
            pltpu.VMEM((slots, LANES), F32),
            pltpu.VMEM((slots, LANES), F32),
            pltpu.VMEM((slots, LANES), F32),
            pltpu.VMEM((cells, 2 * LANES), BF16),
            pltpu.VMEM((7, cells, LANES), F32),
            pltpu.VMEM((3, 2, LANES), F32),
            pltpu.VMEM((3, tiles, 2, LANES), F32),
            pltpu.VMEM((3, 2, LANES), F32),
            pltpu.VMEM((3, regions, 2, LANES), F32),
            dma((8, 8)), dma((8, 8)),
            dma((tiles,)), dma((tiles,)), dma((tiles,)), dma((tiles,)),
            dma((3, tiles)), dma((3, tiles)), dma((3, regions)), dma((3, regions)),
        ],
        compiler_params=pltpu.CompilerParams(collective_id=0, has_side_effects=True, vmem_limit_bytes=48 * 1024 * 1024),
    )(
        kx.reshape(levels * rows_x, cols_y), ky.reshape(levels * rows_x, cols_y), mask.reshape(levels * rows_x, cols_y),
        obs_owner.reshape(line), obs_row.reshape(line), obs_col.reshape(line),
        innovation.reshape(line), inverse_var.reshape(line), obs_weight,
    )
    shape = (32 // levels, levels, rows_x, cols_y)
    return control.reshape(shape), residual.reshape(shape)


def solution(mesh):
    return jax.shard_map(
        functools.partial(body, mesh.shape["region"], mesh.shape["tile"]),
        mesh=mesh,
        in_specs=(
            P(None, "region", "tile"),
            P(None, "region", "tile"),
            P(None, "region", "tile"),
            P(("region", "tile"), None),
            P(("region", "tile")),
            P(("region", "tile")),
            P(("region", "tile"), None),
            P(("region", "tile")),
            P(("region", "tile")),
        ),
        out_specs=(P(None, None, "region", "tile"), P(None, None, "region", "tile")),
        check_vma=False,
    )
```

time: 1030 us -> 111 us (0.11); the launches traced: 1020 us -> 110 us
  blocking collectives: 340 us -> 0 us
  waiting for transfers between devices: 275 us -> 0 us
  starting transfers between devices: 237 us -> 0 us
  Pallas kernels: 0 us -> 104 us
  other arithmetic: 100 us -> 0 us
  local copies, waits for them, and re-layouts: 58 us -> 5.58 us
    ppermute x84 -> x0, waiting for transfers between devices: 275 us -> none  [the longest x42 140 us: padded_2(): lax.ppermute(head, axis, [((i + 1) % count, i) for i in range(ends)])]
    psum x3 -> x0, blocking collectives: 232 us -> none  [the longest x2 153 us: squares(): return lax.psum(jnp.sum(residual * residual), ('region', 'tile'))]
    ppermute x84 -> x0, starting transfers between devices: 215 us -> none  [the longest x42 139 us: padded_2(): lax.ppermute(tail, axis, [(i, (i + 1) % count) for i in range(ends)])]
    all_to_all x4 -> x0, blocking collectives: 108 us -> none  [the longest x2 66.5 us: body(): lax.all_to_all(pick_table[corners].reshape(-1, width).reshape(tiles, capa...]
    pallas_call x0 -> x1, Pallas kernels: none -> 104 us  [body(): pl.pallas_call(functools.partial(kernel, regions, tiles), out_shape=(out,...]
    scatter-add x3 -> x0, other arithmetic: 68.7 us -> none  [place(): table = jnp.zeros((rows_x * cols_y, slices), jnp.float32).at[corners.resh...]
    gather x2 -> x0, local copies, waits for them, and re-layouts: 28.4 us -> none  [body(): pick_table[corners].reshape(-1, width).reshape(tiles, capacity, width)]
    all_to_all x2 -> x0, starting transfers between devices: 21.5 us -> none  [the longest x1 12 us: body(): lax.all_to_all(send_places.reshape(tiles, capacity), 'tile', split_axis=0...]
  transfers between devices with their start and end apart: 86 -> 0, of which waited for: 63 -> 0; matrix products, arithmetic and copies ran while one was open for 1% -> 0% of each run, Pallas kernels for 0% -> 0%
where the time goes in v1:
time: 111 us; the launch traced here: 110 us
  Pallas kernels  104 us (94%)
  local copies, waits for them, and re-layouts  5.58 us (5%)
    pallas_call x1, Pallas kernels, body(): pl.pallas_call(functools.partial(kernel, regions, tiles), out_shape=(out,...  104 us
    unnamed x20, local copies, waits for them, and re-layouts  5.58 us

profile of v1, /device:TPU:1, one launch (start us, length us, event | category | flops | bytes accessed | tf_op | source)
XLA Modules:
  0.0 110.5 jit_solution(3493037005455209802)
XLA Ops:
  0.6 0.0 copy-start.8
  0.6 0.0 copy-start.7
  0.7 0.0 copy-start.6
  0.7 0.0 copy-start.5
  0.7 0.0 copy-start.4
  0.7 0.6 copy-done.8
  1.3 0.0 copy-done.7
  1.3 0.0 copy-done.6
  1.3 0.0 copy-done.5
  1.4 0.0 copy-done.4
  1.4 0.0 copy-start
  1.4 0.9 copy-done
  2.3 0.0 copy-start.1
  2.3 0.8 copy-done.1
  3.2 0.0 copy-start.2
  3.2 0.8 copy-done.2
  4.0 0.0 copy-start.3
  4.0 0.8 copy-done.3
  4.8 104.2 %shard_map.104 = (f32[512,128]{1,0:T(8,128)S(1)}, f32[512,128]{1,0:T(8,128)S(1)}) custom-call(f32[128,128]{1,0:T(8,128)S(1)} %bitcast.12, f32[128,128]{1,0:T(8,128)S(1)} %bitcast.13, s32[128,128]{1,0:T(8,128)S(1)} %bitcast.14, s32[1,512]{1,0:T(1,128)S(1)} %bitcast.15, s32[1,512]{1,0:T(1,128)S(1)} %bitcast.16, s32[1,512]{1,0:T(1,128)S(1)} %bitcast.17, ...), custom_call_target="tpu_custom_call" | custom-call | tf_op jit(solution)/shard_map/pallas_call | solution.py:407
  109.1 0.7 copy.13
  109.8 0.7 copy.14
Async XLA Ops:
  0.6 0.7 copy-start.8
  0.6 0.7 copy-start.7
  0.7 0.7 copy-start.6
  0.7 0.7 copy-start.5
  0.7 0.7 copy-start.4
  1.4 0.9 copy-start
  2.3 0.8 copy-start.1
  3.2 0.8 copy-start.2
  4.0 0.8 copy-start.3

commit v2 on v0

v2 whole, which is shorter than its diff:
```python
import functools

import jax
import jax.numpy as jnp
from jax import lax
from jax.experimental import pallas as pl
from jax.experimental.pallas import tpu as pltpu
from jax.sharding import PartitionSpec as P

MESH = pl.DeviceIdType.MESH
F32 = jnp.float32
BF16 = jnp.bfloat16
CAP = 32
LANES = 128
GROUPS = 4
HALO = 8
WIDE = HALO + 32 + HALO
TALL = HALO + 16 + HALO
FRAME = (TALL + 1) * WIDE
EXCHANGES = 6


def iota(shape, dim):
    return lax.broadcasted_iota(jnp.int32, shape, dim)


def split(x, parts):
    out = []
    for i in range(parts):
        part = x.astype(BF16)
        out.append(part)
        if i + 1 < parts:
            x = x - part.astype(F32)
    return out


def dot(a, b):
    return jnp.dot(a, b, preferred_element_type=F32)


def dot_nt(a, b):
    return lax.dot_general(a, b, (((1,), (1,)), ((), ())), preferred_element_type=F32)


def swap_blocks(four):
    lane = iota(four[0].shape, 1)
    low = lane < 64
    even = (lane // 32) % 2 == 0
    a, b, c, d = four
    a, c = jnp.where(low, a, pltpu.roll(c, 64, 1)), jnp.where(low, pltpu.roll(a, 64, 1), c)
    b, d = jnp.where(low, b, pltpu.roll(d, 64, 1)), jnp.where(low, pltpu.roll(b, 64, 1), d)
    a, b = jnp.where(even, a, pltpu.roll(b, 32, 1)), jnp.where(even, pltpu.roll(a, 96, 1), b)
    c, d = jnp.where(even, c, pltpu.roll(d, 32, 1)), jnp.where(even, pltpu.roll(c, 96, 1), d)
    return a, b, c, d


def kernel(
    regions, tiles, kx_any, ky_any, mask_any, owner_any, row_any, col_any, innov_any, var_any, weight_any,
    control_ref, residual_ref,
    kx_ref, ky_ref, mask_ref, owner_ref, row_ref, col_ref, innov_ref, var_ref, weight_ref,
    dense, rows_in, left_in, right_in, packed, frame_a, frame_b, coef, wsplit, wsend, wrecv, msend, mrecv, expanded,
    pick, pick_t, terms, var_b, z_b, q_b, acc, group_b, state16, fields, natural, sums_send, sums_region, sums_mid, sums_tile,
    in_sem, halo_send, halo_recv, w_send_sem, w_recv_sem, m_send_sem, m_recv_sem, r_send_sem, r_recv_sem, t_send_sem, t_recv_sem,
):
    reg, til = lax.axis_index("region"), lax.axis_index("tile")
    up, down = lax.rem(reg + regions - 1, regions), lax.rem(reg + 1, regions)
    left, right = lax.rem(til + tiles - 1, tiles), lax.rem(til + 1, tiles)
    count = owner_ref.shape[1]
    slots = tiles * CAP
    planes = tiles // 4
    late = []

    barrier = pltpu.get_barrier_semaphore()
    for i in range(1, tiles):
        pl.semaphore_signal(barrier, inc=1, device_id=(reg, lax.rem(til + i, tiles)), device_id_type=MESH)
    for i in range(1, regions):
        pl.semaphore_signal(barrier, inc=1, device_id=(lax.rem(reg + i, regions), til), device_id_type=MESH)
    for a in (up, down):
        for b in (left, right):
            pl.semaphore_signal(barrier, inc=1, device_id=(a, b), device_id_type=MESH)

    pairs = (
        (owner_any, owner_ref), (weight_any, weight_ref), (row_any, row_ref), (col_any, col_ref), (innov_any, innov_ref),
        (var_any, var_ref), (mask_any, mask_ref), (kx_any, kx_ref), (ky_any, ky_ref),
    )
    loads = [pltpu.make_async_copy(a, b, in_sem.at[i]) for i, (a, b) in enumerate(pairs)]
    for c in loads:
        c.start()
    for c in loads:
        c.wait()

    owner = owner_ref[...]
    marks = jnp.where(iota((tiles, count), 0) == owner, 1.0, 0.0)
    upper = jnp.where(iota((count, count), 0) < iota((count, count), 1), 1.0, 0.0).astype(BF16)
    before = dot(marks.astype(BF16), upper)
    slot = owner * CAP + jnp.sum(before * marks, axis=0, keepdims=True).astype(jnp.int32)
    for i, part in enumerate(split(weight_ref[...], 3)):
        wsplit[:, i * LANES:(i + 1) * LANES] = part
    meta_rows = [row_ref[...].astype(F32), col_ref[...].astype(F32)]
    meta_rows += [p.astype(F32) for p in split(innov_ref[...], 3) + split(var_ref[...], 3)]
    meta = jnp.zeros((8, count), F32)
    for i, line in enumerate(meta_rows):
        meta = jnp.where(iota((8, count), 0) == i, line, meta)
    meta = meta.astype(BF16)
    lane8 = iota((8, LANES), 1)

    def sort_plane(b, _):
        chosen = jnp.where(iota((LANES, count), 0) + b * LANES == slot, 1.0, 0.0).astype(BF16)
        block = dot(chosen, wsplit[...])
        block = block[:, :LANES] + block[:, LANES:2 * LANES] + block[:, 2 * LANES:]
        wsend[pl.ds(4 * b, 4)] = block.reshape(4, CAP, LANES)
        facts = dot_nt(meta, chosen)
        place = jnp.broadcast_to(facts[0:1] * LANES + facts[1:2], (8, LANES))
        innov = jnp.broadcast_to(facts[2:3] + facts[3:4] + facts[4:5], (8, LANES))
        var = jnp.broadcast_to(facts[5:6] + facts[6:7] + facts[7:8], (8, LANES))
        for k in range(4):
            turned = [pltpu.roll(x, (i - k) * 32 % LANES, 1) for i, x in enumerate((place, innov, var))]
            line = jnp.where(lane8 < 32, turned[0], jnp.where(lane8 < 64, turned[1], jnp.where(lane8 < 96, turned[2], 0.0)))
            msend[4 * b + k] = line[0:1]
        return 0

    lax.fori_loop(0, planes, sort_plane, 0)

    turns = sorted(range(planes), key=lambda i: (min(i, planes - i), i))
    plane, place_in = til // 4, lax.rem(til, 4)

    def sends(src, dst, send_sem, recv_sem):
        out = []
        for j, turn in enumerate(turns):
            for k in range(4):
                if j or k:
                    to = lax.rem(plane + turn, planes) * 4 + lax.rem(place_in + k, 4)
                    n = 4 * j + k
                    out.append(pltpu.make_async_remote_copy(
                        src_ref=src.at[to], dst_ref=dst.at[n], send_sem=send_sem.at[n], recv_sem=recv_sem.at[n],
                        device_id=(reg, to), device_id_type=MESH))
        return out

    m_copies = sends(msend, mrecv, m_send_sem, m_recv_sem)
    w_copies = sends(wsend, wrecv, w_send_sem, w_recv_sem)
    late.extend(m_copies + w_copies)
    pl.semaphore_wait(barrier, (tiles - 1) + (regions - 1) + 4)
    for c in m_copies + w_copies:
        c.start()
    wrecv[0] = wsend[til]
    mrecv[0] = msend[til]

    def halo_copies(e, deep):
        def copy(n, src, dst, device):
            return pltpu.make_async_remote_copy(
                src_ref=src, dst_ref=dst, send_sem=halo_send.at[e, n], recv_sem=halo_recv.at[e, n],
                device_id=device, device_id_type=MESH)
        size, packs = deep * 32, deep // 4
        return [
            copy(4, packed.at[e, pl.ds(0, packs)], left_in.at[e, pl.ds(6, packs)], (up, right)),
            copy(5, packed.at[e, pl.ds(4 - packs, packs)], left_in.at[e, pl.ds(2 - packs, packs)], (down, right)),
            copy(6, packed.at[e, pl.ds(4, packs)], right_in.at[e, pl.ds(6, packs)], (up, left)),
            copy(7, packed.at[e, pl.ds(8 - packs, packs)], right_in.at[e, pl.ds(2 - packs, packs)], (down, left)),
            copy(2, packed.at[e, pl.ds(0, 4)], left_in.at[e, pl.ds(2, 4)], (reg, right)),
            copy(3, packed.at[e, pl.ds(4, 4)], right_in.at[e, pl.ds(2, 4)], (reg, left)),
            copy(0, dense.at[e, pl.ds(0, size)], rows_in.at[e, 1, pl.ds(0, size)], (up, til)),
            copy(1, dense.at[e, pl.ds(512 - size, size)], rows_in.at[e, 0, pl.ds(256 - size, size)], (down, til)),
        ]

    def halo_start(e, deep=8):
        for j in range(4):
            first = swap_blocks([dense[e, (4 * j + b) * 32:(4 * j + b) * 32 + 8, :] for b in range(4)])
            last = swap_blocks([dense[e, (4 * j + b) * 32 + 24:(4 * j + b) * 32 + 32, :] for b in range(4)])
            packed[e, j] = last[3]
            packed[e, 4 + j] = first[0]
        copies = halo_copies(e, deep)
        late.extend(copies)
        for c in copies:
            c.start()
        return copies

    def build_frame(e, copies, out, deep=8):
        for j in range(16):
            out[(8 + j) * WIDE + 16:(9 + j) * WIDE, :] = dense[e, j * 32:(j + 1) * 32, :]
        for c in copies:
            c.wait_recv()
        if e == 0:
            inside_up = jnp.where(reg > 0, 1.0, 0.0)
            inside_down = jnp.where(reg < regions - 1, 1.0, 0.0)
            rows_in[0, 0] = rows_in[0, 0] * inside_up
            rows_in[0, 1] = rows_in[0, 1] * inside_down
            for side, inside in ((left_in, jnp.where(til > 0, 1.0, 0.0)), (right_in, jnp.where(til < tiles - 1, 1.0, 0.0))):
                for j in range(8):
                    side[0, j] = side[0, j] * (inside * inside_up if j < 2 else inside if j < 6 else inside * inside_down)
        for j in range(8 - deep, 8):
            out[j * WIDE + 16:(j + 1) * WIDE, :] = rows_in[e, 0, j * 32:(j + 1) * 32, :]
        for j in range(deep):
            out[(24 + j) * WIDE + 16:(25 + j) * WIDE, :] = rows_in[e, 1, j * 32:(j + 1) * 32, :]

        def four_rows(j, _):
            for b in range(4):
                base = pl.multiple_of((4 * j + b) * WIDE, 8)
                ends, starts = out[pl.ds(base + 40, 8), :], out[pl.ds(base + 16, 8), :]
                out[pl.ds(base + 8, 8), :] = jnp.where(
                    lane8 < 32, pltpu.roll(left_in[e, j], -b * 32 % LANES, 1), pltpu.roll(ends, 32, 1))
                out[pl.ds(base + WIDE, 8), :] = jnp.where(
                    lane8 >= 96, pltpu.roll(right_in[e, j], (3 - b) * 32, 1), pltpu.roll(starts, 96, 1))
            return 0

        lax.fori_loop(2 - deep // 4, 6 + deep // 4, four_rows, 0)

    def to_cells(source, e):
        def four_rows(j, _):
            lines = [source[pl.ds(4 * j + b, 8, stride=16), :].astype(F32) for b in range(4)]
            many = jnp.concatenate([x for x in lines for _ in range(4)], axis=0).T
            for b, x in enumerate(swap_blocks([many[32 * g:32 * g + 32] for g in range(4)])):
                dense[e, pl.ds(pl.multiple_of((4 * j + b) * 32, 32), 32), :] = x
            return 0
        lax.fori_loop(0, 4, four_rows, 0)

    def to_natural(field, out):
        def four_rows(j, _):
            lines = [field[pl.ds(pl.multiple_of((4 * j + b) * 32, 32), 32), :] for b in range(4)]
            many = jnp.concatenate(swap_blocks(lines), axis=0).T
            for b in range(4):
                out[pl.ds(4 * j + b, 32, stride=16), :] = many[32 * b:32 * b + 32]
            return 0
        lax.fori_loop(0, 4, four_rows, 0)

    waiting = []
    for e, source in enumerate((mask_ref, kx_ref, ky_ref)):
        to_cells(source, e)
        waiting.append(halo_start(e))
    for e in range(3):
        build_frame(e, waiting[e], coef.at[e])

    def make_faces(k, _):
        base = pl.multiple_of(k * WIDE, 8)
        wet = coef[0, pl.ds(base, WIDE), :]
        coef[1, pl.ds(base, WIDE), :] = coef[1, pl.ds(base, WIDE), :] * wet * coef[0, pl.ds(base + WIDE, WIDE), :]
        coef[2, pl.ds(base, WIDE), :] = coef[2, pl.ds(base, WIDE), :] * wet * coef[0, pl.ds(base + 1, WIDE), :]
        return 0

    lax.fori_loop(0, TALL, make_faces, 0)

    def make_centre(k, _):
        base = pl.multiple_of(k * WIDE, 8)
        faces = coef[1, pl.ds(base, WIDE), :] + coef[1, pl.ds(base - WIDE, WIDE), :]
        faces = faces + coef[2, pl.ds(base, WIDE), :] + coef[2, pl.ds(base - 1, WIDE), :]
        coef[0, pl.ds(base, WIDE), :] = coef[0, pl.ds(base, WIDE), :] - faces
        return 0

    lax.fori_loop(1, TALL, make_centre, 0)

    def diffuse(first, last):
        for s in range(first, last + 1):
            src, dst = (frame_a, frame_b) if (s - first) % 2 == 0 else (frame_b, frame_a)

            def line(k, carry):
                before, here, west = carry
                base = pl.multiple_of(k * WIDE, 8)
                after = src[pl.ds(base + WIDE, WIDE), :]
                east = coef[1, pl.ds(base, WIDE), :]
                out = coef[0, pl.ds(base, WIDE), :] * here + east * after + west * before
                out = out + coef[2, pl.ds(base, WIDE), :] * src[pl.ds(base + 1, WIDE), :]
                out = out + coef[2, pl.ds(base - 1, WIDE), :] * src[pl.ds(base - 1, WIDE), :]
                dst[pl.ds(base, WIDE), :] = out
                return here, after, east

            at = (s - 1) * WIDE
            lax.fori_loop(s, TALL + 1 - s, line, (src[at:at + WIDE, :], src[at + WIDE:at + 2 * WIDE, :], coef[1, at:at + WIDE, :]))

    def inner(out):
        for j in range(16):
            out[j * 32:(j + 1) * 32, :] = frame_a[(8 + j) * WIDE + 16:(9 + j) * WIDE, :]

    for c in m_copies:
        c.wait_recv()
    lane = iota((LANES, LANES), 1)
    seat = iota((LANES, LANES), 0) % CAP
    ones = jnp.ones((3 * LANES, LANES), BF16)
    cells = pick.shape[2]

    def corner_of(place, c):
        row = (place >> 7) + c // 2
        col = (place & 127) + c % 2
        return row * 32 + (col & 31), col >> 5

    def read_facts(j, _):
        at = pl.ds(pl.multiple_of(j * LANES, LANES), LANES)
        facts = jnp.broadcast_to(mrecv[pl.ds(4 * j, 4)], (4, CAP, LANES)).reshape(LANES, LANES)

        def spread_lanes(kind):
            return jnp.concatenate(split(jnp.where(lane == seat + 32 * kind, facts, 0.0), 3), axis=1)

        place3 = spread_lanes(0)
        place_col = dot(place3, ones).astype(jnp.int32)
        place_row = dot_nt(jnp.ones((8, 3 * LANES), BF16), place3).astype(jnp.int32)[0:1]
        var = dot(spread_lanes(2), ones)
        var_b[at, :] = var
        z_b[at, :] = var * dot(spread_lanes(1), ones)
        for c in range(4):
            cell, group = corner_of(place_col, c)
            group_b[c, at, :] = jnp.where(group == lane // 32, 1.0, 0.0)
            for t in range(cells // LANES):
                pick[c, at, t * LANES:(t + 1) * LANES] = jnp.where(cell == lane + t * LANES, 1.0, 0.0).astype(BF16)
            cell, _ = corner_of(place_row, c)
            there = pl.ds(pl.multiple_of((4 * j + c) * LANES, LANES), LANES)
            pick_t[:, there] = jnp.where(iota((cells, LANES), 0) == cell, 1.0, 0.0).astype(BF16)
        return 0

    lax.fori_loop(0, planes, read_facts, 0)

    def put_terms(j, c):
        at = pl.ds(pl.multiple_of(j * LANES, LANES), LANES)
        there = pl.ds(pl.multiple_of((4 * j + c) * LANES, LANES), LANES)
        hi, lo = split(z_b[at, :] * expanded[c, at, :], 2)
        terms[there, :LANES] = hi
        terms[there, LANES:] = lo

    copy_lanes = jnp.where(
        iota((3 * LANES, 4 * LANES), 0) % LANES == iota((3 * LANES, 4 * LANES), 1) // LANES * 32 + iota((3 * LANES, 4 * LANES), 1) % 32,
        1.0, 0.0).astype(BF16)
    total = jnp.zeros((cells, 2 * LANES), F32)
    for j in range(planes):
        for c in w_copies[max(4 * j - 1, 0):4 * j + 3]:
            c.wait_recv()
        wide = dot(jnp.concatenate(split(wrecv[4 * j:4 * j + 4].reshape(LANES, LANES), 3), axis=1), copy_lanes)
        at = slice(j * LANES, (j + 1) * LANES)
        for c in range(4):
            expanded[c, at, :] = wide[:, c * LANES:(c + 1) * LANES] * group_b[c, at, :]
            put_terms(j, c)
        there = slice(4 * j * LANES, 4 * (j + 1) * LANES)
        total = total + dot(pick_t[:, there], terms[there, :])
    dense[3] = total[:, :LANES] + total[:, LANES:]

    def adjoint(e):
        def one(j, _):
            for c in range(4):
                put_terms(j, c)
            return 0
        lax.fori_loop(0, planes, one, 0)
        total = dot(pick_t[...], terms[...])
        dense[e] = total[:, :LANES] + total[:, LANES:]

    def observe(field, n):
        hi, lo = split(field[...], 2)
        state16[:, :LANES] = hi
        state16[:, LANES:] = lo
        acc[...] = jnp.zeros_like(acc)

        def one(c, _):
            values = dot(pick[c], state16[...])
            acc[...] += (values[:, :LANES] + values[:, LANES:]) * expanded[c]
            return 0

        lax.fori_loop(0, 4, one, 0)
        q = dot(jnp.concatenate(split(acc[...], 2), axis=1), ones[:2 * LANES])
        q_b[n] = q
        z_b[...] = var_b[...] * q

    def r_copies(n):
        return [pltpu.make_async_remote_copy(
            src_ref=sums_send.at[n], dst_ref=sums_region.at[n, i], send_sem=r_send_sem.at[n, i], recv_sem=r_recv_sem.at[n, i],
            device_id=(lax.rem(reg + i, regions), til), device_id_type=MESH) for i in range(1, regions)]

    def t_copies(n):
        return [pltpu.make_async_remote_copy(
            src_ref=sums_mid.at[n], dst_ref=sums_tile.at[n, i], send_sem=t_send_sem.at[n, i], recv_sem=t_recv_sem.at[n, i],
            device_id=(reg, lax.rem(til + i, tiles)), device_id_type=MESH) for i in range(1, tiles)]

    def sums_start(n, sums):
        for i in range(4):
            sums_send[n, i:i + 1, :] = sums[i] if i < len(sums) else jnp.zeros((1, LANES), F32)
        copies = r_copies(n)
        late.extend(copies)
        for c in copies:
            c.start()
        sums_region[n, 0] = sums_send[n]
        return copies

    def sums_middle(n, copies):
        for c in copies:
            c.wait_recv()
        sums_mid[n] = jnp.sum(sums_region[n], axis=0)
        copies = t_copies(n)
        late.extend(copies)
        for c in copies:
            c.start()
        sums_tile[n, 0] = sums_mid[n]
        return copies

    def sums_finish(n, copies):
        for c in copies:
            c.wait_recv()
        return jnp.sum(jnp.sum(sums_tile[n], axis=0), axis=1, keepdims=True)

    def product(a, b):
        return jnp.sum(a * b, axis=0, keepdims=True)

    lane1 = iota((1, LANES), 1)

    def energy(a, b):
        return jnp.where(lane1 == 0, product(var_b[...] * q_b[a], q_b[b]), 0.0)

    copies = halo_start(3)
    build_frame(3, copies, frame_a)
    diffuse(1, 4)
    inner(fields.at[0])
    diffuse(5, 8)
    inner(fields.at[1])

    observe(fields.at[1], 0)
    summing = sums_start(0, (product(fields[0], fields[0]), energy(0, 0)))
    adjoint(4)
    copies = halo_start(4)
    summing = sums_middle(0, summing)
    to_natural(fields.at[0], natural.at[0])
    build_frame(4, copies, frame_a)
    diffuse(1, 4)
    inner(fields.at[2])
    diffuse(5, 8)
    inner(fields.at[4])
    found = sums_finish(0, summing)
    norm_0, energy_0 = found[0:1], found[1:2]
    alpha_0 = norm_0 / (norm_0 + energy_0)
    fields[4] = fields[1] - alpha_0 * (fields[1] + fields[4])

    observe(fields.at[4], 1)
    fields[2] = fields[0] + fields[2]
    fields[3] = fields[0] - alpha_0 * fields[2]
    summing = sums_start(1, (product(fields[3], fields[3]), product(fields[3], fields[0]), energy(1, 1), energy(1, 0)))
    adjoint(5)
    copies = halo_start(5, 4)
    summing = sums_middle(1, summing)
    to_natural(fields.at[2], natural.at[1])
    to_natural(fields.at[3], natural.at[2])
    build_frame(5, copies, frame_a, 4)
    diffuse(5, 8)
    inner(fields.at[5])
    to_natural(fields.at[5], natural.at[3])
    found = sums_finish(1, summing)
    norm_1 = found[0:1]
    beta = norm_1 / norm_0
    curve = norm_1 + 2.0 * beta * found[1:2] + beta * beta * norm_0 + found[2:3] + 2.0 * beta * found[3:4] + beta * beta * energy_0
    alpha_1 = norm_1 / curve
    control_ref[...] = (alpha_0 + alpha_1 * beta) * natural[0] + alpha_1 * natural[2]
    residual_ref[...] = natural[2] - alpha_1 * (natural[2] + natural[3] + beta * natural[1])

    for c in late:
        c.wait_send()


def body(regions, tiles, kx, ky, mask, obs_owner, obs_row, obs_col, obs_weight, innovation, inverse_var):
    levels, rows_x, cols_y = kx.shape
    count = obs_row.shape[0]
    slots = tiles * CAP
    cells = rows_x * cols_y // GROUPS
    line, flat = (1, count), (levels * rows_x, cols_y)
    out = jax.ShapeDtypeStruct((32 * rows_x, cols_y), F32)
    dma = pltpu.SemaphoreType.DMA
    args = (
        kx.reshape(flat), ky.reshape(flat), mask.reshape(flat), obs_owner.reshape(line), obs_row.reshape(line),
        obs_col.reshape(line), innovation.reshape(line), inverse_var.reshape(line), obs_weight,
    )
    control, residual = pl.pallas_call(
        functools.partial(kernel, regions, tiles),
        out_shape=(out, out),
        in_specs=[pl.BlockSpec(memory_space=pl.ANY)] * 9,
        out_specs=[pl.BlockSpec(memory_space=pltpu.VMEM)] * 2,
        scratch_shapes=[
            *[pltpu.VMEM(x.shape, x.dtype) for x in args],
            pltpu.VMEM((EXCHANGES, cells, LANES), F32),
            pltpu.VMEM((EXCHANGES, 2, 32 * HALO, LANES), F32),
            pltpu.VMEM((EXCHANGES, 8, 8, LANES), F32),
            pltpu.VMEM((EXCHANGES, 8, 8, LANES), F32),
            pltpu.VMEM((EXCHANGES, 8, 8, LANES), F32),
            pltpu.VMEM((FRAME, LANES), F32),
            pltpu.VMEM((FRAME, LANES), F32),
            pltpu.VMEM((3, FRAME, LANES), F32),
            pltpu.VMEM((count, 3 * LANES), BF16),
            pltpu.VMEM((tiles, CAP, LANES), F32),
            pltpu.VMEM((tiles, CAP, LANES), F32),
            pltpu.VMEM((tiles, 1, LANES), F32),
            pltpu.VMEM((tiles, 1, LANES), F32),
            pltpu.VMEM((4, slots, LANES), F32),
            pltpu.VMEM((4, slots, cells), BF16),
            pltpu.VMEM((cells, 4 * slots), BF16),
            pltpu.VMEM((4 * slots, 2 * LANES), BF16),
            pltpu.VMEM((slots, LANES), F32),
            pltpu.VMEM((slots, LANES), F32),
            pltpu.VMEM((2, slots, LANES), F32),
            pltpu.VMEM((slots, LANES), F32),
            pltpu.VMEM((4, slots, LANES), F32),
            pltpu.VMEM((cells, 2 * LANES), BF16),
            pltpu.VMEM((6, cells, LANES), F32),
            pltpu.VMEM((4, cells, LANES), F32),
            pltpu.VMEM((2, 4, LANES), F32),
            pltpu.VMEM((2, regions, 4, LANES), F32),
            pltpu.VMEM((2, 4, LANES), F32),
            pltpu.VMEM((2, tiles, 4, LANES), F32),
            dma((9,)), dma((EXCHANGES, 8)), dma((EXCHANGES, 8)),
            dma((tiles,)), dma((tiles,)), dma((tiles,)), dma((tiles,)),
            dma((2, regions)), dma((2, regions)), dma((2, tiles)), dma((2, tiles)),
        ],
        compiler_params=pltpu.CompilerParams(collective_id=0, has_side_effects=True, vmem_limit_bytes=48 * 1024 * 1024),
    )(*args)
    shape = (32 // levels, levels, rows_x, cols_y)
    return control.reshape(shape), residual.reshape(shape)


def solution(mesh):
    return jax.shard_map(
        functools.partial(body, mesh.shape["region"], mesh.shape["tile"]),
        mesh=mesh,
        in_specs=(
            P(None, "region", "tile"),
            P(None, "region", "tile"),
            P(None, "region", "tile"),
            P(("region", "tile"), None),
            P(("region", "tile")),
            P(("region", "tile")),
            P(("region", "tile"), None),
            P(("region", "tile")),
            P(("region", "tile")),
        ),
        out_specs=(P(None, None, "region", "tile"), P(None, None, "region", "tile")),
        check_vma=False,
    )
```

time: 1030 us -> 84.2 us (0.08); the launches traced: 1020 us -> 84 us
  blocking collectives: 340 us -> 0 us
  waiting for transfers between devices: 275 us -> 0 us
  starting transfers between devices: 237 us -> 0 us
  other arithmetic: 100 us -> 0 us
  Pallas kernels: 0 us -> 77.7 us
  local copies, waits for them, and re-layouts: 58 us -> 5.58 us
    ppermute x84 -> x0, waiting for transfers between devices: 275 us -> none  [the longest x42 140 us: padded_2(): lax.ppermute(head, axis, [((i + 1) % count, i) for i in range(ends)])]
    psum x3 -> x0, blocking collectives: 232 us -> none  [the longest x2 153 us: squares(): return lax.psum(jnp.sum(residual * residual), ('region', 'tile'))]
    ppermute x84 -> x0, starting transfers between devices: 215 us -> none  [the longest x42 139 us: padded_2(): lax.ppermute(tail, axis, [(i, (i + 1) % count) for i in range(ends)])]
    all_to_all x4 -> x0, blocking collectives: 108 us -> none  [the longest x2 66.5 us: body(): lax.all_to_all(pick_table[corners].reshape(-1, width).reshape(tiles, capa...]
    pallas_call x0 -> x1, Pallas kernels: none -> 77.7 us  [body(): pl.pallas_call(functools.partial(kernel, regions, tiles), out_shape=(out,...]
    scatter-add x3 -> x0, other arithmetic: 68.7 us -> none  [place(): table = jnp.zeros((rows_x * cols_y, slices), jnp.float32).at[corners.resh...]
    gather x2 -> x0, local copies, waits for them, and re-layouts: 28.4 us -> none  [body(): pick_table[corners].reshape(-1, width).reshape(tiles, capacity, width)]
    all_to_all x2 -> x0, starting transfers between devices: 21.5 us -> none  [the longest x1 12 us: body(): lax.all_to_all(send_places.reshape(tiles, capacity), 'tile', split_axis=0...]
  transfers between devices with their start and end apart: 86 -> 0, of which waited for: 63 -> 0; matrix products, arithmetic and copies ran while one was open for 1% -> 0% of each run, Pallas kernels for 0% -> 0%
where the time goes in v2:
time: 84.2 us; the launch traced here: 84 us
  Pallas kernels  77.7 us (92%)
  local copies, waits for them, and re-layouts  5.58 us (7%)
    pallas_call x1, Pallas kernels, body(): pl.pallas_call(functools.partial(kernel, regions, tiles), out_shape=(out,...  77.7 us
    unnamed x20, local copies, waits for them, and re-layouts  5.58 us

profile of v2, /device:TPU:1, one launch (start us, length us, event | category | flops | bytes accessed | tf_op | source)
XLA Modules:
  0.0 84.0 jit_solution(16458022400887366523)
XLA Ops:
  0.6 0.0 copy-start.8
  0.6 0.0 copy-start.7
  0.7 0.0 copy-start.6
  0.7 0.0 copy-start.5
  0.7 0.0 copy-start.4
  0.7 0.6 copy-done.8
  1.3 0.0 copy-done.7
  1.3 0.0 copy-done.6
  1.3 0.0 copy-done.5
  1.4 0.0 copy-done.4
  1.4 0.0 copy-start
  1.4 0.9 %copy-done = f32[512,128]{1,0:T(8,128)S(1)} copy-done((f32[512,128]{1,0:T(8,128)S(1)}, f32[512,128]{1,0:T(8,128)}, u32[]{:S(2)}) %copy-start) | copy-done | bytes 262168
  2.3 0.0 copy-start.1
  2.3 0.8 copy-done.1
  3.2 0.0 copy-start.2
  3.2 0.8 copy-done.2
  4.0 0.0 copy-start.3
  4.0 0.8 copy-done.3
  4.8 77.7 %shard_map.104 = (f32[512,128]{1,0:T(8,128)S(1)}, f32[512,128]{1,0:T(8,128)S(1)}) custom-call(f32[128,128]{1,0:T(8,128)S(1)} %bitcast.12, f32[128,128]{1,0:T(8,128)S(1)} %bitcast.13, s32[128,128]{1,0:T(8,128)S(1)} %bitcast.14, s32[1,512]{1,0:T(1,128)S(1)} %bitcast.15, s32[1,512]{1,0:T(1,128)S(1)} %bitcast.16, s32[1,512]{1,0:T(1,128)S(1)} %bitcast.17, ...), custom_call_target="tpu_custom_call" | custom-call | tf_op jit(solution)/shard_map/pallas_call | solution.py:461
  82.5 0.7 copy.13
  83.3 0.7 copy.14
Async XLA Ops:
  0.6 0.7 copy-start.8
  0.6 0.7 copy-start.7
  0.7 0.7 copy-start.6
  0.7 0.7 copy-start.5
  0.7 0.7 copy-start.4
  1.4 0.9 %copy-start = (f32[512,128]{1,0:T(8,128)S(1)}, f32[512,128]{1,0:T(8,128)}, u32[]{:S(2)}) copy-start(f32[512,128]{1,0:T(8,128)} %weight_any.1) | copy-start | bytes 786436
  2.3 0.8 copy-start.1
  3.2 0.8 copy-start.2
  4.0 0.8 copy-start.3

commit v3 on v2

--- a/solution.py
+++ b/solution.py
@@ -80,14 +80,121 @@
             pl.semaphore_signal(barrier, inc=1, device_id=(a, b), device_id_type=MESH)
 
     pairs = (
-        (owner_any, owner_ref), (weight_any, weight_ref), (row_any, row_ref), (col_any, col_ref), (innov_any, innov_ref),
-        (var_any, var_ref), (mask_any, mask_ref), (kx_any, kx_ref), (ky_any, ky_ref),
+        (mask_any, mask_ref), (kx_any, kx_ref), (ky_any, ky_ref), (owner_any, owner_ref), (row_any, row_ref), (col_any, col_ref),
+        (innov_any, innov_ref), (var_any, var_ref), (weight_any, weight_ref),
     )
     loads = [pltpu.make_async_copy(a, b, in_sem.at[i]) for i, (a, b) in enumerate(pairs)]
     for c in loads:
         c.start()
     for c in loads:
         c.wait()
+    lane8 = iota((8, LANES), 1)
+
+    def halo_copies(e, deep, fields):
+        def copy(n, src, dst, device):
+            return pltpu.make_async_remote_copy(
+                src_ref=src, dst_ref=dst, send_sem=halo_send.at[e, n], recv_sem=halo_recv.at[e, n],
+                device_id=device, device_id_type=MESH)
+        size, packs, at = deep * 32, deep // 4, pl.ds(e, fields)
+        return [
+            copy(4, packed.at[at, pl.ds(0, packs)], left_in.at[at, pl.ds(6, packs)], (up, right)),
+            copy(5, packed.at[at, pl.ds(4 - packs, packs)], left_in.at[at, pl.ds(2 - packs, packs)], (down, right)),
+            copy(6, packed.at[at, pl.ds(4, packs)], right_in.at[at, pl.ds(6, packs)], (up, left)),
+            copy(7, packed.at[at, pl.ds(8 - packs, packs)], right_in.at[at, pl.ds(2 - packs, packs)], (down, left)),
+            copy(2, packed.at[at, pl.ds(0, 4)], left_in.at[at, pl.ds(2, 4)], (reg, right)),
+            copy(3, packed.at[at, pl.ds(4, 4)], right_in.at[at, pl.ds(2, 4)], (reg, left)),
+            copy(0, dense.at[at, pl.ds(0, size)], rows_in.at[at, 1, pl.ds(0, size)], (up, til)),
+            copy(1, dense.at[at, pl.ds(512 - size, size)], rows_in.at[at, 0, pl.ds(256 - size, size)], (down, til)),
+        ]
+
+    def halo_pack(e):
+        for j in range(4):
+            first = swap_blocks([dense[e, (4 * j + b) * 32:(4 * j + b) * 32 + 8, :] for b in range(4)])
+            last = swap_blocks([dense[e, (4 * j + b) * 32 + 24:(4 * j + b) * 32 + 32, :] for b in range(4)])
+            packed[e, j] = last[3]
+            packed[e, 4 + j] = first[0]
+
+    def halo_start(e, deep=8, fields=1):
+        copies = halo_copies(e, deep, fields)
+        late.extend(copies)
+        for c in copies:
+            c.start()
+        return copies
+
+    def frame_own(e, out):
+        def four_rows(j, _):
+            for b in range(4):
+                row = 4 * j + b
+                base = pl.multiple_of((row + 8) * WIDE, 8)
+                own = dense[e, pl.ds(pl.multiple_of(row * 32, 32), 32), :]
+                out[pl.ds(base + 16, 32), :] = own
+                out[pl.ds(base + 8, 8), :] = pltpu.roll(own[24:], 32, 1)
+                out[pl.ds(base + WIDE, 8), :] = pltpu.roll(own[:8], 96, 1)
+            return 0
+        lax.fori_loop(0, 4, four_rows, 0)
+
+    def frame_halo(e, out, deep=8):
+        if e == 0:
+            inside_up = jnp.where(reg > 0, 1.0, 0.0)
+            inside_down = jnp.where(reg < regions - 1, 1.0, 0.0)
+            rows_in[0, 0] = rows_in[0, 0] * inside_up
+            rows_in[0, 1] = rows_in[0, 1] * inside_down
+            for side, inside in ((left_in, jnp.where(til > 0, 1.0, 0.0)), (right_in, jnp.where(til < tiles - 1, 1.0, 0.0))):
+                for j in range(8):
+                    side[0, j] = side[0, j] * (inside * inside_up if j < 2 else inside if j < 6 else inside * inside_down)
+
+        def beside(j, b):
+            return pltpu.roll(left_in[e, j], -b * 32 % LANES, 1), pltpu.roll(right_in[e, j], (3 - b) * 32, 1)
+
+        def own_rows(j, _):
+            for b in range(4):
+                base = pl.multiple_of((4 * j + b) * WIDE, 8)
+                start, end = beside(j, b)
+                out[pl.ds(base + 8, 8), :] = jnp.where(lane8 < 32, start, out[pl.ds(base + 8, 8), :])
+                out[pl.ds(base + WIDE, 8), :] = jnp.where(lane8 >= 96, end, out[pl.ds(base + WIDE, 8), :])
+            return 0
+
+        lax.fori_loop(2, 6, own_rows, 0)
+        for side in range(2):
+            def outer_rows(j, _):
+                for b in range(4):
+                    row = 4 * j + b
+                    base = pl.multiple_of((row + 24 * side) * WIDE, 8)
+                    came = rows_in[e, side, pl.ds(pl.multiple_of(row * 32, 32), 32), :]
+                    start, end = beside(j + 6 * side, b)
+                    out[pl.ds(base + 16, 32), :] = came
+                    out[pl.ds(base + 8, 8), :] = jnp.where(lane8 < 32, start, pltpu.roll(came[24:], 32, 1))
+                    out[pl.ds(base + WIDE, 8), :] = jnp.where(lane8 >= 96, end, pltpu.roll(came[:8], 96, 1))
+                return 0
+            lax.fori_loop(0 if side else 2 - deep // 4, deep // 4 if side else 2, outer_rows, 0)
+
+    def build_frame(e, copies, out, deep=8):
+        frame_own(e, out)
+        for c in copies:
+            c.wait_recv()
+        frame_halo(e, out, deep)
+
+    def to_cells(source, e):
+        def four_rows(j, _):
+            lines = [source[pl.ds(4 * j + b, 8, stride=16), :].astype(F32) for b in range(4)]
+            many = jnp.concatenate([x for x in lines for _ in range(4)], axis=0).T
+            for b, x in enumerate(swap_blocks([many[32 * g:32 * g + 32] for g in range(4)])):
+                dense[e, pl.ds(pl.multiple_of((4 * j + b) * 32, 32), 32), :] = x
+            return 0
+        lax.fori_loop(0, 4, four_rows, 0)
+
+    def to_natural(field, out):
+        def four_rows(j, _):
+            lines = [field[pl.ds(pl.multiple_of((4 * j + b) * 32, 32), 32), :] for b in range(4)]
+            many = jnp.concatenate(swap_blocks(lines), axis=0).T
+            for b in range(4):
+                out[pl.ds(4 * j + b, 32, stride=16), :] = many[32 * b:32 * b + 32]
+            return 0
+        lax.fori_loop(0, 4, four_rows, 0)
+
+    for e, source in enumerate((mask_ref, kx_ref, ky_ref)):
+        to_cells(source, e)
+        halo_pack(e)
 
     owner = owner_ref[...]
     marks = jnp.where(iota((tiles, count), 0) == owner, 1.0, 0.0)
@@ -102,7 +209,6 @@
     for i, line in enumerate(meta_rows):
         meta = jnp.where(iota((8, count), 0) == i, line, meta)
     meta = meta.astype(BF16)
-    lane8 = iota((8, LANES), 1)
 
     def sort_plane(b, _):
         chosen = jnp.where(iota((LANES, count), 0) + b * LANES == slot, 1.0, 0.0).astype(BF16)
@@ -140,94 +246,18 @@
     w_copies = sends(wsend, wrecv, w_send_sem, w_recv_sem)
     late.extend(m_copies + w_copies)
     pl.semaphore_wait(barrier, (tiles - 1) + (regions - 1) + 4)
+    copies = halo_start(0, 8, 3)
     for c in m_copies + w_copies:
         c.start()
     wrecv[0] = wsend[til]
     mrecv[0] = msend[til]
 
-    def halo_copies(e, deep):
-        def copy(n, src, dst, device):
-            return pltpu.make_async_remote_copy(
-                src_ref=src, dst_ref=dst, send_sem=halo_send.at[e, n], recv_sem=halo_recv.at[e, n],
-                device_id=device, device_id_type=MESH)
-        size, packs = deep * 32, deep // 4
-        return [
-            copy(4, packed.at[e, pl.ds(0, packs)], left_in.at[e, pl.ds(6, packs)], (up, right)),
-            copy(5, packed.at[e, pl.ds(4 - packs, packs)], left_in.at[e, pl.ds(2 - packs, packs)], (down, right)),
-            copy(6, packed.at[e, pl.ds(4, packs)], right_in.at[e, pl.ds(6, packs)], (up, left)),
-            copy(7, packed.at[e, pl.ds(8 - packs, packs)], right_in.at[e, pl.ds(2 - packs, packs)], (down, left)),
-            copy(2, packed.at[e, pl.ds(0, 4)], left_in.at[e, pl.ds(2, 4)], (reg, right)),
-            copy(3, packed.at[e, pl.ds(4, 4)], right_in.at[e, pl.ds(2, 4)], (reg, left)),
-            copy(0, dense.at[e, pl.ds(0, size)], rows_in.at[e, 1, pl.ds(0, size)], (up, til)),
-            copy(1, dense.at[e, pl.ds(512 - size, size)], rows_in.at[e, 0, pl.ds(256 - size, size)], (down, til)),
-        ]
-
-    def halo_start(e, deep=8):
-        for j in range(4):
-            first = swap_blocks([dense[e, (4 * j + b) * 32:(4 * j + b) * 32 + 8, :] for b in range(4)])
-            last = swap_blocks([dense[e, (4 * j + b) * 32 + 24:(4 * j + b) * 32 + 32, :] for b in range(4)])
-            packed[e, j] = last[3]
-            packed[e, 4 + j] = first[0]
-        copies = halo_copies(e, deep)
-        late.extend(copies)
-        for c in copies:
-            c.start()
-        return copies
-
-    def build_frame(e, copies, out, deep=8):
-        for j in range(16):
-            out[(8 + j) * WIDE + 16:(9 + j) * WIDE, :] = dense[e, j * 32:(j + 1) * 32, :]
-        for c in copies:
-            c.wait_recv()
-        if e == 0:
-            inside_up = jnp.where(reg > 0, 1.0, 0.0)
-            inside_down = jnp.where(reg < regions - 1, 1.0, 0.0)
-            rows_in[0, 0] = rows_in[0, 0] * inside_up
-            rows_in[0, 1] = rows_in[0, 1] * inside_down
-            for side, inside in ((left_in, jnp.where(til > 0, 1.0, 0.0)), (right_in, jnp.where(til < tiles - 1, 1.0, 0.0))):
-                for j in range(8):
-                    side[0, j] = side[0, j] * (inside * inside_up if j < 2 else inside if j < 6 else inside * inside_down)
-        for j in range(8 - deep, 8):
-            out[j * WIDE + 16:(j + 1) * WIDE, :] = rows_in[e, 0, j * 32:(j + 1) * 32, :]
-        for j in range(deep):
-            out[(24 + j) * WIDE + 16:(25 + j) * WIDE, :] = rows_in[e, 1, j * 32:(j + 1) * 32, :]
-
-        def four_rows(j, _):
-            for b in range(4):
-                base = pl.multiple_of((4 * j + b) * WIDE, 8)
-                ends, starts = out[pl.ds(base + 40, 8), :], out[pl.ds(base + 16, 8), :]
-                out[pl.ds(base + 8, 8), :] = jnp.where(
-                    lane8 < 32, pltpu.roll(left_in[e, j], -b * 32 % LANES, 1), pltpu.roll(ends, 32, 1))
-                out[pl.ds(base + WIDE, 8), :] = jnp.where(
-                    lane8 >= 96, pltpu.roll(right_in[e, j], (3 - b) * 32, 1), pltpu.roll(starts, 96, 1))
-            return 0
-
-        lax.fori_loop(2 - deep // 4, 6 + deep // 4, four_rows, 0)
-
-    def to_cells(source, e):
-        def four_rows(j, _):
-            lines = [source[pl.ds(4 * j + b, 8, stride=16), :].astype(F32) for b in range(4)]
-            many = jnp.concatenate([x for x in lines for _ in range(4)], axis=0).T
-            for b, x in enumerate(swap_blocks([many[32 * g:32 * g + 32] for g in range(4)])):
-                dense[e, pl.ds(pl.multiple_of((4 * j + b) * 32, 32), 32), :] = x
-            return 0
-        lax.fori_loop(0, 4, four_rows, 0)
-
-    def to_natural(field, out):
-        def four_rows(j, _):
-            lines = [field[pl.ds(pl.multiple_of((4 * j + b) * 32, 32), 32), :] for b in range(4)]
-            many = jnp.concatenate(swap_blocks(lines), axis=0).T
-            for b in range(4):
-                out[pl.ds(4 * j + b, 32, stride=16), :] = many[32 * b:32 * b + 32]
-            return 0
-        lax.fori_loop(0, 4, four_rows, 0)
-
-    waiting = []
-    for e, source in enumerate((mask_ref, kx_ref, ky_ref)):
-        to_cells(source, e)
-        waiting.append(halo_start(e))
     for e in range(3):
-        build_frame(e, waiting[e], coef.at[e])
+        frame_own(e, coef.at[e])
+    for c in copies:
+        c.wait_recv()
+    for e in range(3):
+        frame_halo(e, coef.at[e])
 
     def make_faces(k, _):
         base = pl.multiple_of(k * WIDE, 8)
@@ -316,18 +346,28 @@
     copy_lanes = jnp.where(
         iota((3 * LANES, 4 * LANES), 0) % LANES == iota((3 * LANES, 4 * LANES), 1) // LANES * 32 + iota((3 * LANES, 4 * LANES), 1) % 32,
         1.0, 0.0).astype(BF16)
-    total = jnp.zeros((cells, 2 * LANES), F32)
-    for j in range(planes):
-        for c in w_copies[max(4 * j - 1, 0):4 * j + 3]:
-            c.wait_recv()
-        wide = dot(jnp.concatenate(split(wrecv[4 * j:4 * j + 4].reshape(LANES, LANES), 3), axis=1), copy_lanes)
-        at = slice(j * LANES, (j + 1) * LANES)
+    def take_plane(j, first):
+        for k in range(first, 4):
+            n = 4 * j + k
+            pltpu.make_async_remote_copy(
+                src_ref=wsend.at[n], dst_ref=wrecv.at[n], send_sem=w_send_sem.at[n], recv_sem=w_recv_sem.at[n],
+                device_id=(reg, left), device_id_type=MESH).wait_recv()
+        wide = dot(jnp.concatenate(split(wrecv[pl.ds(4 * j, 4)].reshape(LANES, LANES), 3), axis=1), copy_lanes)
+        at = pl.ds(pl.multiple_of(j * LANES, LANES), LANES)
         for c in range(4):
             expanded[c, at, :] = wide[:, c * LANES:(c + 1) * LANES] * group_b[c, at, :]
             put_terms(j, c)
-        there = slice(4 * j * LANES, 4 * (j + 1) * LANES)
-        total = total + dot(pick_t[:, there], terms[there, :])
-    dense[3] = total[:, :LANES] + total[:, LANES:]
+        there = pl.ds(pl.multiple_of(4 * j * LANES, LANES), 4 * LANES)
+        part = dot(pick_t[:, there], terms[there, :])
+        return part[:, :LANES] + part[:, LANES:]
+
+    dense[3] = take_plane(0, 1)
+
+    def later_plane(j, _):
+        dense[3] = dense[3] + take_plane(j, 0)
+        return 0
+
+    lax.fori_loop(1, planes, later_plane, 0)
 
     def adjoint(e):
         def one(j, _):
@@ -398,6 +438,7 @@
     def energy(a, b):
         return jnp.where(lane1 == 0, product(var_b[...] * q_b[a], q_b[b]), 0.0)
 
+    halo_pack(3)
     copies = halo_start(3)
     build_frame(3, copies, frame_a)
     diffuse(1, 4)
@@ -408,6 +449,7 @@
     observe(fields.at[1], 0)
     summing = sums_start(0, (product(fields[0], fields[0]), energy(0, 0)))
     adjoint(4)
+    halo_pack(4)
     copies = halo_start(4)
     summing = sums_middle(0, summing)
     to_natural(fields.at[0], natural.at[0])
@@ -426,6 +468,7 @@
     fields[3] = fields[0] - alpha_0 * fields[2]
     summing = sums_start(1, (product(fields[3], fields[3]), product(fields[3], fields[0]), energy(1, 1), energy(1, 0)))
     adjoint(5)
+    halo_pack(5)
     copies = halo_start(5, 4)
     summing = sums_middle(1, summing)
     to_natural(fields.at[2], natural.at[1])
@@ -498,7 +541,7 @@
             dma((tiles,)), dma((tiles,)), dma((tiles,)), dma((tiles,)),
             dma((2, regions)), dma((2, regions)), dma((2, tiles)), dma((2, tiles)),
         ],
-        compiler_params=pltpu.CompilerParams(collective_id=0, has_side_effects=True, vmem_limit_bytes=48 * 1024 * 1024),
+        compiler_params=pltpu.CompilerParams(collective_id=0, has_side_effects=True, vmem_limit_bytes=60 * 1024 * 1024),
     )(*args)
     shape = (32 // levels, levels, rows_x, cols_y)
     return control.reshape(shape), residual.reshape(shape)

time: 84.2 us -> 76.8 us (0.912)
  Pallas kernels: 77.7 us -> 73.6 us
  local copies, waits for them, and re-layouts: 5.58 us -> 2.42 us
    pallas_call x1, Pallas kernels: 77.7 us -> 73.6 us  [body(): pl.pallas_call(functools.partial(kernel, regions, tiles), out_shape=(out,...]
    unnamed x20 -> x4, local copies, waits for them, and re-layouts: 5.58 us -> 2.42 us
where the time goes in v3:
time: 76.8 us; the launch traced here: 76.7 us
  Pallas kernels  73.6 us (96%)
  local copies, waits for them, and re-layouts  2.42 us (3%)
    pallas_call x1, Pallas kernels, body(): pl.pallas_call(functools.partial(kernel, regions, tiles), out_shape=(out,...  73.6 us
    unnamed x4, local copies, waits for them, and re-layouts  2.42 us

profile of v3, /device:TPU:1, one launch (start us, length us, event | category | flops | bytes accessed | tf_op | source)
XLA Modules:
  0.0 76.7 jit_solution(5349305662542268352)
XLA Ops:
  0.6 73.6 %shard_map.104 = (f32[512,128]{1,0:T(8,128)}, f32[512,128]{1,0:T(8,128)}) custom-call(f32[128,128]{1,0:T(8,128)} %bitcast.12, f32[128,128]{1,0:T(8,128)} %bitcast.13, s32[128,128]{1,0:T(8,128)} %bitcast.14, s32[1,512]{1,0:T(1,128)} %bitcast.15, s32[1,512]{1,0:T(1,128)} %bitcast.16, s32[1,512]{1,0:T(1,128)} %bitcast.17, f32[1,512]{1,0:T(1,128)} %bitcast.18, ...), custom_call_target="tpu_custom_call" | custom-call | tf_op jit(solution)/shard_map/pallas_call | solution.py:504
  74.3 0.0 copy-start
  74.3 1.7 %copy.13 = f32[4,8,16,128]{3,2,1,0:T(8,128)} copy(f32[4,8,16,128]{3,2,1,0:T(8,128)} %bitcast.11) | data formatting | bytes 524288
  76.0 0.0 copy-done
  76.0 0.7 copy.14
Async XLA Ops:
  74.3 1.7 %copy-start = (f32[512,128]{1,0:T(8,128)S(1)}, f32[512,128]{1,0:T(8,128)}, u32[]{:S(2)}) copy-start(f32[512,128]{1,0:T(8,128)} %get-tuple-element.5) | copy-start | bytes 786436

commit v4 on v3

--- a/solution.py
+++ b/solution.py
@@ -16,7 +16,8 @@
 HALO = 8
 WIDE = HALO + 32 + HALO
 TALL = HALO + 16 + HALO
-FRAME = (TALL + 1) * WIDE
+ROWS_AT_ONCE = 3
+FRAME = (TALL + 3) * WIDE
 EXCHANGES = 6
 
 
@@ -58,7 +59,7 @@
     regions, tiles, kx_any, ky_any, mask_any, owner_any, row_any, col_any, innov_any, var_any, weight_any,
     control_ref, residual_ref,
     kx_ref, ky_ref, mask_ref, owner_ref, row_ref, col_ref, innov_ref, var_ref, weight_ref,
-    dense, rows_in, left_in, right_in, packed, frame_a, frame_b, coef, wsplit, wsend, wrecv, msend, mrecv, expanded,
+    dense, rows_in, left_in, right_in, packed, frame_a, frame_b, coef, wsplit, wsend, wrecv, msend, mrecv, expanded, expanded_0, coef_rows, coef_in,
     pick, pick_t, terms, var_b, z_b, q_b, acc, group_b, state16, fields, natural, sums_send, sums_region, sums_mid, sums_tile,
     in_sem, halo_send, halo_recv, w_send_sem, w_recv_sem, m_send_sem, m_recv_sem, r_send_sem, r_recv_sem, t_send_sem, t_recv_sem,
 ):
@@ -71,7 +72,7 @@
     late = []
 
     barrier = pltpu.get_barrier_semaphore()
-    for i in range(1, tiles):
+    for i in sorted(range(1, tiles), key=lambda i: -min(i, tiles - i)):
         pl.semaphore_signal(barrier, inc=1, device_id=(reg, lax.rem(til + i, tiles)), device_id_type=MESH)
     for i in range(1, regions):
         pl.semaphore_signal(barrier, inc=1, device_id=(lax.rem(reg + i, regions), til), device_id_type=MESH)
@@ -103,8 +104,10 @@
             copy(7, packed.at[at, pl.ds(8 - packs, packs)], right_in.at[at, pl.ds(2 - packs, packs)], (down, left)),
             copy(2, packed.at[at, pl.ds(0, 4)], left_in.at[at, pl.ds(2, 4)], (reg, right)),
             copy(3, packed.at[at, pl.ds(4, 4)], right_in.at[at, pl.ds(2, 4)], (reg, left)),
-            copy(0, dense.at[at, pl.ds(0, size)], rows_in.at[at, 1, pl.ds(0, size)], (up, til)),
-            copy(1, dense.at[at, pl.ds(512 - size, size)], rows_in.at[at, 0, pl.ds(256 - size, size)], (down, til)),
+            copy(0, coef_rows.at[pl.ds(0, 8)], coef_in.at[1], (up, til)) if e == 0 else
+            copy(0, dense.at[e, pl.ds(0, size)], rows_in.at[e, 1, pl.ds(0, size)], (up, til)),
+            copy(1, coef_rows.at[pl.ds(8, 8)], coef_in.at[0], (down, til)) if e == 0 else
+            copy(1, dense.at[e, pl.ds(512 - size, size)], rows_in.at[e, 0, pl.ds(256 - size, size)], (down, til)),
         ]
 
     def halo_pack(e):
@@ -170,18 +173,19 @@
 
     def build_frame(e, copies, out, deep=8):
         frame_own(e, out)
+        drain()
         for c in copies:
             c.wait_recv()
         frame_halo(e, out, deep)
 
-    def to_cells(source, e):
+    def to_cells(line, out, rows):
         def four_rows(j, _):
-            lines = [source[pl.ds(4 * j + b, 8, stride=16), :].astype(F32) for b in range(4)]
+            lines = [line(4 * j + b) for b in range(4)]
             many = jnp.concatenate([x for x in lines for _ in range(4)], axis=0).T
             for b, x in enumerate(swap_blocks([many[32 * g:32 * g + 32] for g in range(4)])):
-                dense[e, pl.ds(pl.multiple_of((4 * j + b) * 32, 32), 32), :] = x
+                out[pl.ds(pl.multiple_of((4 * j + b) * 32, 32), 32), :] = x
             return 0
-        lax.fori_loop(0, 4, four_rows, 0)
+        lax.fori_loop(0, rows // 4, four_rows, 0)
 
     def to_natural(field, out):
         def four_rows(j, _):
@@ -192,8 +196,14 @@
             return 0
         lax.fori_loop(0, 4, four_rows, 0)
 
-    for e, source in enumerate((mask_ref, kx_ref, ky_ref)):
-        to_cells(source, e)
+    def stage(r, _):
+        for e, source in enumerate((mask_ref, kx_ref, ky_ref)):
+            coef_rows[r, 8 * e:8 * e + 8, :] = source[pl.ds(r, 8, stride=16), :].astype(F32)
+        return 0
+
+    lax.fori_loop(0, 16, stage, 0)
+    for e in range(3):
+        to_cells(lambda r: coef_rows[r, 8 * e:8 * e + 8, :], dense.at[e], 16)
         halo_pack(e)
 
     owner = owner_ref[...]
@@ -242,12 +252,23 @@
                         device_id=(reg, to), device_id_type=MESH))
         return out
 
+    def both_ways(copies):
+        order = list(range(3))
+        for j in range(1, planes, 2):
+            order += [4 * i + k - 1 for k in range(4) for i in (j, j + 1) if i < planes]
+        return [copies[i] for i in order]
+
     m_copies = sends(msend, mrecv, m_send_sem, m_recv_sem)
     w_copies = sends(wsend, wrecv, w_send_sem, w_recv_sem)
     late.extend(m_copies + w_copies)
+    def drain():
+        for c in late:
+            c.wait_send()
+        late.clear()
+
     pl.semaphore_wait(barrier, (tiles - 1) + (regions - 1) + 4)
     copies = halo_start(0, 8, 3)
-    for c in m_copies + w_copies:
+    for c in both_ways(m_copies) + both_ways(w_copies):
         c.start()
     wrecv[0] = wsend[til]
     mrecv[0] = msend[til]
@@ -257,6 +278,8 @@
     for c in copies:
         c.wait_recv()
     for e in range(3):
+        for side in range(2):
+            to_cells(lambda r: coef_in[side, r, 8 * e:8 * e + 8, :], rows_in.at[e, side], 8)
         frame_halo(e, coef.at[e])
 
     def make_faces(k, _):
@@ -281,19 +304,24 @@
         for s in range(first, last + 1):
             src, dst = (frame_a, frame_b) if (s - first) % 2 == 0 else (frame_b, frame_a)
 
-            def line(k, carry):
+            def lines(i, carry):
                 before, here, west = carry
-                base = pl.multiple_of(k * WIDE, 8)
-                after = src[pl.ds(base + WIDE, WIDE), :]
-                east = coef[1, pl.ds(base, WIDE), :]
-                out = coef[0, pl.ds(base, WIDE), :] * here + east * after + west * before
-                out = out + coef[2, pl.ds(base, WIDE), :] * src[pl.ds(base + 1, WIDE), :]
-                out = out + coef[2, pl.ds(base - 1, WIDE), :] * src[pl.ds(base - 1, WIDE), :]
-                dst[pl.ds(base, WIDE), :] = out
-                return here, after, east
+                base = pl.multiple_of((s + ROWS_AT_ONCE * i) * WIDE, 8)
+                for u in range(ROWS_AT_ONCE):
+                    at = base + u * WIDE
+                    after = src[pl.ds(at + WIDE, WIDE), :]
+                    east = coef[1, pl.ds(at, WIDE), :]
+                    out = (coef[0, pl.ds(at, WIDE), :] * here + east * after) + west * before
+                    dst[pl.ds(at, WIDE), :] = out + (
+                        coef[2, pl.ds(at, WIDE), :] * src[pl.ds(at + 1, WIDE), :]
+                        + coef[2, pl.ds(at - 1, WIDE), :] * src[pl.ds(at - 1, WIDE), :])
+                    before, here, west = here, after, east
+                return before, here, west
 
             at = (s - 1) * WIDE
-            lax.fori_loop(s, TALL + 1 - s, line, (src[at:at + WIDE, :], src[at + WIDE:at + 2 * WIDE, :], coef[1, at:at + WIDE, :]))
+            rows = 16 if s == HALO else TALL + 1 - 2 * s
+            lax.fori_loop(
+                0, -(-rows // ROWS_AT_ONCE), lines, (src[at:at + WIDE, :], src[at + WIDE:at + 2 * WIDE, :], coef[1, at:at + WIDE, :]))
 
     def inner(out):
         for j in range(16):
@@ -304,7 +332,7 @@
     lane = iota((LANES, LANES), 1)
     seat = iota((LANES, LANES), 0) % CAP
     ones = jnp.ones((3 * LANES, LANES), BF16)
-    cells = pick.shape[2]
+    cells = pick_t.shape[0]
 
     def corner_of(place, c):
         row = (place >> 7) + c // 2
@@ -327,8 +355,11 @@
         for c in range(4):
             cell, group = corner_of(place_col, c)
             group_b[c, at, :] = jnp.where(group == lane // 32, 1.0, 0.0)
-            for t in range(cells // LANES):
-                pick[c, at, t * LANES:(t + 1) * LANES] = jnp.where(cell == lane + t * LANES, 1.0, 0.0).astype(BF16)
+            if c == 0:
+                for t in range(cells // LANES):
+                    hit = jnp.where(cell == lane + t * LANES, 1.0, 0.0).astype(BF16)
+                    pick[at, t * LANES:(t + 1) * LANES] = hit
+                    pick[at, cells + t * LANES:cells + (t + 1) * LANES] = hit
             cell, _ = corner_of(place_row, c)
             there = pl.ds(pl.multiple_of((4 * j + c) * LANES, LANES), LANES)
             pick_t[:, there] = jnp.where(iota((cells, LANES), 0) == cell, 1.0, 0.0).astype(BF16)
@@ -356,11 +387,13 @@
         at = pl.ds(pl.multiple_of(j * LANES, LANES), LANES)
         for c in range(4):
             expanded[c, at, :] = wide[:, c * LANES:(c + 1) * LANES] * group_b[c, at, :]
+            expanded_0[c, at, :] = wide[:, c * LANES:(c + 1) * LANES] * group_b[0, at, :]
             put_terms(j, c)
         there = pl.ds(pl.multiple_of(4 * j * LANES, LANES), 4 * LANES)
         part = dot(pick_t[:, there], terms[there, :])
         return part[:, :LANES] + part[:, LANES:]
 
+    state16[...] = jnp.zeros_like(state16)
     dense[3] = take_plane(0, 1)
 
     def later_plane(j, _):
@@ -379,18 +412,28 @@
         dense[e] = total[:, :LANES] + total[:, LANES:]
 
     def observe(field, n):
-        hi, lo = split(field[...], 2)
-        state16[:, :LANES] = hi
-        state16[:, LANES:] = lo
+        def corners(r, _):
+            at = pl.multiple_of(r * 32, 32)
+            here = field[pl.ds(at, 32), :]
+            past = jnp.broadcast_to(pltpu.roll(here[:8], 96, 1)[0:1], (32, LANES))
+            beside = jnp.where(iota((32, LANES), 0) == 31, past, field[pl.ds(at + 1, 32), :])
+            above = pl.multiple_of(jnp.maximum(at - 32, 0), 32)
+            for c, value in enumerate((here, beside)):
+                for h, part in enumerate(split(value, 2)):
+                    state16[pl.ds(h * cells + at, 32), c * LANES:(c + 1) * LANES] = part
+                    state16[pl.ds(h * cells + above, 32), (2 + c) * LANES:(3 + c) * LANES] = part
+            return 0
+
+        lax.fori_loop(0, 16, corners, 0)
         acc[...] = jnp.zeros_like(acc)
 
-        def one(c, _):
-            values = dot(pick[c], state16[...])
-            acc[...] += (values[:, :LANES] + values[:, LANES:]) * expanded[c]
+        def one(i, _):
+            values = dot(pick[...], state16[:, pl.ds(pl.multiple_of(i * 2 * LANES, LANES), 2 * LANES)])
+            acc[...] += values[:, :LANES] * expanded_0[2 * i] + values[:, LANES:] * expanded_0[2 * i + 1]
             return 0
 
-        lax.fori_loop(0, 4, one, 0)
-        q = dot(jnp.concatenate(split(acc[...], 2), axis=1), ones[:2 * LANES])
+        lax.fori_loop(0, 2, one, 0)
+        q = jnp.broadcast_to(jnp.sum(acc[...], axis=1, keepdims=True), acc.shape)
         q_b[n] = q
         z_b[...] = var_b[...] * q
 
@@ -447,7 +490,7 @@
     inner(fields.at[1])
 
     observe(fields.at[1], 0)
-    summing = sums_start(0, (product(fields[0], fields[0]), energy(0, 0)))
+    summing = sums_start(0, (product(fields[0, :512, :], fields[0, :512, :]), energy(0, 0)))
     adjoint(4)
     halo_pack(4)
     copies = halo_start(4)
@@ -461,12 +504,12 @@
     found = sums_finish(0, summing)
     norm_0, energy_0 = found[0:1], found[1:2]
     alpha_0 = norm_0 / (norm_0 + energy_0)
-    fields[4] = fields[1] - alpha_0 * (fields[1] + fields[4])
+    fields[4, :512, :] = fields[1, :512, :] - alpha_0 * (fields[1, :512, :] + fields[4, :512, :])
 
     observe(fields.at[4], 1)
-    fields[2] = fields[0] + fields[2]
-    fields[3] = fields[0] - alpha_0 * fields[2]
-    summing = sums_start(1, (product(fields[3], fields[3]), product(fields[3], fields[0]), energy(1, 1), energy(1, 0)))
+    fields[2, :512, :] = fields[0, :512, :] + fields[2, :512, :]
+    fields[3, :512, :] = fields[0, :512, :] - alpha_0 * fields[2, :512, :]
+    summing = sums_start(1, (product(fields[3, :512, :], fields[3, :512, :]), product(fields[3, :512, :], fields[0, :512, :]), energy(1, 1), energy(1, 0)))
     adjoint(5)
     halo_pack(5)
     copies = halo_start(5, 4)
@@ -477,6 +520,7 @@
     diffuse(5, 8)
     inner(fields.at[5])
     to_natural(fields.at[5], natural.at[3])
+    drain()
     found = sums_finish(1, summing)
     norm_1 = found[0:1]
     beta = norm_1 / norm_0
@@ -485,8 +529,13 @@
     control_ref[...] = (alpha_0 + alpha_1 * beta) * natural[0] + alpha_1 * natural[2]
     residual_ref[...] = natural[2] - alpha_1 * (natural[2] + natural[3] + beta * natural[1])
 
-    for c in late:
-        c.wait_send()
+
+def hand_over(control, residual, control_out, residual_out, sem):
+    copies = [pltpu.make_async_copy(control, control_out, sem.at[0]), pltpu.make_async_copy(residual, residual_out, sem.at[1])]
+    for c in copies:
+        c.start()
+    for c in copies:
+        c.wait()
 
 
 def body(regions, tiles, kx, ky, mask, obs_owner, obs_row, obs_col, obs_weight, innovation, inverse_var):
@@ -522,7 +571,10 @@
             pltpu.VMEM((tiles, 1, LANES), F32),
             pltpu.VMEM((tiles, 1, LANES), F32),
             pltpu.VMEM((4, slots, LANES), F32),
-            pltpu.VMEM((4, slots, cells), BF16),
+            pltpu.VMEM((4, slots, LANES), F32),
+            pltpu.VMEM((16, 24, LANES), F32),
+            pltpu.VMEM((2, HALO, 24, LANES), F32),
+            pltpu.VMEM((slots, 2 * cells), BF16),
             pltpu.VMEM((cells, 4 * slots), BF16),
             pltpu.VMEM((4 * slots, 2 * LANES), BF16),
             pltpu.VMEM((slots, LANES), F32),
@@ -530,8 +582,8 @@
             pltpu.VMEM((2, slots, LANES), F32),
             pltpu.VMEM((slots, LANES), F32),
             pltpu.VMEM((4, slots, LANES), F32),
-            pltpu.VMEM((cells, 2 * LANES), BF16),
-            pltpu.VMEM((6, cells, LANES), F32),
+            pltpu.VMEM((2 * cells, 4 * LANES), BF16),
+            pltpu.VMEM((6, cells + 8, LANES), F32),
             pltpu.VMEM((4, cells, LANES), F32),
             pltpu.VMEM((2, 4, LANES), F32),
             pltpu.VMEM((2, regions, 4, LANES), F32),
@@ -543,6 +595,14 @@
         ],
         compiler_params=pltpu.CompilerParams(collective_id=0, has_side_effects=True, vmem_limit_bytes=60 * 1024 * 1024),
     )(*args)
+    control, residual = pl.pallas_call(
+        hand_over,
+        out_shape=(out, out),
+        in_specs=[pl.BlockSpec(memory_space=pl.ANY)] * 2,
+        out_specs=[pl.BlockSpec(memory_space=pl.ANY)] * 2,
+        scratch_shapes=[dma((2,))],
+        compiler_params=pltpu.CompilerParams(vmem_limit_bytes=60 * 1024 * 1024),
+    )(control, residual)
     shape = (32 // levels, levels, rows_x, cols_y)
     return control.reshape(shape), residual.reshape(shape)
 

time: 76.8 us -> 92 us (1.20)
  Pallas kernels: 73.6 us -> 91.2 us
  local copies, waits for them, and re-layouts: 2.42 us -> 0 us
    pallas_call x0 -> x1, Pallas kernels: none -> 17 us  [body(): pl.pallas_call(hand_over, out_shape=(out, out), in_specs=[pl.BlockSpec(me...]
    unnamed x4 -> x0, local copies, waits for them, and re-layouts: 2.42 us -> none
where the time goes in v4:
time: 92 us; the launch traced here: 91.9 us
  Pallas kernels  91.2 us (99%)
    pallas_call x1, Pallas kernels, body(): pl.pallas_call(functools.partial(kernel, regions, tiles), out_shape=(out,...  74.2 us
    pallas_call x1, Pallas kernels, body(): pl.pallas_call(hand_over, out_shape=(out, out), in_specs=[pl.BlockSpec(me...  17 us

profile of v4, /device:TPU:1, one launch (start us, length us, event | category | flops | bytes accessed | tf_op | source)
XLA Modules:
  0.0 91.9 jit_solution(14261697749866961517)
XLA Ops:
  0.6 74.2 %shard_map.104 = (f32[512,128]{1,0:T(8,128)}, f32[512,128]{1,0:T(8,128)}) custom-call(f32[128,128]{1,0:T(8,128)} %bitcast.10, f32[128,128]{1,0:T(8,128)} %bitcast.11, s32[128,128]{1,0:T(8,128)} %bitcast.12, s32[1,512]{1,0:T(1,128)} %bitcast.13, s32[1,512]{1,0:T(1,128)} %bitcast.14, s32[1,512]{1,0:T(1,128)} %bitcast.15, f32[1,512]{1,0:T(1,128)} %bitcast.16, ...), custom_call_target="tpu_custom_call" | custom-call | tf_op jit(solution)/shard_map/pallas_call | solution.py:553
  74.9 17.0 %shard_map.105 = (f32[512,128]{1,0:T(8,128)}, f32[512,128]{1,0:T(8,128)}) custom-call(f32[512,128]{1,0:T(8,128)} %get-tuple-element.6.control, f32[512,128]{1,0:T(8,128)} %get-tuple-element.7.residual), custom_call_target="tpu_custom_call" | custom-call | tf_op jit(solution)/shard_map/pallas_call | solution.py:598

commit v5 on v4

--- a/solution.py
+++ b/solution.py
@@ -61,7 +61,7 @@
     kx_ref, ky_ref, mask_ref, owner_ref, row_ref, col_ref, innov_ref, var_ref, weight_ref,
     dense, rows_in, left_in, right_in, packed, frame_a, frame_b, coef, wsplit, wsend, wrecv, msend, mrecv, expanded, expanded_0, coef_rows, coef_in,
     pick, pick_t, terms, var_b, z_b, q_b, acc, group_b, state16, fields, natural, sums_send, sums_region, sums_mid, sums_tile,
-    in_sem, halo_send, halo_recv, w_send_sem, w_recv_sem, m_send_sem, m_recv_sem, r_send_sem, r_recv_sem, t_send_sem, t_recv_sem,
+    in_sem, halo_send, halo_recv, w_send_sem, w_recv_sem, m_sem, r_sem, t_sem,
 ):
     reg, til = lax.axis_index("region"), lax.axis_index("tile")
     up, down = lax.rem(reg + regions - 1, regions), lax.rem(reg + 1, regions)
@@ -71,6 +71,9 @@
     planes = tiles // 4
     late = []
 
+    def wait_all(ref, sem):
+        pltpu.make_async_copy(ref, ref, sem).wait()
+
     barrier = pltpu.get_barrier_semaphore()
     for i in sorted(range(1, tiles), key=lambda i: -min(i, tiles - i)):
         pl.semaphore_signal(barrier, inc=1, device_id=(reg, lax.rem(til + i, tiles)), device_id_type=MESH)
@@ -81,33 +84,33 @@
             pl.semaphore_signal(barrier, inc=1, device_id=(a, b), device_id_type=MESH)
 
     pairs = (
-        (mask_any, mask_ref), (kx_any, kx_ref), (ky_any, ky_ref), (owner_any, owner_ref), (row_any, row_ref), (col_any, col_ref),
-        (innov_any, innov_ref), (var_any, var_ref), (weight_any, weight_ref),
+        (owner_any, owner_ref), (row_any, row_ref), (col_any, col_ref), (innov_any, innov_ref), (var_any, var_ref),
+        (weight_any, weight_ref), (mask_any, mask_ref), (kx_any, kx_ref), (ky_any, ky_ref),
     )
     loads = [pltpu.make_async_copy(a, b, in_sem.at[i]) for i, (a, b) in enumerate(pairs)]
     for c in loads:
         c.start()
-    for c in loads:
+    for c in loads[:6]:
         c.wait()
     lane8 = iota((8, LANES), 1)
 
     def halo_copies(e, deep, fields):
-        def copy(n, src, dst, device):
+        def copy(src, dst, device):
             return pltpu.make_async_remote_copy(
-                src_ref=src, dst_ref=dst, send_sem=halo_send.at[e, n], recv_sem=halo_recv.at[e, n],
+                src_ref=src, dst_ref=dst, send_sem=halo_send.at[e], recv_sem=halo_recv.at[e],
                 device_id=device, device_id_type=MESH)
         size, packs, at = deep * 32, deep // 4, pl.ds(e, fields)
         return [
-            copy(4, packed.at[at, pl.ds(0, packs)], left_in.at[at, pl.ds(6, packs)], (up, right)),
-            copy(5, packed.at[at, pl.ds(4 - packs, packs)], left_in.at[at, pl.ds(2 - packs, packs)], (down, right)),
-            copy(6, packed.at[at, pl.ds(4, packs)], right_in.at[at, pl.ds(6, packs)], (up, left)),
-            copy(7, packed.at[at, pl.ds(8 - packs, packs)], right_in.at[at, pl.ds(2 - packs, packs)], (down, left)),
-            copy(2, packed.at[at, pl.ds(0, 4)], left_in.at[at, pl.ds(2, 4)], (reg, right)),
-            copy(3, packed.at[at, pl.ds(4, 4)], right_in.at[at, pl.ds(2, 4)], (reg, left)),
-            copy(0, coef_rows.at[pl.ds(0, 8)], coef_in.at[1], (up, til)) if e == 0 else
-            copy(0, dense.at[e, pl.ds(0, size)], rows_in.at[e, 1, pl.ds(0, size)], (up, til)),
-            copy(1, coef_rows.at[pl.ds(8, 8)], coef_in.at[0], (down, til)) if e == 0 else
-            copy(1, dense.at[e, pl.ds(512 - size, size)], rows_in.at[e, 0, pl.ds(256 - size, size)], (down, til)),
+            copy(packed.at[at, pl.ds(0, packs)], left_in.at[at, pl.ds(6, packs)], (up, right)),
+            copy(packed.at[at, pl.ds(4 - packs, packs)], left_in.at[at, pl.ds(2 - packs, packs)], (down, right)),
+            copy(packed.at[at, pl.ds(4, packs)], right_in.at[at, pl.ds(6, packs)], (up, left)),
+            copy(packed.at[at, pl.ds(8 - packs, packs)], right_in.at[at, pl.ds(2 - packs, packs)], (down, left)),
+            copy(packed.at[at, pl.ds(0, 4)], left_in.at[at, pl.ds(2, 4)], (reg, right)),
+            copy(packed.at[at, pl.ds(4, 4)], right_in.at[at, pl.ds(2, 4)], (reg, left)),
+            copy(coef_rows.at[pl.ds(0, 8)], coef_in.at[1], (up, til)) if e == 0 else
+            copy(dense.at[e, pl.ds(0, size)], rows_in.at[e, 1, pl.ds(0, size)], (up, til)),
+            copy(coef_rows.at[pl.ds(8, 8)], coef_in.at[0], (down, til)) if e == 0 else
+            copy(dense.at[e, pl.ds(512 - size, size)], rows_in.at[e, 0, pl.ds(256 - size, size)], (down, til)),
         ]
 
     def halo_pack(e):
@@ -118,11 +121,11 @@
             packed[e, 4 + j] = first[0]
 
     def halo_start(e, deep=8, fields=1):
-        copies = halo_copies(e, deep, fields)
-        late.extend(copies)
-        for c in copies:
+        for c in halo_copies(e, deep, fields):
             c.start()
-        return copies
+        amount = frame_b.at[pl.ds(0, 768 if e == 0 else 72 * deep + 64)]
+        late.append(lambda: wait_all(amount, halo_send.at[e]))
+        return lambda: wait_all(amount, halo_recv.at[e])
 
     def frame_own(e, out):
         def four_rows(j, _):
@@ -171,11 +174,10 @@
                 return 0
             lax.fori_loop(0 if side else 2 - deep // 4, deep // 4 if side else 2, outer_rows, 0)
 
-    def build_frame(e, copies, out, deep=8):
+    def build_frame(e, arrive, out, deep=8):
         frame_own(e, out)
         drain()
-        for c in copies:
-            c.wait_recv()
+        arrive()
         frame_halo(e, out, deep)
 
     def to_cells(line, out, rows):
@@ -195,16 +197,6 @@
                 out[pl.ds(4 * j + b, 32, stride=16), :] = many[32 * b:32 * b + 32]
             return 0
         lax.fori_loop(0, 4, four_rows, 0)
-
-    def stage(r, _):
-        for e, source in enumerate((mask_ref, kx_ref, ky_ref)):
-            coef_rows[r, 8 * e:8 * e + 8, :] = source[pl.ds(r, 8, stride=16), :].astype(F32)
-        return 0
-
-    lax.fori_loop(0, 16, stage, 0)
-    for e in range(3):
-        to_cells(lambda r: coef_rows[r, 8 * e:8 * e + 8, :], dense.at[e], 16)
-        halo_pack(e)
 
     owner = owner_ref[...]
     marks = jnp.where(iota((tiles, count), 0) == owner, 1.0, 0.0)
@@ -240,7 +232,7 @@
     turns = sorted(range(planes), key=lambda i: (min(i, planes - i), i))
     plane, place_in = til // 4, lax.rem(til, 4)
 
-    def sends(src, dst, send_sem, recv_sem):
+    def sends(src, dst, send_sem, recv_sem, together):
         out = []
         for j, turn in enumerate(turns):
             for k in range(4):
@@ -248,7 +240,7 @@
                     to = lax.rem(plane + turn, planes) * 4 + lax.rem(place_in + k, 4)
                     n = 4 * j + k
                     out.append(pltpu.make_async_remote_copy(
-                        src_ref=src.at[to], dst_ref=dst.at[n], send_sem=send_sem.at[n], recv_sem=recv_sem.at[n],
+                        src_ref=src.at[to], dst_ref=dst.at[n], send_sem=send_sem, recv_sem=recv_sem.at[n // together],
                         device_id=(reg, to), device_id_type=MESH))
         return out
 
@@ -258,47 +250,34 @@
             order += [4 * i + k - 1 for k in range(4) for i in (j, j + 1) if i < planes]
         return [copies[i] for i in order]
 
-    m_copies = sends(msend, mrecv, m_send_sem, m_recv_sem)
-    w_copies = sends(wsend, wrecv, w_send_sem, w_recv_sem)
-    late.extend(m_copies + w_copies)
+    m_copies = sends(msend, mrecv, m_sem.at[0], m_sem.at[pl.ds(1, 1)], tiles)
+    w_copies = sends(wsend, wrecv, w_send_sem.at[0], w_recv_sem, 4)
+    late.append(lambda: wait_all(msend.at[pl.ds(1, tiles - 1)], m_sem.at[0]))
+    late.append(lambda: wait_all(wsend.at[pl.ds(1, tiles - 1)], w_send_sem.at[0]))
     def drain():
-        for c in late:
-            c.wait_send()
+        for wait in late:
+            wait()
         late.clear()
 
     pl.semaphore_wait(barrier, (tiles - 1) + (regions - 1) + 4)
-    copies = halo_start(0, 8, 3)
     for c in both_ways(m_copies) + both_ways(w_copies):
         c.start()
     wrecv[0] = wsend[til]
     mrecv[0] = msend[til]
 
+    for c in loads[6:]:
+        c.wait()
+
+    def stage(r, _):
+        for e, source in enumerate((mask_ref, kx_ref, ky_ref)):
+            coef_rows[r, 8 * e:8 * e + 8, :] = source[pl.ds(r, 8, stride=16), :].astype(F32)
+        return 0
+
+    lax.fori_loop(0, 16, stage, 0)
     for e in range(3):
-        frame_own(e, coef.at[e])
-    for c in copies:
-        c.wait_recv()
-    for e in range(3):
-        for side in range(2):
-            to_cells(lambda r: coef_in[side, r, 8 * e:8 * e + 8, :], rows_in.at[e, side], 8)
-        frame_halo(e, coef.at[e])
-
-    def make_faces(k, _):
-        base = pl.multiple_of(k * WIDE, 8)
-        wet = coef[0, pl.ds(base, WIDE), :]
-        coef[1, pl.ds(base, WIDE), :] = coef[1, pl.ds(base, WIDE), :] * wet * coef[0, pl.ds(base + WIDE, WIDE), :]
-        coef[2, pl.ds(base, WIDE), :] = coef[2, pl.ds(base, WIDE), :] * wet * coef[0, pl.ds(base + 1, WIDE), :]
-        return 0
-
-    lax.fori_loop(0, TALL, make_faces, 0)
-
-    def make_centre(k, _):
-        base = pl.multiple_of(k * WIDE, 8)
-        faces = coef[1, pl.ds(base, WIDE), :] + coef[1, pl.ds(base - WIDE, WIDE), :]
-        faces = faces + coef[2, pl.ds(base, WIDE), :] + coef[2, pl.ds(base - 1, WIDE), :]
-        coef[0, pl.ds(base, WIDE), :] = coef[0, pl.ds(base, WIDE), :] - faces
-        return 0
-
-    lax.fori_loop(1, TALL, make_centre, 0)
+        to_cells(lambda r: coef_rows[r, 8 * e:8 * e + 8, :], dense.at[e], 16)
+        halo_pack(e)
+    coef_arrive = halo_start(0, 8, 3)
 
     def diffuse(first, last):
         for s in range(first, last + 1):
@@ -327,8 +306,7 @@
         for j in range(16):
             out[j * 32:(j + 1) * 32, :] = frame_a[(8 + j) * WIDE + 16:(9 + j) * WIDE, :]
 
-    for c in m_copies:
-        c.wait_recv()
+    wait_all(mrecv.at[pl.ds(1, tiles - 1)], m_sem.at[1])
     lane = iota((LANES, LANES), 1)
     seat = iota((LANES, LANES), 0) % CAP
     ones = jnp.ones((3 * LANES, LANES), BF16)
@@ -378,11 +356,7 @@
         iota((3 * LANES, 4 * LANES), 0) % LANES == iota((3 * LANES, 4 * LANES), 1) // LANES * 32 + iota((3 * LANES, 4 * LANES), 1) % 32,
         1.0, 0.0).astype(BF16)
     def take_plane(j, first):
-        for k in range(first, 4):
-            n = 4 * j + k
-            pltpu.make_async_remote_copy(
-                src_ref=wsend.at[n], dst_ref=wrecv.at[n], send_sem=w_send_sem.at[n], recv_sem=w_recv_sem.at[n],
-                device_id=(reg, left), device_id_type=MESH).wait_recv()
+        wait_all(wrecv.at[pl.ds(4 * j + first, 4 - first)], w_recv_sem.at[j])
         wide = dot(jnp.concatenate(split(wrecv[pl.ds(4 * j, 4)].reshape(LANES, LANES), 3), axis=1), copy_lanes)
         at = pl.ds(pl.multiple_of(j * LANES, LANES), LANES)
         for c in range(4):
@@ -439,38 +413,32 @@
 
     def r_copies(n):
         return [pltpu.make_async_remote_copy(
-            src_ref=sums_send.at[n], dst_ref=sums_region.at[n, i], send_sem=r_send_sem.at[n, i], recv_sem=r_recv_sem.at[n, i],
+            src_ref=sums_send.at[n], dst_ref=sums_region.at[n, i], send_sem=r_sem.at[n, 0], recv_sem=r_sem.at[n, 1],
             device_id=(lax.rem(reg + i, regions), til), device_id_type=MESH) for i in range(1, regions)]
 
     def t_copies(n):
         return [pltpu.make_async_remote_copy(
-            src_ref=sums_mid.at[n], dst_ref=sums_tile.at[n, i], send_sem=t_send_sem.at[n, i], recv_sem=t_recv_sem.at[n, i],
+            src_ref=sums_mid.at[n], dst_ref=sums_tile.at[n, i], send_sem=t_sem.at[n, 0], recv_sem=t_sem.at[n, 1],
             device_id=(reg, lax.rem(til + i, tiles)), device_id_type=MESH) for i in range(1, tiles)]
 
     def sums_start(n, sums):
         for i in range(4):
             sums_send[n, i:i + 1, :] = sums[i] if i < len(sums) else jnp.zeros((1, LANES), F32)
-        copies = r_copies(n)
-        late.extend(copies)
-        for c in copies:
+        for c in r_copies(n):
             c.start()
+        late.append(lambda: wait_all(sums_region.at[n, pl.ds(1, regions - 1)], r_sem.at[n, 0]))
         sums_region[n, 0] = sums_send[n]
-        return copies
-
-    def sums_middle(n, copies):
-        for c in copies:
-            c.wait_recv()
+
+    def sums_middle(n):
+        wait_all(sums_region.at[n, pl.ds(1, regions - 1)], r_sem.at[n, 1])
         sums_mid[n] = jnp.sum(sums_region[n], axis=0)
-        copies = t_copies(n)
-        late.extend(copies)
-        for c in copies:
+        for c in t_copies(n):
             c.start()
+        late.append(lambda: wait_all(sums_tile.at[n, pl.ds(1, tiles - 1)], t_sem.at[n, 0]))
         sums_tile[n, 0] = sums_mid[n]
-        return copies
-
-    def sums_finish(n, copies):
-        for c in copies:
-            c.wait_recv()
+
+    def sums_finish(n):
+        wait_all(sums_tile.at[n, pl.ds(1, tiles - 1)], t_sem.at[n, 1])
         return jnp.sum(jnp.sum(sums_tile[n], axis=0), axis=1, keepdims=True)
 
     def product(a, b):
@@ -482,26 +450,53 @@
         return jnp.where(lane1 == 0, product(var_b[...] * q_b[a], q_b[b]), 0.0)
 
     halo_pack(3)
-    copies = halo_start(3)
-    build_frame(3, copies, frame_a)
+    arrive = halo_start(3)
+
+    for e in range(3):
+        frame_own(e, coef.at[e])
+    coef_arrive()
+    for e in range(3):
+        for side in range(2):
+            to_cells(lambda r: coef_in[side, r, 8 * e:8 * e + 8, :], rows_in.at[e, side], 8)
+        frame_halo(e, coef.at[e])
+
+    def make_faces(k, _):
+        base = pl.multiple_of(k * WIDE, 8)
+        wet = coef[0, pl.ds(base, WIDE), :]
+        coef[1, pl.ds(base, WIDE), :] = coef[1, pl.ds(base, WIDE), :] * wet * coef[0, pl.ds(base + WIDE, WIDE), :]
+        coef[2, pl.ds(base, WIDE), :] = coef[2, pl.ds(base, WIDE), :] * wet * coef[0, pl.ds(base + 1, WIDE), :]
+        return 0
+
+    lax.fori_loop(0, TALL, make_faces, 0)
+
+    def make_centre(k, _):
+        base = pl.multiple_of(k * WIDE, 8)
+        faces = coef[1, pl.ds(base, WIDE), :] + coef[1, pl.ds(base - WIDE, WIDE), :]
+        faces = faces + coef[2, pl.ds(base, WIDE), :] + coef[2, pl.ds(base - 1, WIDE), :]
+        coef[0, pl.ds(base, WIDE), :] = coef[0, pl.ds(base, WIDE), :] - faces
+        return 0
+
+    lax.fori_loop(1, TALL, make_centre, 0)
+
+    build_frame(3, arrive, frame_a)
     diffuse(1, 4)
     inner(fields.at[0])
     diffuse(5, 8)
     inner(fields.at[1])
 
     observe(fields.at[1], 0)
-    summing = sums_start(0, (product(fields[0, :512, :], fields[0, :512, :]), energy(0, 0)))
+    sums_start(0, (product(fields[0, :512, :], fields[0, :512, :]), energy(0, 0)))
     adjoint(4)
     halo_pack(4)
-    copies = halo_start(4)
-    summing = sums_middle(0, summing)
+    arrive = halo_start(4)
+    sums_middle(0)
     to_natural(fields.at[0], natural.at[0])
-    build_frame(4, copies, frame_a)
+    build_frame(4, arrive, frame_a)
     diffuse(1, 4)
     inner(fields.at[2])
     diffuse(5, 8)
     inner(fields.at[4])
-    found = sums_finish(0, summing)
+    found = sums_finish(0)
     norm_0, energy_0 = found[0:1], found[1:2]
     alpha_0 = norm_0 / (norm_0 + energy_0)
     fields[4, :512, :] = fields[1, :512, :] - alpha_0 * (fields[1, :512, :] + fields[4, :512, :])
@@ -509,19 +504,19 @@
     observe(fields.at[4], 1)
     fields[2, :512, :] = fields[0, :512, :] + fields[2, :512, :]
     fields[3, :512, :] = fields[0, :512, :] - alpha_0 * fields[2, :512, :]
-    summing = sums_start(1, (product(fields[3, :512, :], fields[3, :512, :]), product(fields[3, :512, :], fields[0, :512, :]), energy(1, 1), energy(1, 0)))
+    sums_start(1, (product(fields[3, :512, :], fields[3, :512, :]), product(fields[3, :512, :], fields[0, :512, :]), energy(1, 1), energy(1, 0)))
     adjoint(5)
     halo_pack(5)
-    copies = halo_start(5, 4)
-    summing = sums_middle(1, summing)
+    arrive = halo_start(5, 4)
+    sums_middle(1)
     to_natural(fields.at[2], natural.at[1])
     to_natural(fields.at[3], natural.at[2])
-    build_frame(5, copies, frame_a, 4)
+    build_frame(5, arrive, frame_a, 4)
     diffuse(5, 8)
     inner(fields.at[5])
     to_natural(fields.at[5], natural.at[3])
     drain()
-    found = sums_finish(1, summing)
+    found = sums_finish(1)
     norm_1 = found[0:1]
     beta = norm_1 / norm_0
     curve = norm_1 + 2.0 * beta * found[1:2] + beta * beta * norm_0 + found[2:3] + 2.0 * beta * found[3:4] + beta * beta * energy_0
@@ -530,12 +525,9 @@
     residual_ref[...] = natural[2] - alpha_1 * (natural[2] + natural[3] + beta * natural[1])
 
 
-def hand_over(control, residual, control_out, residual_out, sem):
-    copies = [pltpu.make_async_copy(control, control_out, sem.at[0]), pltpu.make_async_copy(residual, residual_out, sem.at[1])]
-    for c in copies:
-        c.start()
-    for c in copies:
-        c.wait()
+def hand_over(control, residual, control_out, residual_out):
+    control_out[...] = control[...]
+    residual_out[...] = residual[...]
 
 
 def body(regions, tiles, kx, ky, mask, obs_owner, obs_row, obs_col, obs_weight, innovation, inverse_var):
@@ -589,18 +581,15 @@
             pltpu.VMEM((2, regions, 4, LANES), F32),
             pltpu.VMEM((2, 4, LANES), F32),
             pltpu.VMEM((2, tiles, 4, LANES), F32),
-            dma((9,)), dma((EXCHANGES, 8)), dma((EXCHANGES, 8)),
-            dma((tiles,)), dma((tiles,)), dma((tiles,)), dma((tiles,)),
-            dma((2, regions)), dma((2, regions)), dma((2, tiles)), dma((2, tiles)),
+            dma((9,)), dma((EXCHANGES,)), dma((EXCHANGES,)), dma((1,)), dma((tiles // 4,)), dma((2,)), dma((2, 2)), dma((2, 2)),
         ],
         compiler_params=pltpu.CompilerParams(collective_id=0, has_side_effects=True, vmem_limit_bytes=60 * 1024 * 1024),
     )(*args)
     control, residual = pl.pallas_call(
         hand_over,
         out_shape=(out, out),
-        in_specs=[pl.BlockSpec(memory_space=pl.ANY)] * 2,
-        out_specs=[pl.BlockSpec(memory_space=pl.ANY)] * 2,
-        scratch_shapes=[dma((2,))],
+        in_specs=[pl.BlockSpec(memory_space=pltpu.VMEM)] * 2,
+        out_specs=[pl.BlockSpec(memory_space=pltpu.VMEM)] * 2,
         compiler_params=pltpu.CompilerParams(vmem_limit_bytes=60 * 1024 * 1024),
     )(control, residual)
     shape = (32 // levels, levels, rows_x, cols_y)

time: 92 us -> 68 us (0.74)
  Pallas kernels: 91.2 us -> 67.3 us
    pallas_call x1, Pallas kernels: 17 us -> 1.84 us  [body(): pl.pallas_call(hand_over, out_shape=(out, out), in_specs=[pl.BlockSpec(me...]
    pallas_call x1, Pallas kernels: 74.2 us -> 65.4 us  [body(): pl.pallas_call(functools.partial(kernel, regions, tiles), out_shape=(out,...]
where the time goes in v5:
time: 68 us; the launch traced here: 67.9 us
  Pallas kernels  67.3 us (99%)
    pallas_call x1, Pallas kernels, body(): pl.pallas_call(functools.partial(kernel, regions, tiles), out_shape=(out,...  65.4 us
    pallas_call x1, Pallas kernels, body(): pl.pallas_call(hand_over, out_shape=(out, out), in_specs=[pl.BlockSpec(me...  1.84 us

profile of v5, /device:TPU:1, one launch (start us, length us, event | category | flops | bytes accessed | tf_op | source)
XLA Modules:
  0.0 67.9 jit_solution(9150141788636777839)
XLA Ops:
  0.6 65.4 %shard_map.104 = (f32[512,128]{1,0:T(8,128)}, f32[512,128]{1,0:T(8,128)}) custom-call(f32[128,128]{1,0:T(8,128)} %bitcast.10, f32[128,128]{1,0:T(8,128)} %bitcast.11, s32[128,128]{1,0:T(8,128)} %bitcast.12, s32[1,512]{1,0:T(1,128)} %bitcast.13, s32[1,512]{1,0:T(1,128)} %bitcast.14, s32[1,512]{1,0:T(1,128)} %bitcast.15, f32[1,512]{1,0:T(1,128)} %bitcast.16, ...), custom_call_target="tpu_custom_call" | custom-call | tf_op jit(solution)/shard_map/pallas_call | solution.py:545
  66.1 1.8 %shard_map.105 = (f32[512,128]{1,0:T(8,128)}, f32[512,128]{1,0:T(8,128)}) custom-call(f32[512,128]{1,0:T(8,128)} %get-tuple-element.6.control, f32[512,128]{1,0:T(8,128)} %get-tuple-element.7.residual), custom_call_target="tpu_custom_call" | custom-call | tf_op jit(solution)/shard_map/pallas_call | solution.py:588

commit v6 on v5

--- a/solution.py
+++ b/solution.py
@@ -90,7 +90,7 @@
     loads = [pltpu.make_async_copy(a, b, in_sem.at[i]) for i, (a, b) in enumerate(pairs)]
     for c in loads:
         c.start()
-    for c in loads[:6]:
+    for c in loads[:5]:
         c.wait()
     lane8 = iota((8, LANES), 1)
 
@@ -174,9 +174,10 @@
                 return 0
             lax.fori_loop(0 if side else 2 - deep // 4, deep // 4 if side else 2, outer_rows, 0)
 
-    def build_frame(e, arrive, out, deep=8):
+    def build_frame(e, arrive, out, deep=8, meanwhile=lambda: None):
         frame_own(e, out)
         drain()
+        meanwhile()
         arrive()
         frame_halo(e, out, deep)
 
@@ -203,8 +204,6 @@
     upper = jnp.where(iota((count, count), 0) < iota((count, count), 1), 1.0, 0.0).astype(BF16)
     before = dot(marks.astype(BF16), upper)
     slot = owner * CAP + jnp.sum(before * marks, axis=0, keepdims=True).astype(jnp.int32)
-    for i, part in enumerate(split(weight_ref[...], 3)):
-        wsplit[:, i * LANES:(i + 1) * LANES] = part
     meta_rows = [row_ref[...].astype(F32), col_ref[...].astype(F32)]
     meta_rows += [p.astype(F32) for p in split(innov_ref[...], 3) + split(var_ref[...], 3)]
     meta = jnp.zeros((8, count), F32)
@@ -212,22 +211,28 @@
         meta = jnp.where(iota((8, count), 0) == i, line, meta)
     meta = meta.astype(BF16)
 
-    def sort_plane(b, _):
+    def choose(b, _):
         chosen = jnp.where(iota((LANES, count), 0) + b * LANES == slot, 1.0, 0.0).astype(BF16)
-        block = dot(chosen, wsplit[...])
-        block = block[:, :LANES] + block[:, LANES:2 * LANES] + block[:, 2 * LANES:]
-        wsend[pl.ds(4 * b, 4)] = block.reshape(4, CAP, LANES)
-        facts = dot_nt(meta, chosen)
-        place = jnp.broadcast_to(facts[0:1] * LANES + facts[1:2], (8, LANES))
-        innov = jnp.broadcast_to(facts[2:3] + facts[3:4] + facts[4:5], (8, LANES))
-        var = jnp.broadcast_to(facts[5:6] + facts[6:7] + facts[7:8], (8, LANES))
+        pick[pl.ds(pl.multiple_of(b * LANES, LANES), LANES), :count] = chosen
+        return 0
+
+    lax.fori_loop(0, planes, choose, 0)
+    facts = dot_nt(meta, pick[:, :count])
+    place = facts[0:1] * LANES + facts[1:2]
+    innov = facts[2:3] + facts[3:4] + facts[4:5]
+    var = facts[5:6] + facts[6:7] + facts[7:8]
+    for b in range(planes):
+        at = slice(b * LANES, (b + 1) * LANES)
+        three = [jnp.broadcast_to(x[:, at], (8, LANES)) for x in (place, innov, var)]
         for k in range(4):
-            turned = [pltpu.roll(x, (i - k) * 32 % LANES, 1) for i, x in enumerate((place, innov, var))]
+            turned = [pltpu.roll(x, (i - k) * 32 % LANES, 1) for i, x in enumerate(three)]
             line = jnp.where(lane8 < 32, turned[0], jnp.where(lane8 < 64, turned[1], jnp.where(lane8 < 96, turned[2], 0.0)))
             msend[4 * b + k] = line[0:1]
-        return 0
-
-    lax.fori_loop(0, planes, sort_plane, 0)
+    loads[5].wait()
+    for i, part in enumerate(split(weight_ref[...], 3)):
+        wsplit[:, i * LANES:(i + 1) * LANES] = part
+    block = dot(pick[:, :count], wsplit[...])
+    wsend[...] = (block[:, :LANES] + block[:, LANES:2 * LANES] + block[:, 2 * LANES:]).reshape(tiles, CAP, LANES)
 
     turns = sorted(range(planes), key=lambda i: (min(i, planes - i), i))
     plane, place_in = til // 4, lax.rem(til, 4)
@@ -352,6 +357,9 @@
         terms[there, :LANES] = hi
         terms[there, LANES:] = lo
 
+    for e in range(3):
+        frame_own(e, coef.at[e])
+
     copy_lanes = jnp.where(
         iota((3 * LANES, 4 * LANES), 0) % LANES == iota((3 * LANES, 4 * LANES), 1) // LANES * 32 + iota((3 * LANES, 4 * LANES), 1) % 32,
         1.0, 0.0).astype(BF16)
@@ -409,37 +417,30 @@
         lax.fori_loop(0, 2, one, 0)
         q = jnp.broadcast_to(jnp.sum(acc[...], axis=1, keepdims=True), acc.shape)
         q_b[n] = q
-        z_b[...] = var_b[...] * q
-
-    def r_copies(n):
-        return [pltpu.make_async_remote_copy(
-            src_ref=sums_send.at[n], dst_ref=sums_region.at[n, i], send_sem=r_sem.at[n, 0], recv_sem=r_sem.at[n, 1],
-            device_id=(lax.rem(reg + i, regions), til), device_id_type=MESH) for i in range(1, regions)]
-
-    def t_copies(n):
-        return [pltpu.make_async_remote_copy(
-            src_ref=sums_mid.at[n], dst_ref=sums_tile.at[n, i], send_sem=t_sem.at[n, 0], recv_sem=t_sem.at[n, 1],
-            device_id=(reg, lax.rem(til + i, tiles)), device_id_type=MESH) for i in range(1, tiles)]
 
     def sums_start(n, sums):
         for i in range(4):
             sums_send[n, i:i + 1, :] = sums[i] if i < len(sums) else jnp.zeros((1, LANES), F32)
-        for c in r_copies(n):
-            c.start()
+        for i in sorted(range(1, tiles), key=lambda i: -min(i, tiles - i)):
+            pltpu.make_async_remote_copy(
+                src_ref=sums_send.at[n], dst_ref=sums_tile.at[n, i], send_sem=t_sem.at[n, 0], recv_sem=t_sem.at[n, 1],
+                device_id=(reg, lax.rem(til + i, tiles)), device_id_type=MESH).start()
+        late.append(lambda: wait_all(sums_tile.at[n, pl.ds(1, tiles - 1)], t_sem.at[n, 0]))
+        sums_tile[n, 0] = sums_send[n]
+
+    def sums_middle(n):
+        wait_all(sums_tile.at[n, pl.ds(1, tiles - 1)], t_sem.at[n, 1])
+        sums_mid[n] = jnp.sum(sums_tile[n], axis=0)
+        for i in sorted(range(1, regions), key=lambda i: -min(i, regions - i)):
+            pltpu.make_async_remote_copy(
+                src_ref=sums_mid.at[n], dst_ref=sums_region.at[n, i], send_sem=r_sem.at[n, 0], recv_sem=r_sem.at[n, 1],
+                device_id=(lax.rem(reg + i, regions), til), device_id_type=MESH).start()
         late.append(lambda: wait_all(sums_region.at[n, pl.ds(1, regions - 1)], r_sem.at[n, 0]))
-        sums_region[n, 0] = sums_send[n]
-
-    def sums_middle(n):
+        sums_region[n, 0] = sums_mid[n]
+
+    def sums_finish(n):
         wait_all(sums_region.at[n, pl.ds(1, regions - 1)], r_sem.at[n, 1])
-        sums_mid[n] = jnp.sum(sums_region[n], axis=0)
-        for c in t_copies(n):
-            c.start()
-        late.append(lambda: wait_all(sums_tile.at[n, pl.ds(1, tiles - 1)], t_sem.at[n, 0]))
-        sums_tile[n, 0] = sums_mid[n]
-
-    def sums_finish(n):
-        wait_all(sums_tile.at[n, pl.ds(1, tiles - 1)], t_sem.at[n, 1])
-        return jnp.sum(jnp.sum(sums_tile[n], axis=0), axis=1, keepdims=True)
+        return jnp.sum(jnp.sum(sums_region[n], axis=0), axis=1, keepdims=True)
 
     def product(a, b):
         return jnp.sum(a * b, axis=0, keepdims=True)
@@ -452,8 +453,6 @@
     halo_pack(3)
     arrive = halo_start(3)
 
-    for e in range(3):
-        frame_own(e, coef.at[e])
     coef_arrive()
     for e in range(3):
         for side in range(2):
@@ -484,34 +483,35 @@
     diffuse(5, 8)
     inner(fields.at[1])
 
+    norm = product(fields[0, :512, :], fields[0, :512, :])
     observe(fields.at[1], 0)
-    sums_start(0, (product(fields[0, :512, :], fields[0, :512, :]), energy(0, 0)))
+    sums_start(0, (norm, energy(0, 0)))
+    z_b[...] = var_b[...] * q_b[0]
     adjoint(4)
     halo_pack(4)
     arrive = halo_start(4)
-    sums_middle(0)
     to_natural(fields.at[0], natural.at[0])
-    build_frame(4, arrive, frame_a)
+    build_frame(4, arrive, frame_a, 8, lambda: sums_middle(0))
     diffuse(1, 4)
     inner(fields.at[2])
     diffuse(5, 8)
     inner(fields.at[4])
+    observe(fields.at[4], 1)
+    fields[2, :512, :] = fields[0, :512, :] + fields[2, :512, :]
     found = sums_finish(0)
     norm_0, energy_0 = found[0:1], found[1:2]
     alpha_0 = norm_0 / (norm_0 + energy_0)
-    fields[4, :512, :] = fields[1, :512, :] - alpha_0 * (fields[1, :512, :] + fields[4, :512, :])
-
-    observe(fields.at[4], 1)
-    fields[2, :512, :] = fields[0, :512, :] + fields[2, :512, :]
+    q_b[1] = q_b[0] - alpha_0 * (q_b[0] + q_b[1])
     fields[3, :512, :] = fields[0, :512, :] - alpha_0 * fields[2, :512, :]
-    sums_start(1, (product(fields[3, :512, :], fields[3, :512, :]), product(fields[3, :512, :], fields[0, :512, :]), energy(1, 1), energy(1, 0)))
+    sums_start(1, (
+        product(fields[3, :512, :], fields[3, :512, :]), product(fields[3, :512, :], fields[0, :512, :]), energy(1, 1), energy(1, 0)))
+    z_b[...] = var_b[...] * q_b[1]
     adjoint(5)
     halo_pack(5)
     arrive = halo_start(5, 4)
-    sums_middle(1)
     to_natural(fields.at[2], natural.at[1])
     to_natural(fields.at[3], natural.at[2])
-    build_frame(5, arrive, frame_a, 4)
+    build_frame(5, arrive, frame_a, 4, lambda: sums_middle(1))
     diffuse(5, 8)
     inner(fields.at[5])
     to_natural(fields.at[5], natural.at[3])

time: 68 us -> 66.5 us (0.978)
  Pallas kernels: 67.3 us -> 65.8 us
    pallas_call x1, Pallas kernels: 65.4 us -> 63.9 us  [body(): pl.pallas_call(functools.partial(kernel, regions, tiles), out_shape=(out,...]
where the time goes in v6:
time: 66.5 us; the launch traced here: 66.4 us
  Pallas kernels  65.8 us (99%)
    pallas_call x1, Pallas kernels, body(): pl.pallas_call(functools.partial(kernel, regions, tiles), out_shape=(out,...  63.9 us
    pallas_call x1, Pallas kernels, body(): pl.pallas_call(hand_over, out_shape=(out, out), in_specs=[pl.BlockSpec(me...  1.84 us

profile of v6, /device:TPU:1, one launch (start us, length us, event | category | flops | bytes accessed | tf_op | source)
XLA Modules:
  0.0 66.4 jit_solution(7136081050415077221)
XLA Ops:
  0.6 63.9 %shard_map.104 = (f32[512,128]{1,0:T(8,128)}, f32[512,128]{1,0:T(8,128)}) custom-call(f32[128,128]{1,0:T(8,128)} %bitcast.10, f32[128,128]{1,0:T(8,128)} %bitcast.11, s32[128,128]{1,0:T(8,128)} %bitcast.12, s32[1,512]{1,0:T(1,128)} %bitcast.13, s32[1,512]{1,0:T(1,128)} %bitcast.14, s32[1,512]{1,0:T(1,128)} %bitcast.15, f32[1,512]{1,0:T(1,128)} %bitcast.16, ...), custom_call_target="tpu_custom_call" | custom-call | tf_op jit(solution)/shard_map/pallas_call | solution.py:545
  64.6 1.8 %shard_map.105 = (f32[512,128]{1,0:T(8,128)}, f32[512,128]{1,0:T(8,128)}) custom-call(f32[512,128]{1,0:T(8,128)} %get-tuple-element.6.control, f32[512,128]{1,0:T(8,128)} %get-tuple-element.7.residual), custom_call_target="tpu_custom_call" | custom-call | tf_op jit(solution)/shard_map/pallas_call | solution.py:588

commit v7 on v6

--- a/solution.py
+++ b/solution.py
@@ -57,11 +57,11 @@
 
 def kernel(
     regions, tiles, kx_any, ky_any, mask_any, owner_any, row_any, col_any, innov_any, var_any, weight_any,
-    control_ref, residual_ref,
+    natural_out, factor_out,
     kx_ref, ky_ref, mask_ref, owner_ref, row_ref, col_ref, innov_ref, var_ref, weight_ref,
     dense, rows_in, left_in, right_in, packed, frame_a, frame_b, coef, wsplit, wsend, wrecv, msend, mrecv, expanded, expanded_0, coef_rows, coef_in,
     pick, pick_t, terms, var_b, z_b, q_b, acc, group_b, state16, fields, natural, sums_send, sums_region, sums_mid, sums_tile,
-    in_sem, halo_send, halo_recv, w_send_sem, w_recv_sem, m_sem, r_sem, t_sem,
+    in_sem, out_sem, halo_send, halo_recv, w_send_sem, w_recv_sem, m_sem, r_sem, t_sem,
 ):
     reg, til = lax.axis_index("region"), lax.axis_index("tile")
     up, down = lax.rem(reg + regions - 1, regions), lax.rem(reg + 1, regions)
@@ -491,8 +491,11 @@
     halo_pack(4)
     arrive = halo_start(4)
     to_natural(fields.at[0], natural.at[0])
-    build_frame(4, arrive, frame_a, 8, lambda: sums_middle(0))
+    leaving = [pltpu.make_async_copy(natural.at[i], natural_out.at[i], out_sem.at[i]) for i in range(4)]
+    leaving[0].start()
+    build_frame(4, arrive, frame_a)
     diffuse(1, 4)
+    sums_middle(0)
     inner(fields.at[2])
     diffuse(5, 8)
     inner(fields.at[4])
@@ -509,25 +512,31 @@
     adjoint(5)
     halo_pack(5)
     arrive = halo_start(5, 4)
-    to_natural(fields.at[2], natural.at[1])
-    to_natural(fields.at[3], natural.at[2])
+    for i in (1, 2):
+        to_natural(fields.at[i + 1], natural.at[i])
+        leaving[i].start()
     build_frame(5, arrive, frame_a, 4, lambda: sums_middle(1))
     diffuse(5, 8)
     inner(fields.at[5])
     to_natural(fields.at[5], natural.at[3])
+    leaving[3].start()
     drain()
     found = sums_finish(1)
     norm_1 = found[0:1]
     beta = norm_1 / norm_0
     curve = norm_1 + 2.0 * beta * found[1:2] + beta * beta * norm_0 + found[2:3] + 2.0 * beta * found[3:4] + beta * beta * energy_0
     alpha_1 = norm_1 / curve
-    control_ref[...] = (alpha_0 + alpha_1 * beta) * natural[0] + alpha_1 * natural[2]
-    residual_ref[...] = natural[2] - alpha_1 * (natural[2] + natural[3] + beta * natural[1])
-
-
-def hand_over(control, residual, control_out, residual_out):
-    control_out[...] = control[...]
-    residual_out[...] = residual[...]
+    factor_out[...] = jnp.zeros_like(factor_out)
+    for i, x in enumerate((alpha_0 + alpha_1 * beta, alpha_1, alpha_1 * beta)):
+        factor_out[i:i + 1, :] = jnp.broadcast_to(x, (1, LANES))
+    for c in leaving:
+        c.wait()
+
+
+def combine(natural, factor, control, residual):
+    whole, second, mixed = factor[0:1, :], factor[1:2, :], factor[2:3, :]
+    control[...] = whole * natural[0] + second * natural[2]
+    residual[...] = natural[2] - second * (natural[2] + natural[3]) - mixed * natural[1]
 
 
 def body(regions, tiles, kx, ky, mask, obs_owner, obs_row, obs_col, obs_weight, innovation, inverse_var):
@@ -542,11 +551,11 @@
         kx.reshape(flat), ky.reshape(flat), mask.reshape(flat), obs_owner.reshape(line), obs_row.reshape(line),
         obs_col.reshape(line), innovation.reshape(line), inverse_var.reshape(line), obs_weight,
     )
-    control, residual = pl.pallas_call(
+    natural, factor = pl.pallas_call(
         functools.partial(kernel, regions, tiles),
-        out_shape=(out, out),
+        out_shape=(jax.ShapeDtypeStruct((4, 32 * rows_x, cols_y), F32), jax.ShapeDtypeStruct((8, LANES), F32)),
         in_specs=[pl.BlockSpec(memory_space=pl.ANY)] * 9,
-        out_specs=[pl.BlockSpec(memory_space=pltpu.VMEM)] * 2,
+        out_specs=[pl.BlockSpec(memory_space=pl.ANY), pl.BlockSpec(memory_space=pltpu.VMEM)],
         scratch_shapes=[
             *[pltpu.VMEM(x.shape, x.dtype) for x in args],
             pltpu.VMEM((EXCHANGES, cells, LANES), F32),
@@ -581,17 +590,17 @@
             pltpu.VMEM((2, regions, 4, LANES), F32),
             pltpu.VMEM((2, 4, LANES), F32),
             pltpu.VMEM((2, tiles, 4, LANES), F32),
-            dma((9,)), dma((EXCHANGES,)), dma((EXCHANGES,)), dma((1,)), dma((tiles // 4,)), dma((2,)), dma((2, 2)), dma((2, 2)),
+            dma((9,)), dma((4,)), dma((EXCHANGES,)), dma((EXCHANGES,)), dma((1,)), dma((tiles // 4,)), dma((2,)), dma((2, 2)), dma((2, 2)),
         ],
         compiler_params=pltpu.CompilerParams(collective_id=0, has_side_effects=True, vmem_limit_bytes=60 * 1024 * 1024),
     )(*args)
     control, residual = pl.pallas_call(
-        hand_over,
+        combine,
         out_shape=(out, out),
         in_specs=[pl.BlockSpec(memory_space=pltpu.VMEM)] * 2,
         out_specs=[pl.BlockSpec(memory_space=pltpu.VMEM)] * 2,
         compiler_params=pltpu.CompilerParams(vmem_limit_bytes=60 * 1024 * 1024),
-    )(control, residual)
+    )(natural, factor)
     shape = (32 // levels, levels, rows_x, cols_y)
     return control.reshape(shape), residual.reshape(shape)
 

time: 66.5 us -> 66.5 us (level)
  no operation moved by 1% of the time
where the time goes in v7:
time: 66.5 us; the launch traced here: 66.4 us
  Pallas kernels  65.7 us (99%)
    pallas_call x1, Pallas kernels, body(): pl.pallas_call(functools.partial(kernel, regions, tiles), out_shape=(jax....  63.7 us
    pallas_call x1, Pallas kernels, body(): pl.pallas_call(combine, out_shape=(out, out), in_specs=[pl.BlockSpec(memo...  2.05 us

profile of v7, /device:TPU:1, one launch (start us, length us, event | category | flops | bytes accessed | tf_op | source)
XLA Modules:
  0.0 66.4 jit_solution(8990435405517694684)
XLA Ops:
  0.6 63.7 %shard_map.104 = (f32[4,512,128]{2,1,0:T(8,128)}, f32[8,128]{1,0:T(8,128)}) custom-call(f32[128,128]{1,0:T(8,128)} %bitcast.10, f32[128,128]{1,0:T(8,128)} %bitcast.11, s32[128,128]{1,0:T(8,128)} %bitcast.12, s32[1,512]{1,0:T(1,128)} %bitcast.13, s32[1,512]{1,0:T(1,128)} %bitcast.14, s32[1,512]{1,0:T(1,128)} %bitcast.15, f32[1,512]{1,0:T(1,128)} %bitcast.16, ...), custom_call_target="tpu_custom_call" | custom-call | tf_op jit(solution)/shard_map/pallas_call | solution.py:554
  64.3 2.0 %shard_map.105 = (f32[512,128]{1,0:T(8,128)}, f32[512,128]{1,0:T(8,128)}) custom-call(f32[4,512,128]{2,1,0:T(8,128)} %get-tuple-element.6.natural, f32[8,128]{1,0:T(8,128)} %get-tuple-element.7.factor), custom_call_target="tpu_custom_call" | custom-call | tf_op jit(solution)/shard_map/pallas_call | solution.py:597

commit v8 on v7

--- a/solution.py
+++ b/solution.py
@@ -121,7 +121,15 @@
             packed[e, 4 + j] = first[0]
 
     def halo_start(e, deep=8, fields=1):
-        for c in halo_copies(e, deep, fields):
+        copies = halo_copies(e, deep, fields)
+        for c in copies[6:]:
+            c.start()
+        if e == 0:
+            for i in range(3):
+                to_cells(lambda r: coef_rows[r, 8 * i:8 * i + 8, :], dense.at[i], 16)
+        for i in range(fields):
+            halo_pack(e + i)
+        for c in copies[:6]:
             c.start()
         amount = frame_b.at[pl.ds(0, 768 if e == 0 else 72 * deep + 64)]
         late.append(lambda: wait_all(amount, halo_send.at[e]))
@@ -279,9 +287,6 @@
         return 0
 
     lax.fori_loop(0, 16, stage, 0)
-    for e in range(3):
-        to_cells(lambda r: coef_rows[r, 8 * e:8 * e + 8, :], dense.at[e], 16)
-        halo_pack(e)
     coef_arrive = halo_start(0, 8, 3)
 
     def diffuse(first, last):
@@ -450,7 +455,6 @@
     def energy(a, b):
         return jnp.where(lane1 == 0, product(var_b[...] * q_b[a], q_b[b]), 0.0)
 
-    halo_pack(3)
     arrive = halo_start(3)
 
     coef_arrive()
@@ -485,11 +489,10 @@
 
     norm = product(fields[0, :512, :], fields[0, :512, :])
     observe(fields.at[1], 0)
-    sums_start(0, (norm, energy(0, 0)))
     z_b[...] = var_b[...] * q_b[0]
     adjoint(4)
-    halo_pack(4)
     arrive = halo_start(4)
+    sums_start(0, (norm, energy(0, 0)))
     to_natural(fields.at[0], natural.at[0])
     leaving = [pltpu.make_async_copy(natural.at[i], natural_out.at[i], out_sem.at[i]) for i in range(4)]
     leaving[0].start()
@@ -510,7 +513,6 @@
         product(fields[3, :512, :], fields[3, :512, :]), product(fields[3, :512, :], fields[0, :512, :]), energy(1, 1), energy(1, 0)))
     z_b[...] = var_b[...] * q_b[1]
     adjoint(5)
-    halo_pack(5)
     arrive = halo_start(5, 4)
     for i in (1, 2):
         to_natural(fields.at[i + 1], natural.at[i])

time: 66.5 us -> 66.6 us (level)
  no operation moved by 1% of the time
where the time goes in v8:
time: 66.6 us; the launch traced here: 66.4 us
  Pallas kernels  65.8 us (99%)
    pallas_call x1, Pallas kernels, body(): pl.pallas_call(functools.partial(kernel, regions, tiles), out_shape=(jax....  63.8 us
    pallas_call x1, Pallas kernels, body(): pl.pallas_call(combine, out_shape=(out, out), in_specs=[pl.BlockSpec(memo...  2.05 us

profile of v8, /device:TPU:1, one launch (start us, length us, event | category | flops | bytes accessed | tf_op | source)
XLA Modules:
  0.0 66.4 jit_solution(14222920415202313337)
XLA Ops:
  0.6 63.8 %shard_map.104 = (f32[4,512,128]{2,1,0:T(8,128)}, f32[8,128]{1,0:T(8,128)}) custom-call(f32[128,128]{1,0:T(8,128)} %bitcast.10, f32[128,128]{1,0:T(8,128)} %bitcast.11, s32[128,128]{1,0:T(8,128)} %bitcast.12, s32[1,512]{1,0:T(1,128)} %bitcast.13, s32[1,512]{1,0:T(1,128)} %bitcast.14, s32[1,512]{1,0:T(1,128)} %bitcast.15, f32[1,512]{1,0:T(1,128)} %bitcast.16, ...), custom_call_target="tpu_custom_call" | custom-call | tf_op jit(solution)/shard_map/pallas_call | solution.py:556
  64.4 2.0 %shard_map.105 = (f32[512,128]{1,0:T(8,128)}, f32[512,128]{1,0:T(8,128)}) custom-call(f32[4,512,128]{2,1,0:T(8,128)} %get-tuple-element.6.natural, f32[8,128]{1,0:T(8,128)} %get-tuple-element.7.factor), custom_call_target="tpu_custom_call" | custom-call | tf_op jit(solution)/shard_map/pallas_call | solution.py:599

commit v9 on v8

--- a/solution.py
+++ b/solution.py
@@ -59,9 +59,9 @@
     regions, tiles, kx_any, ky_any, mask_any, owner_any, row_any, col_any, innov_any, var_any, weight_any,
     natural_out, factor_out,
     kx_ref, ky_ref, mask_ref, owner_ref, row_ref, col_ref, innov_ref, var_ref, weight_ref,
-    dense, rows_in, left_in, right_in, packed, frame_a, frame_b, coef, wsplit, wsend, wrecv, msend, mrecv, expanded, expanded_0, coef_rows, coef_in,
+    dense, rows_in, left_in, right_in, packed, frame_a, frame_b, coef, wsplit, wsend, wrecv, expanded, expanded_0, coef_rows, coef_in,
     pick, pick_t, terms, var_b, z_b, q_b, acc, group_b, state16, fields, natural, sums_send, sums_region, sums_mid, sums_tile,
-    in_sem, out_sem, halo_send, halo_recv, w_send_sem, w_recv_sem, m_sem, r_sem, t_sem,
+    in_sem, out_sem, halo_send, halo_recv, w_send_sem, w_recv_sem, r_sem, t_sem,
 ):
     reg, til = lax.axis_index("region"), lax.axis_index("tile")
     up, down = lax.rem(reg + regions - 1, regions), lax.rem(reg + 1, regions)
@@ -235,12 +235,12 @@
         for k in range(4):
             turned = [pltpu.roll(x, (i - k) * 32 % LANES, 1) for i, x in enumerate(three)]
             line = jnp.where(lane8 < 32, turned[0], jnp.where(lane8 < 64, turned[1], jnp.where(lane8 < 96, turned[2], 0.0)))
-            msend[4 * b + k] = line[0:1]
+            wsend[4 * b + k, CAP:CAP + 1, :] = line[0:1]
     loads[5].wait()
     for i, part in enumerate(split(weight_ref[...], 3)):
         wsplit[:, i * LANES:(i + 1) * LANES] = part
     block = dot(pick[:, :count], wsplit[...])
-    wsend[...] = (block[:, :LANES] + block[:, LANES:2 * LANES] + block[:, 2 * LANES:]).reshape(tiles, CAP, LANES)
+    wsend[:, :CAP, :] = (block[:, :LANES] + block[:, LANES:2 * LANES] + block[:, 2 * LANES:]).reshape(tiles, CAP, LANES)
 
     turns = sorted(range(planes), key=lambda i: (min(i, planes - i), i))
     plane, place_in = til // 4, lax.rem(til, 4)
@@ -263,9 +263,7 @@
             order += [4 * i + k - 1 for k in range(4) for i in (j, j + 1) if i < planes]
         return [copies[i] for i in order]
 
-    m_copies = sends(msend, mrecv, m_sem.at[0], m_sem.at[pl.ds(1, 1)], tiles)
     w_copies = sends(wsend, wrecv, w_send_sem.at[0], w_recv_sem, 4)
-    late.append(lambda: wait_all(msend.at[pl.ds(1, tiles - 1)], m_sem.at[0]))
     late.append(lambda: wait_all(wsend.at[pl.ds(1, tiles - 1)], w_send_sem.at[0]))
     def drain():
         for wait in late:
@@ -273,10 +271,9 @@
         late.clear()
 
     pl.semaphore_wait(barrier, (tiles - 1) + (regions - 1) + 4)
-    for c in both_ways(m_copies) + both_ways(w_copies):
+    for c in both_ways(w_copies):
         c.start()
     wrecv[0] = wsend[til]
-    mrecv[0] = msend[til]
 
     for c in loads[6:]:
         c.wait()
@@ -316,7 +313,6 @@
         for j in range(16):
             out[j * 32:(j + 1) * 32, :] = frame_a[(8 + j) * WIDE + 16:(9 + j) * WIDE, :]
 
-    wait_all(mrecv.at[pl.ds(1, tiles - 1)], m_sem.at[1])
     lane = iota((LANES, LANES), 1)
     seat = iota((LANES, LANES), 0) % CAP
     ones = jnp.ones((3 * LANES, LANES), BF16)
@@ -327,9 +323,9 @@
         col = (place & 127) + c % 2
         return row * 32 + (col & 31), col >> 5
 
-    def read_facts(j, _):
+    def read_facts(j):
         at = pl.ds(pl.multiple_of(j * LANES, LANES), LANES)
-        facts = jnp.broadcast_to(mrecv[pl.ds(4 * j, 4)], (4, CAP, LANES)).reshape(LANES, LANES)
+        facts = jnp.broadcast_to(wrecv[pl.ds(4 * j, 4), CAP:CAP + 1, :], (4, CAP, LANES)).reshape(LANES, LANES)
 
         def spread_lanes(kind):
             return jnp.concatenate(split(jnp.where(lane == seat + 32 * kind, facts, 0.0), 3), axis=1)
@@ -351,9 +347,6 @@
             cell, _ = corner_of(place_row, c)
             there = pl.ds(pl.multiple_of((4 * j + c) * LANES, LANES), LANES)
             pick_t[:, there] = jnp.where(iota((cells, LANES), 0) == cell, 1.0, 0.0).astype(BF16)
-        return 0
-
-    lax.fori_loop(0, planes, read_facts, 0)
 
     def put_terms(j, c):
         at = pl.ds(pl.multiple_of(j * LANES, LANES), LANES)
@@ -370,7 +363,8 @@
         1.0, 0.0).astype(BF16)
     def take_plane(j, first):
         wait_all(wrecv.at[pl.ds(4 * j + first, 4 - first)], w_recv_sem.at[j])
-        wide = dot(jnp.concatenate(split(wrecv[pl.ds(4 * j, 4)].reshape(LANES, LANES), 3), axis=1), copy_lanes)
+        read_facts(j)
+        wide = dot(jnp.concatenate(split(wrecv[pl.ds(4 * j, 4), :CAP, :].reshape(LANES, LANES), 3), axis=1), copy_lanes)
         at = pl.ds(pl.multiple_of(j * LANES, LANES), LANES)
         for c in range(4):
             expanded[c, at, :] = wide[:, c * LANES:(c + 1) * LANES] * group_b[c, at, :]
@@ -569,10 +563,8 @@
             pltpu.VMEM((FRAME, LANES), F32),
             pltpu.VMEM((3, FRAME, LANES), F32),
             pltpu.VMEM((count, 3 * LANES), BF16),
-            pltpu.VMEM((tiles, CAP, LANES), F32),
-            pltpu.VMEM((tiles, CAP, LANES), F32),
-            pltpu.VMEM((tiles, 1, LANES), F32),
-            pltpu.VMEM((tiles, 1, LANES), F32),
+            pltpu.VMEM((tiles, CAP + 1, LANES), F32),
+            pltpu.VMEM((tiles, CAP + 1, LANES), F32),
             pltpu.VMEM((4, slots, LANES), F32),
             pltpu.VMEM((4, slots, LANES), F32),
             pltpu.VMEM((16, 24, LANES), F32),
@@ -592,7 +584,7 @@
             pltpu.VMEM((2, regions, 4, LANES), F32),
             pltpu.VMEM((2, 4, LANES), F32),
             pltpu.VMEM((2, tiles, 4, LANES), F32),
-            dma((9,)), dma((4,)), dma((EXCHANGES,)), dma((EXCHANGES,)), dma((1,)), dma((tiles // 4,)), dma((2,)), dma((2, 2)), dma((2, 2)),
+            dma((9,)), dma((4,)), dma((EXCHANGES,)), dma((EXCHANGES,)), dma((1,)), dma((tiles // 4,)), dma((2, 2)), dma((2, 2)),
         ],
         compiler_params=pltpu.CompilerParams(collective_id=0, has_side_effects=True, vmem_limit_bytes=60 * 1024 * 1024),
     )(*args)

time: 66.6 us -> 66.8 us (level)
  no operation moved by 1% of the time
where the time goes in v9:
time: 66.8 us; the launch traced here: 66.7 us
  Pallas kernels  66.1 us (99%)
    pallas_call x1, Pallas kernels, body(): pl.pallas_call(functools.partial(kernel, regions, tiles), out_shape=(jax....  64 us
    pallas_call x1, Pallas kernels, body(): pl.pallas_call(combine, out_shape=(out, out), in_specs=[pl.BlockSpec(memo...  2.05 us

profile of v9, /device:TPU:1, one launch (start us, length us, event | category | flops | bytes accessed | tf_op | source)
XLA Modules:
  0.0 66.7 jit_solution(14096510572743418056)
XLA Ops:
  0.6 64.0 %shard_map.104 = (f32[4,512,128]{2,1,0:T(8,128)}, f32[8,128]{1,0:T(8,128)}) custom-call(f32[128,128]{1,0:T(8,128)} %bitcast.10, f32[128,128]{1,0:T(8,128)} %bitcast.11, s32[128,128]{1,0:T(8,128)} %bitcast.12, s32[1,512]{1,0:T(1,128)} %bitcast.13, s32[1,512]{1,0:T(1,128)} %bitcast.14, s32[1,512]{1,0:T(1,128)} %bitcast.15, f32[1,512]{1,0:T(1,128)} %bitcast.16, ...), custom_call_target="tpu_custom_call" | custom-call | tf_op jit(solution)/shard_map/pallas_call | solution.py:550
  64.6 2.0 %shard_map.105 = (f32[512,128]{1,0:T(8,128)}, f32[512,128]{1,0:T(8,128)}) custom-call(f32[4,512,128]{2,1,0:T(8,128)} %get-tuple-element.6.natural, f32[8,128]{1,0:T(8,128)} %get-tuple-element.7.factor), custom_call_target="tpu_custom_call" | custom-call | tf_op jit(solution)/shard_map/pallas_call | solution.py:591

commit v10 on v8

--- a/solution.py
+++ b/solution.py
@@ -87,7 +87,7 @@
         (owner_any, owner_ref), (row_any, row_ref), (col_any, col_ref), (innov_any, innov_ref), (var_any, var_ref),
         (weight_any, weight_ref), (mask_any, mask_ref), (kx_any, kx_ref), (ky_any, ky_ref),
     )
-    loads = [pltpu.make_async_copy(a, b, in_sem.at[i]) for i, (a, b) in enumerate(pairs)]
+    loads = [pltpu.make_async_copy(a, b.at[pl.ds(0, a.shape[0])] if i > 5 else b, in_sem.at[i]) for i, (a, b) in enumerate(pairs)]
     for c in loads:
         c.start()
     for c in loads[:5]:
@@ -494,7 +494,7 @@
     arrive = halo_start(4)
     sums_start(0, (norm, energy(0, 0)))
     to_natural(fields.at[0], natural.at[0])
-    leaving = [pltpu.make_async_copy(natural.at[i], natural_out.at[i], out_sem.at[i]) for i in range(4)]
+    leaving = [pltpu.make_async_copy(natural.at[i, pl.ds(0, 512)], natural_out.at[i], out_sem.at[i]) for i in range(4)]
     leaving[0].start()
     build_frame(4, arrive, frame_a)
     diffuse(1, 4)
@@ -559,7 +559,7 @@
         in_specs=[pl.BlockSpec(memory_space=pl.ANY)] * 9,
         out_specs=[pl.BlockSpec(memory_space=pl.ANY), pl.BlockSpec(memory_space=pltpu.VMEM)],
         scratch_shapes=[
-            *[pltpu.VMEM(x.shape, x.dtype) for x in args],
+            *[pltpu.VMEM((x.shape[0] + (16 if i < 3 else 0), x.shape[1]), x.dtype) for i, x in enumerate(args)],
             pltpu.VMEM((EXCHANGES, cells, LANES), F32),
             pltpu.VMEM((EXCHANGES, 2, 32 * HALO, LANES), F32),
             pltpu.VMEM((EXCHANGES, 8, 8, LANES), F32),
@@ -587,7 +587,7 @@
             pltpu.VMEM((4, slots, LANES), F32),
             pltpu.VMEM((2 * cells, 4 * LANES), BF16),
             pltpu.VMEM((6, cells + 8, LANES), F32),
-            pltpu.VMEM((4, cells, LANES), F32),
+            pltpu.VMEM((4, cells + 16, LANES), F32),
             pltpu.VMEM((2, 4, LANES), F32),
             pltpu.VMEM((2, regions, 4, LANES), F32),
             pltpu.VMEM((2, 4, LANES), F32),

time: 66.6 us -> 66.6 us (level)
  no operation moved by 1% of the time
where the time goes in v10:
time: 66.6 us; the launch traced here: 66.5 us
  Pallas kernels  65.8 us (99%)
    pallas_call x1, Pallas kernels, body(): pl.pallas_call(functools.partial(kernel, regions, tiles), out_shape=(jax....  63.8 us
    pallas_call x1, Pallas kernels, body(): pl.pallas_call(combine, out_shape=(out, out), in_specs=[pl.BlockSpec(memo...  2.05 us

profile of v10, /device:TPU:1, one launch (start us, length us, event | category | flops | bytes accessed | tf_op | source)
XLA Modules:
  0.0 66.5 jit_solution(3926543125988514190)
XLA Ops:
  0.6 63.8 %shard_map.104 = (f32[4,512,128]{2,1,0:T(8,128)}, f32[8,128]{1,0:T(8,128)}) custom-call(f32[128,128]{1,0:T(8,128)} %bitcast.10, f32[128,128]{1,0:T(8,128)} %bitcast.11, s32[128,128]{1,0:T(8,128)} %bitcast.12, s32[1,512]{1,0:T(1,128)} %bitcast.13, s32[1,512]{1,0:T(1,128)} %bitcast.14, s32[1,512]{1,0:T(1,128)} %bitcast.15, f32[1,512]{1,0:T(1,128)} %bitcast.16, ...), custom_call_target="tpu_custom_call" | custom-call | tf_op jit(solution)/shard_map/pallas_call | solution.py:556
  64.4 2.0 %shard_map.105 = (f32[512,128]{1,0:T(8,128)}, f32[512,128]{1,0:T(8,128)}) custom-call(f32[4,512,128]{2,1,0:T(8,128)} %get-tuple-element.6.natural, f32[8,128]{1,0:T(8,128)} %get-tuple-element.7.factor), custom_call_target="tpu_custom_call" | custom-call | tf_op jit(solution)/shard_map/pallas_call | solution.py:599
